TPU v7x, 32 devices: a whole 2x2x4 slice. The times are simulated.
32 devices in a mesh: dp: 8 (over z, x), tile: 4 (over y, core).
Axes of the slice: x: 2, y: 2, z: 4, core: 2. Of those that a mesh axis runs over, the one named last changes fastest.
Arguments:
- queries: bfloat16 [8, 960, 1536], P('dp', 'tile'), may hold values from -100 to 100
- key_vectors: bfloat16 [8, 960, 1536], P('dp', 'tile'), may hold values from -4 to 4
- value_vectors: bfloat16 [8, 960, 1536], P('dp', 'tile'), may hold values from -6 to 6
- out_weight: bfloat16 [1536, 3072], P('dp', 'tile'), may hold values from -0.15625 to 0.15625
- cotangent: bfloat16 [8, 960, 3072], P('dp', 'tile'), may hold values from -6 to 6
Outputs:
- projected: bfloat16 [8, 960, 3072], P('dp', 'tile')
- query_grad: bfloat16 [8, 960, 1536], P('dp', 'tile')
- key_grad: bfloat16 [8, 960, 1536], P('dp', 'tile')
- value_grad: bfloat16 [8, 960, 1536], P('dp', 'tile')
- weight_grad: float32 [1536, 3072], P('dp', 'tile')
All inputs are finite; a program needn't handle non-finite values.
Results may differ from a plain program's by a relative error of at most 0.035.
Values may be sent and summed in bfloat16 or wider, within the bound.
No kernel may reach another device: no remote copies, remote signals or barrier semaphores. Data moves between devices by JAX's collectives and lax.ppermute only.
A program may use at most 128 MiB of HBM per device.

v0:
```python
import jax
import jax.numpy as jnp
from jax import lax
from jax.sharding import PartitionSpec as P

HEADS = 12
HEAD = 128
TILE = 120


def extended_2(block, sides, width):
    for axis, dim in sides:
        count = lax.axis_size(axis)
        forward = [(i, i + 1) for i in range(count - 1)]
        backward = [(target, source) for source, target in forward]
        low = lax.ppermute(
            lax.slice_in_dim(block, block.shape[dim] - width, None, axis=dim), axis, forward
        )
        high = lax.ppermute(lax.slice_in_dim(block, 0, width, axis=dim), axis, backward)
        block = jnp.concatenate([low, block, high], axis=dim)
    return block


def passed_along(block, axis, distance):
    devices = range(lax.axis_size(axis))
    route = [(i - distance, i) for i in devices if i - distance in devices]
    return lax.ppermute(block, axis, route)


def contract_rows(left, right):
    return lax.dot_general(
        left, right, (((0,), (0,)), ((), ())), preferred_element_type=jnp.float32
    )


def contract_cols(left, right):
    return lax.dot_general(
        left, right, (((1,), (1,)), ((), ())), preferred_element_type=jnp.float32
    )


def shards(queries, key_vectors, value_vectors, out_weight, cotangent):
    query_rows = queries[0]
    key_rows = key_vectors[0]
    value_rows = value_vectors[0]
    grad_rows = cotangent[0]
    tokens = query_rows.shape[0]
    inner_width = query_rows.shape[1]
    tile_count = lax.axis_size("tile")
    position = lax.axis_index("tile")
    tiles_here = tokens // TILE
    total_tiles = tiles_here * tile_count
    score_scale = HEAD ** (-0.5)
    joined = jnp.concatenate([key_rows, value_rows], axis=1)
    extended = extended_2(joined, (("tile", 0),), TILE)
    key_ext = extended[:, :inner_width].reshape(-1, HEADS, HEAD)
    value_ext = extended[:, inner_width:].reshape(-1, HEADS, HEAD)
    query_tile = position * tiles_here + jnp.arange(tokens) // TILE
    key_tile = position * tiles_here - 1 + jnp.arange(tokens + 2 * TILE) // TILE
    visible = (
        (jnp.abs(query_tile[:, None] - key_tile[None, :]) <= 1)
        & (key_tile >= 0)[None, :]
        & (key_tile < total_tiles)[None, :]
    )
    query_heads = query_rows.reshape(tokens, HEADS, HEAD)
    scores = (
        jnp.einsum("qhd,khd->hqk", query_heads, key_ext, preferred_element_type=jnp.float32)
        * score_scale
    )
    scores = jnp.where(visible[None], scores, -1e30)
    row_max = jnp.max(scores, axis=-1, keepdims=True)
    expd = jnp.exp(scores - row_max)
    attn_probs = expd / jnp.sum(expd, axis=-1, keepdims=True)
    probs_half = attn_probs.astype(jnp.bfloat16)
    attention = jnp.einsum(
        "hqk,khd->qhd", probs_half, value_ext, preferred_element_type=jnp.float32
    )
    attention = attention.astype(jnp.bfloat16).reshape(tokens, inner_width)
    weight_rows = lax.all_gather(out_weight, "dp", axis=0, tiled=True)
    weight_full = lax.all_gather(weight_rows, "tile", axis=1, tiled=True)
    projected = jnp.dot(attention, weight_full, preferred_element_type=jnp.float32).astype(
        jnp.bfloat16
    )
    grad_attention = contract_cols(grad_rows, weight_full).astype(jnp.bfloat16)
    row_share = lax.psum_scatter(
        contract_rows(attention, grad_rows), "dp", scatter_dimension=0, tiled=True
    )
    weight_grad = lax.psum_scatter(row_share, "tile", scatter_dimension=1, tiled=True)
    grad_heads = grad_attention.reshape(tokens, HEADS, HEAD)
    attn_heads = attention.reshape(tokens, HEADS, HEAD)
    row_dots = jnp.einsum("qhd,qhd->hq", grad_heads, attn_heads, preferred_element_type=jnp.float32)
    grad_probs = jnp.einsum(
        "qhd,khd->hqk", grad_heads, value_ext, preferred_element_type=jnp.float32
    )
    grad_scores = (attn_probs * (grad_probs - row_dots[:, :, None])).astype(jnp.bfloat16)
    query_grad = (
        jnp.einsum("hqk,khd->qhd", grad_scores, key_ext, preferred_element_type=jnp.float32)
        * score_scale
    )
    query_grad = query_grad.astype(jnp.bfloat16).reshape(tokens, inner_width)
    key_ext_grad = (
        jnp.einsum("hqk,qhd->khd", grad_scores, query_heads, preferred_element_type=jnp.float32)
        * score_scale
    )
    value_ext_grad = jnp.einsum(
        "hqk,qhd->khd", probs_half, grad_heads, preferred_element_type=jnp.float32
    )
    both_grads = jnp.concatenate(
        [key_ext_grad.reshape(-1, inner_width), value_ext_grad.reshape(-1, inner_width)], axis=1
    )
    left_rim = both_grads[:TILE].astype(jnp.bfloat16)
    right_rim = both_grads[-TILE:].astype(jnp.bfloat16)
    from_right = passed_along(left_rim, "tile", -1)
    from_left = passed_along(right_rim, "tile", 1)
    own_grads = both_grads[TILE : TILE + tokens]
    own_grads = own_grads.at[tokens - TILE :].add(from_right.astype(jnp.float32))
    own_grads = own_grads.at[:TILE].add(from_left.astype(jnp.float32))
    key_grad = own_grads[:, :inner_width].astype(jnp.bfloat16)
    value_grad = own_grads[:, inner_width:].astype(jnp.bfloat16)
    return (projected[None], query_grad[None], key_grad[None], value_grad[None], weight_grad)


def solution(mesh):
    in_specs = (
        P("dp", "tile", None),
        P("dp", "tile", None),
        P("dp", "tile", None),
        P("dp", "tile"),
        P("dp", "tile", None),
    )
    out_specs = (
        P("dp", "tile", None),
        P("dp", "tile", None),
        P("dp", "tile", None),
        P("dp", "tile", None),
        P("dp", "tile"),
    )
    return jax.shard_map(shards, mesh=mesh, in_specs=in_specs, out_specs=out_specs, check_vma=False)
```

profile of v0, /device:TPU:0, one launch (start us, length us, event | category | flops | bytes accessed | tf_op | source)
XLA Modules:
  0.0 544.9 jit_solution(3136063609494381718)
XLA Ops:
  8.0 57.0 %all-gather.3.cloned.1.call-done = bf16[1536,768]{1,0:T(8,128)(2,1)} async-done(((bf16[192,768]{1,0:T(8,128)(2,1)}), bf16[1536,768]{1,0:T(8,128)(2,1)}) %all-gather.3.cloned.1.call-update) | async-done | bytes 2359312 | tf_op jit(solution)/shard_map/all_gather | solution.py:79
  67.7 3.9 collective-permute-start
  71.7 2.4 copy.41
  74.4 2.8 pad_maximum_fusion.1
  81.7 6.4 %fusion.29 = (f32[12,240]{1,0:T(8,128)S(1)}, f32[12,240,480]{1,2,0:T(8,128)}) fusion(pred[240,480]{0,1:T(8,128)(4,1)S(1)} %fusion.17, bf16[480,12,128]{0,2,1:T(8,128)(2,1)S(1)} %bitcast.74, bf16[240,12,128]{0,2,1:T(8,128)(2,1)} %bitcast.78), kind=kOutput, calls=%fused_computation.62 | convolution fusion | flops 359424480 | bytes 7868160 | tf_op jit(solution)/shard_map/sub | solution.py:72
  88.1 4.9 fusion.8
  93.0 38.8 %all-gather.5.cloned.1.call-done = bf16[1536,3072]{1,0:T(8,128)(2,1)} async-done(((bf16[1536,768]{1,0:T(8,128)(2,1)}), bf16[1536,3072]{1,0:T(8,128)(2,1)}) %all-gather.5.cloned.1.call-update) | async-done | bytes 9437200 | tf_op jit(solution)/shard_map/all_gather | solution.py:80
  131.8 6.3 %convolution_convert_fusion.1 = bf16[240,1536]{1,0:T(8,128)(2,1)S(1)} fusion(bf16[1536,3072]{1,0:T(8,128)(2,1)} %all-gather.5.cloned.1.call-done, bf16[1,240,3072]{2,1,0:T(8,128)(2,1)S(1)} %copy-done), kind=kOutput, calls=%fused_computation.20 | convolution fusion | flops 2265292800 | bytes 11649024 | tf_op jit(solution)/shard_map/dot_general | solution.py:37
  139.8 4.0 multiply_reduce_fusion
  144.2 7.8 %fusion.11 = f32[1536,3072]{1,0:T(8,128)} fusion(bf16[240,1536]{0,1:T(8,128)(2,1)S(1)} %bitcast.69, bf16[1,240,3072]{2,1,0:T(8,128)(2,1)S(1)} %copy-done), kind=kOutput, calls=%fused_computation.28 | convolution fusion | flops 2264924160 | bytes 21086208 | tf_op jit(solution)/shard_map/dot_general | solution.py:31
  153.9 3.9 convolution_bitcast_fusion
  157.7 4.5 multiply_convert_fusion
  162.2 303.3 %reduce-scatter.3.cloned.1.call-done = f32[192,3072]{1,0:T(8,128)} async-done(((f32[1536,3072]{1,0:T(8,128)}), f32[192,3072]{1,0:T(8,128)}) %reduce-scatter.3.cloned.1.call-update) | async-done | bytes 2359312 | tf_op jit(solution)/shard_map/reduce_scatter | solution.py:85
  465.5 3.7 multiply_bitcast_fusion
  469.2 2.3 copy.55
  471.5 3.8 copy.57
  475.3 2.5 fusion.1
  485.3 4.2 collective-permute-start.3
  489.5 7.6 %fusion.3 = bf16[1,240,3072]{2,1,0:T(8,128)(2,1)} fusion(bf16[240,1536]{0,1:T(8,128)(2,1)} %bitcast.70, bf16[1536,3072]{1,0:T(8,128)(2,1)} %all-gather.5.cloned.1.call-done), kind=kOutput, calls=%fused_computation.12 | convolution fusion | flops 2265661440 | bytes 11649024 | tf_op jit(solution)/shard_map/dot_general | solution.py:81
  497.1 2.5 fusion.4
  507.1 2.3 copy.59
  509.4 3.2 fusion.10
  512.7 9.8 %scatter-add.6 = f32[240,3072]{0,1:T(8,128)} dynamic-update-slice(f32[240,3072]{0,1:T(8,128)} %fusion.4, f32[120,3072]{0,1:T(8,128)} %fusion.10, s32[]{:T(128)} %constant.84.clone.1, s32[]{:T(128)} %constant.85.clone.1) | dynamic-update-slice | bytes 2949124 | tf_op jit(solution)/shard_map/scatter-add | solution.py:116
  525.5 8.2 %scatter-add.9 = f32[240,3072]{0,1:T(8,128)} dynamic-update-slice(f32[240,3072]{0,1:T(8,128)} %scatter-add.6, f32[120,3072]{0,1:T(8,128)S(1)} %slice_add_fusion, s32[]{:T(128)} %constant.85.clone.1, s32[]{:T(128)} %constant.85.clone.1) | dynamic-update-slice | bytes 2949124 | tf_op jit(solution)/shard_map/scatter-add | solution.py:117
  (66 shorter events, 34.5 us)
Async XLA Ops:
  7.2 124.7 %copy-start = (bf16[1,240,3072]{2,1,0:T(8,128)(2,1)S(1)}, bf16[1,240,3072]{2,1,0:T(8,128)(2,1)}, u32[]{:S(2)}) copy-start(bf16[1,240,3072]{2,1,0:T(8,128)(2,1)} %param.13) | copy-start | bytes 4423684
  7.2 57.9 %copy-start.12 = (bf16[1,240,1536]{2,1,0:T(8,128)(2,1)S(1)}, bf16[1,240,1536]{2,1,0:T(8,128)(2,1)}, u32[]{:S(2)}) copy-start(bf16[1,240,1536]{2,1,0:T(8,128)(2,1)} %param.10) | copy-start | bytes 2211844
  7.2 57.9 %copy-start.13 = (bf16[1,240,1536]{2,1,0:T(8,128)(2,1)S(1)}, bf16[1,240,1536]{2,1,0:T(8,128)(2,1)}, u32[]{:S(2)}) copy-start(bf16[1,240,1536]{2,1,0:T(8,128)(2,1)} %param.11) | copy-start | bytes 2211844
  7.2 57.8 %all-gather.3.cloned.1.call-start = ((), (), s32[]{:S(2)}) async-start(), calls=%async_computation.2 | async-start | bytes 2654208 | tf_op jit(solution)/shard_map/all_gather | solution.py:79
  7.9 123.9 %all-gather.5.cloned.1.call-start = ((), (), s32[]{:S(2)}) async-start(), calls=%async_computation.3 | async-start | bytes 11796480 | tf_op jit(solution)/shard_map/all_gather | solution.py:80
  65.1 400.4 %reduce-scatter.3.cloned.1.call-start = ((), (), s32[]{:S(2)}) async-start(), calls=%async_computation.4 | async-start | bytes 21233664 | tf_op jit(solution)/shard_map/reduce_scatter | solution.py:85
  66.4 7.9 %collective-permute-start.1 = (bf16[120,3072]{1,0:T(8,128)(2,1)}, bf16[120,3072]{1,0:T(8,128)(2,1)}, u32[]{:S(2)}, u32[]{:S(2)}) collective-permute-start(bf16[120,3072]{1,0:T(8,128)(2,1)} %get-tuple-element.46), channel_id=1, source_target_pairs={{1,0},{2,1},{3,2},{5,4},{6,5},{7,6},{9,8},{10,9},{11,10},{13,12},{... | collective-permute-start | bytes 2211848 | tf_op jit(solution)/shard_map/ppermute | solution.py:19
  67.7 6.6 %collective-permute-start = (bf16[120,3072]{1,0:T(8,128)(2,1)}, bf16[120,3072]{1,0:T(8,128)(2,1)}, u32[]{:S(2)}, u32[]{:S(2)}) collective-permute-start(bf16[120,3072]{1,0:T(8,128)(2,1)} %get-tuple-element.45), channel_id=1, source_target_pairs={{0,1},{1,2},{2,3},{4,5},{5,6},{6,7},{8,9},{9,10},{10,11},{12,13},{... | collective-permute-start | bytes 2211848 | tf_op jit(solution)/shard_map/ppermute | solution.py:16
  81.7 6.4 %copy-start.9 = (bf16[480,1536]{0,1:T(8,128)(2,1)}, bf16[480,1536]{0,1:T(8,128)(2,1)S(1)}, u32[]{:S(2)}) copy-start(bf16[480,1536]{0,1:T(8,128)(2,1)S(1)} %copy.40) | copy-start | bytes 4423684
  138.5 5.4 copy-start.7
  144.2 7.9 %copy-start.6 = (bf16[240,12,128]{0,2,1:T(8,128)(2,1)}, bf16[240,12,128]{0,2,1:T(8,128)(2,1)S(1)}, u32[]{:S(2)}) copy-start(bf16[240,12,128]{0,2,1:T(8,128)(2,1)S(1)} %copy.46) | copy-start | bytes 2211844
  152.0 1.8 copy-start.3
  152.1 386.3 %reduce-scatter.5.cloned.1.call-start = ((), (), s32[]{:S(2)}) async-start(), calls=%async_computation.5 | async-start | bytes 2949120 | tf_op jit(solution)/shard_map/reduce_scatter | solution.py:88
  153.9 3.9 copy-start.8
  153.9 3.9 copy-start.11
  162.2 303.3 %copy-start.4 = (bf16[12,240,480]{1,2,0:T(8,128)(2,1)}, bf16[12,240,480]{1,2,0:T(8,128)(2,1)S(1)}, u32[]{:S(2)}) copy-start(bf16[12,240,480]{1,2,0:T(8,128)(2,1)S(1)} %multiply_convert_fusion) | copy-start | bytes 8294404
  481.7 25.4 %collective-permute-start.2 = (bf16[120,3072]{1,0:T(8,128)(2,1)}, bf16[120,3072]{1,0:T(8,128)(2,1)}, u32[]{:S(2)}, u32[]{:S(2)}) collective-permute-start(bf16[120,3072]{1,0:T(8,128)(2,1)} %copy.58), channel_id=1, source_target_pairs={{1,0},{2,1},{3,2},{5,4},{6,5},{7,6},{9,8},{10,9},{11,10},{13,12},{... | collective-permute-start | bytes 2211848 | tf_op jit(solution)/shard_map/ppermute | solution.py:27
  485.3 11.8 %copy-start.2 = (f32[480,12,128]{0,2,1:T(8,128)S(1)}, f32[480,12,128]{0,2,1:T(8,128)}, u32[]{:S(2)}) copy-start(f32[480,12,128]{0,2,1:T(8,128)} %copy.57) | copy-start | bytes 8847364
  485.3 37.2 %collective-permute-start.3 = (bf16[120,3072]{1,0:T(8,128)(2,1)}, bf16[120,3072]{1,0:T(8,128)(2,1)}, u32[]{:S(2)}, u32[]{:S(2)}) collective-permute-start(bf16[120,3072]{1,0:T(8,128)(2,1)} %copy.60), channel_id=1, source_target_pairs={{0,1},{1,2},{2,3},{4,5},{5,6},{6,7},{8,9},{9,10},{10,11},{12,13},{... | collective-permute-start | bytes 2211848 | tf_op jit(solution)/shard_map/ppermute | solution.py:27
  497.1 2.6 copy-start.5
  497.1 3.5 copy-start.10
  533.8 4.5 copy-start.1
Sparse Core Ops, SparseCore 0:
  10.2 54.7 all-gather.2
  66.6 65.2 all-gather.4
  152.2 313.2 reduce-scatter.2
  468.5 38.5 reduce-scatter.4
where the time goes:
time: 546 us; the launch traced here: 545 us
  waiting for transfers between devices  400 us (73%)
  local copies, waits for them, and re-layouts  52.5 us (10%)
  matrix products  46.2 us (8%)
  other arithmetic  21.2 us (4%)
  between operations  14 us (3%)
  starting transfers between devices  11.1 us (2%)
    reduce_scatter x1, waiting for transfers between devices, shards(): lax.psum_scatter(contract_rows(attention, grad_rows), 'dp', scatter_dimen...  303 us
    all_gather x1, waiting for transfers between devices, shards(): weight_rows = lax.all_gather(out_weight, 'dp', axis=0, tiled=True)  57 us
    all_gather x1, waiting for transfers between devices, shards(): weight_full = lax.all_gather(weight_rows, 'tile', axis=1, tiled=True)  38.8 us
  transfers between devices with their start and end apart: 8, of which 3 were waited for; matrix products, arithmetic and copies ran while one was open for 18% of the time, Pallas kernels for 0%

commit v1 on v0

v1 whole, which is shorter than its diff:
```python
import functools

import jax
import jax.numpy as jnp
from jax import lax
from jax.experimental import pallas as pl
from jax.experimental.pallas import tpu as pltpu
from jax.sharding import PartitionSpec as P

HEADS = 12
HEAD = 128
TILE = 120
GROUP = 3
SCALE = HEAD**-0.5
VMEM = 48 * 1024 * 1024
BF16 = jnp.bfloat16
F32 = jnp.float32


def dot_nn(a, b):
    return lax.dot_general(a, b, (((1,), (0,)), ((), ())), preferred_element_type=F32)


def dot_nt(a, b):
    return lax.dot_general(a, b, (((1,), (1,)), ((), ())), preferred_element_type=F32)


def dot_tn(a, b):
    return lax.dot_general(a, b, (((0,), (0,)), ((), ())), preferred_element_type=F32)


def cost(flops, nbytes, exps=0):
    return pl.CostEstimate(flops=int(flops), bytes_accessed=int(nbytes), transcendentals=int(exps))


def params():
    return pltpu.CompilerParams(vmem_limit_bytes=VMEM)


def whole():
    return pl.BlockSpec(memory_space=pltpu.VMEM)


def anywhere():
    return pl.BlockSpec(memory_space=pl.ANY)


def upper_rows(rows, cols):
    return lax.broadcasted_iota(jnp.int32, (rows, cols), 0) < TILE


def forward_kernel(q_ref, k_ref, v_ref, kl_ref, vl_ref, kr_ref, vr_ref, a_ref, p_ref, ph_ref):
    rows = q_ref.shape[0]
    position = lax.axis_index("tile")
    has_left = position > 0
    has_right = position < lax.axis_size("tile") - 1
    top = upper_rows(rows, TILE)
    seen = (top & has_left) | (jnp.logical_not(top) & has_right)
    for h in range(GROUP):
        at = pl.ds(h * HEAD, HEAD)
        q = q_ref[:, at]
        s = dot_nt(q, k_ref[:, at]) * SCALE
        sh = jnp.where(top, dot_nt(q, kl_ref[:, at]), dot_nt(q, kr_ref[:, at])) * SCALE
        sh = jnp.where(seen, sh, -1e30)
        top_score = jnp.maximum(
            jnp.max(s, axis=-1, keepdims=True), jnp.max(sh, axis=-1, keepdims=True)
        )
        e = jnp.exp(s - top_score)
        eh = jnp.exp(sh - top_score)
        total = jnp.sum(e, axis=-1, keepdims=True) + jnp.sum(eh, axis=-1, keepdims=True)
        inverse = 1.0 / total
        p = (e * inverse).astype(BF16)
        ph = eh * inverse
        p_ref[h] = p
        ph_ref[h] = ph.astype(BF16)
        out = dot_nn(p, v_ref[:, at])
        out += dot_nn(jnp.where(top, ph, 0.0).astype(BF16), vl_ref[:, at])
        out += dot_nn(jnp.where(top, 0.0, ph).astype(BF16), vr_ref[:, at])
        a_ref[:, at] = out.astype(BF16)


def halo_specs(groups, width):
    keys = pl.BlockSpec((TILE, width), lambda g: (0, g))
    values = pl.BlockSpec((TILE, width), lambda g: (0, groups + g))
    return keys, values


def attention_forward(q, k, v, left, right):
    rows, feats = q.shape
    width = GROUP * HEAD
    groups = feats // width
    col = pl.BlockSpec((rows, width), lambda g: (0, g))
    hk, hv = halo_specs(groups, width)
    return pl.pallas_call(
        forward_kernel,
        grid=(groups,),
        in_specs=[col, col, col, hk, hv, hk, hv],
        out_specs=[
            col,
            pl.BlockSpec((GROUP, rows, rows), lambda g: (g, 0, 0)),
            pl.BlockSpec((GROUP, rows, TILE), lambda g: (g, 0, 0)),
        ],
        out_shape=[
            jax.ShapeDtypeStruct((rows, feats), BF16),
            jax.ShapeDtypeStruct((HEADS, rows, rows), BF16),
            jax.ShapeDtypeStruct((HEADS, rows, TILE), BF16),
        ],
        compiler_params=params(),
        cost_estimate=cost(1.4e9, 8e6, 1.4e6),
        name="attention_forward",
    )(q, k, v, left, left, right, right)


def halo_backward_kernel(
    go_ref, gr_ref, a_ref, q_ref, vl_ref, vr_ref, ph_ref, ga_ref, ds_ref, kl_ref, vl_out, kr_ref, vr_out
):
    rows = q_ref.shape[0]
    top = upper_rows(rows, TILE)
    for h in range(GROUP):
        at = pl.ds(h * HEAD, HEAD)
        q = q_ref[:, at]
        ga = (go_ref[:, at] + gr_ref[:, at].astype(F32)).astype(BF16)
        ga_ref[:, at] = ga
        dots = jnp.sum(ga.astype(F32) * a_ref[:, at].astype(F32), axis=-1, keepdims=True)
        dp = jnp.where(top, dot_nt(ga, vl_ref[:, at]), dot_nt(ga, vr_ref[:, at]))
        ph = ph_ref[h].astype(F32)
        ds = ph * (dp - dots)
        ds_ref[h] = ds.astype(BF16)
        kl_ref[:, at] = (dot_tn(jnp.where(top, ds, 0.0).astype(BF16), q) * SCALE).astype(BF16)
        kr_ref[:, at] = (dot_tn(jnp.where(top, 0.0, ds).astype(BF16), q) * SCALE).astype(BF16)
        vl_out[:, at] = dot_tn(jnp.where(top, ph, 0.0).astype(BF16), ga).astype(BF16)
        vr_out[:, at] = dot_tn(jnp.where(top, 0.0, ph).astype(BF16), ga).astype(BF16)


def halo_backward(grad_own, grad_recv, att, q, left, right, probs_halo):
    rows, feats = q.shape
    width = GROUP * HEAD
    groups = feats // width
    col = pl.BlockSpec((rows, width), lambda g: (0, g))
    rim = pl.BlockSpec((TILE, width), lambda g: (0, g))
    _, hv = halo_specs(groups, width)
    heads = pl.BlockSpec((GROUP, rows, TILE), lambda g: (g, 0, 0))
    return pl.pallas_call(
        halo_backward_kernel,
        grid=(groups,),
        in_specs=[col, col, col, col, hv, hv, heads],
        out_specs=[col, heads, rim, rim, rim, rim],
        out_shape=[
            jax.ShapeDtypeStruct((rows, feats), BF16),
            jax.ShapeDtypeStruct((HEADS, rows, TILE), BF16),
        ]
        + [jax.ShapeDtypeStruct((TILE, feats), BF16)] * 4,
        compiler_params=params(),
        cost_estimate=cost(1.0e9, 8e6),
        name="halo_backward",
    )(grad_own, grad_recv, att, q, left, right, probs_halo)


def main_backward_kernel(
    ga_ref, a_ref, q_ref, k_ref, v_ref, kl_ref, kr_ref, p_ref, dsh_ref, dq_ref, dk_ref, dv_ref
):
    rows = q_ref.shape[0]
    top = upper_rows(rows, TILE)
    for h in range(GROUP):
        at = pl.ds(h * HEAD, HEAD)
        q = q_ref[:, at]
        ga = ga_ref[:, at]
        dots = jnp.sum(ga.astype(F32) * a_ref[:, at].astype(F32), axis=-1, keepdims=True)
        p = p_ref[h]
        ds = (p.astype(F32) * (dot_nt(ga, v_ref[:, at]) - dots)).astype(BF16)
        dsh = dsh_ref[h].astype(F32)
        dq = dot_nn(ds, k_ref[:, at])
        dq += dot_nn(jnp.where(top, dsh, 0.0).astype(BF16), kl_ref[:, at])
        dq += dot_nn(jnp.where(top, 0.0, dsh).astype(BF16), kr_ref[:, at])
        dq_ref[:, at] = (dq * SCALE).astype(BF16)
        dk_ref[:, at] = dot_tn(ds, q) * SCALE
        dv_ref[:, at] = dot_tn(p, ga)


def main_backward(ga, att, q, k, v, left, right, probs, ds_halo):
    rows, feats = q.shape
    width = GROUP * HEAD
    groups = feats // width
    col = pl.BlockSpec((rows, width), lambda g: (0, g))
    hk, _ = halo_specs(groups, width)
    return pl.pallas_call(
        main_backward_kernel,
        grid=(groups,),
        in_specs=[
            col,
            col,
            col,
            col,
            col,
            hk,
            hk,
            pl.BlockSpec((GROUP, rows, rows), lambda g: (g, 0, 0)),
            pl.BlockSpec((GROUP, rows, TILE), lambda g: (g, 0, 0)),
        ],
        out_specs=[col, col, col],
        out_shape=[
            jax.ShapeDtypeStruct((rows, feats), BF16),
            jax.ShapeDtypeStruct((rows, feats), F32),
            jax.ShapeDtypeStruct((rows, feats), F32),
        ],
        compiler_params=params(),
        cost_estimate=cost(1.5e9, 1e7),
        name="main_backward",
    )(ga, att, q, k, v, left, right, probs, ds_halo)


def add_rims_body(own_k, own_v, lk, lv, rk, rv, out_k, out_v):
    rows = own_k.shape[0]
    for own, low, high, out in ((own_k, lk, rk, out_k), (own_v, lv, rv, out_v)):
        extra = jnp.concatenate([low[...].astype(F32), high[...].astype(F32)], axis=0)
        out[...] = (own[...] + extra[:rows]).astype(BF16)


def add_rims(dk, dv, lk, lv, rk, rv):
    rows, feats = dk.shape
    width = GROUP * HEAD
    col = pl.BlockSpec((rows, width), lambda g: (0, g))
    rim = pl.BlockSpec((TILE, width), lambda g: (0, g))
    return pl.pallas_call(
        add_rims_body,
        grid=(feats // width,),
        in_specs=[col, col, rim, rim, rim, rim],
        out_specs=[col, col],
        out_shape=[jax.ShapeDtypeStruct((rows, feats), BF16)] * 2,
        compiler_params=params(),
        cost_estimate=cost(1e6, 6e6),
        name="add_rims",
    )(dk, dv, lk, lv, rk, rv)


def grad_attention_kernel(c_ref, w_own, w_other, out_ref, *, sliced):
    place = lax.axis_index("tile")
    core = lax.rem(place, 2)
    half = lax.div(place, 2) if sliced else 0
    width = w_own.shape[1]
    own_at = pl.multiple_of((2 * half + core) * width, 128)
    other_at = pl.multiple_of((2 * half + 1 - core) * width, 128)
    total = dot_nt(c_ref[:, pl.ds(own_at, width)], w_own[...])
    total += dot_nt(c_ref[:, pl.ds(other_at, width)], w_other[...])
    out_ref[...] = total.astype(out_ref.dtype)


def grad_attention_part(cot, w_own, w_other, dtype, sliced):
    rows = cot.shape[0]
    feats, width = w_own.shape
    steps = 4
    block = feats // steps
    wspec = pl.BlockSpec((block, width), lambda g: (g, 0))
    return pl.pallas_call(
        functools.partial(grad_attention_kernel, sliced=sliced),
        grid=(steps,),
        in_specs=[pl.BlockSpec(cot.shape, lambda g: (0, 0)), wspec, wspec],
        out_specs=pl.BlockSpec((rows, block), lambda g: (0, g)),
        out_shape=jax.ShapeDtypeStruct((rows, feats), dtype),
        compiler_params=params(),
        cost_estimate=cost(4 * rows * feats * width, 7e6),
        name="grad_attention_part",
    )(cot, w_own, w_other)


def project_kernel(a_ref, w_own, w_other, out_ref):
    core = lax.rem(lax.axis_index("tile"), 2)
    width = w_own.shape[1]
    a = a_ref[...]
    out_ref[:, pl.ds(pl.multiple_of(core * width, 128), width)] = dot_nn(a, w_own[...]).astype(BF16)
    out_ref[:, pl.ds(pl.multiple_of((1 - core) * width, 128), width)] = dot_nn(
        a, w_other[...]
    ).astype(BF16)


def project_half(att, w_own, w_other):
    rows = att.shape[0]
    feats, width = w_own.shape
    return pl.pallas_call(
        project_kernel,
        in_specs=[whole()] * 3,
        out_specs=whole(),
        out_shape=jax.ShapeDtypeStruct((rows, 2 * width), BF16),
        compiler_params=params(),
        cost_estimate=cost(4 * rows * feats * width, 7e6),
        name="project_half",
    )(att, w_own, w_other)


def project_out_kernel(mine, theirs, out_ref):
    half = lax.div(lax.axis_index("tile"), 2)
    width = mine.shape[1]
    out_ref[:, pl.ds(pl.multiple_of(half * width, 128), width)] = mine[...]
    out_ref[:, pl.ds(pl.multiple_of((1 - half) * width, 128), width)] = theirs[...]


def project_out(mine, theirs):
    rows, width = mine.shape
    return pl.pallas_call(
        project_out_kernel,
        in_specs=[whole()] * 2,
        out_specs=whole(),
        out_shape=jax.ShapeDtypeStruct((rows, 2 * width), BF16),
        compiler_params=params(),
        cost_estimate=cost(1e5, 3e6),
        name="project_out",
    )(mine, theirs)


def assemble_kernel(*refs, places):
    *pieces, out, sems = refs
    pos = lax.axis_index("dp")
    z, x = lax.div(pos, 2), lax.rem(pos, 2)
    rows = pieces[0].shape[0]
    copies = []
    for i, (piece, (shift, flip)) in enumerate(zip(pieces, places)):
        block = 2 * lax.rem(z + 4 - shift, 4) + (1 - x if flip else x)
        start = pl.multiple_of(block * rows, 16)
        copies.append(pltpu.make_async_copy(piece, out.at[pl.ds(start, rows)], sems.at[i]))
    for copy in copies:
        copy.start()
    for copy in copies:
        copy.wait()


def assemble(pieces, places):
    rows, width = pieces[0].shape
    n = len(pieces)
    return pl.pallas_call(
        functools.partial(assemble_kernel, places=places),
        in_specs=[anywhere()] * n,
        out_specs=anywhere(),
        out_shape=jax.ShapeDtypeStruct((n * rows, width), BF16),
        scratch_shapes=[pltpu.SemaphoreType.DMA((n,))],
        compiler_params=params(),
        cost_estimate=cost(0, 5e6),
        name="assemble_weight",
    )(*pieces)


def dp_shift(block, shift, flip):
    route = []
    for z in range(4):
        for x in range(2):
            to = 2 * ((z + shift) % 4) + (1 - x if flip else x)
            route.append((2 * z + x, to))
    return lax.ppermute(block, "dp", route)


def gather_weight(shard):
    if lax.axis_size("dp") != 8:
        return lax.all_gather(shard, "dp", axis=0, tiled=True)
    pieces = {(0, False): shard}
    for shift in (1, 3, 2):
        pieces[shift, False] = dp_shift(shard, shift, False)
    for shift in (0, 1, 3, 2):
        pieces[shift, True] = dp_shift(pieces[shift, False], 0, True)
    places = tuple(pieces)
    return assemble([pieces[p] for p in places], places)


def weight_grad_kernel(a0, a1, a2, a3, c0, c1, c2, c3, keep_ref, send_ref, total, *, shift):
    pos = lax.axis_index("dp")
    z, x = lax.div(pos, 2), lax.rem(pos, 2)
    rows = total.shape[0]
    half = rows // 2
    start = pl.multiple_of(lax.rem(z + shift, 4) * rows, 128)
    acc = dot_tn(a0[:, pl.ds(start, rows)], c0[...])
    acc += dot_tn(a1[:, pl.ds(start, rows)], c1[...])
    acc += dot_tn(a2[:, pl.ds(start, rows)], c2[...])
    acc += dot_tn(a3[:, pl.ds(start, rows)], c3[...])
    total[...] = acc
    keep_ref[...] = total[pl.ds(pl.multiple_of(x * half, 16), half), :]
    send_ref[...] = total[pl.ds(pl.multiple_of((1 - x) * half, 16), half), :].astype(BF16)


def weight_grad_part(atts, cots, shift):
    rows, feats = atts[0].shape
    width = cots[0].shape[1]
    part = feats // 4
    return pl.pallas_call(
        functools.partial(weight_grad_kernel, shift=shift),
        in_specs=[whole()] * 8,
        out_specs=[whole()] * 2,
        out_shape=[
            jax.ShapeDtypeStruct((part // 2, width), F32),
            jax.ShapeDtypeStruct((part // 2, width), BF16),
        ],
        scratch_shapes=[pltpu.VMEM((part, width), F32)],
        compiler_params=params(),
        cost_estimate=cost(8 * rows * part * width, 6e6),
        name="weight_grad_part",
    )(*atts, *cots)


def weight_grad_sum(atts, cots):
    if lax.axis_size("dp") != 8:
        total = sum(dot_tn(a, c) for a, c in zip(atts, cots))
        return lax.psum_scatter(total, "dp", scatter_dimension=0, tiled=True)
    arrived = []
    for shift in (2, 1, 3):
        keep, send = weight_grad_part(atts, cots, shift)
        both = keep + dp_shift(send, 0, True).astype(F32)
        arrived.append(dp_shift(both.astype(BF16), shift, False))
    keep, send = weight_grad_part(atts, cots, 0)
    total = keep + dp_shift(send, 0, True).astype(F32)
    for block in arrived:
        total = total + block.astype(F32)
    return total


def along_tile(block, distance):
    count = lax.axis_size("tile")
    route = [(i, i + distance) for i in range(count) if 0 <= i + distance < count]
    return lax.ppermute(block, "tile", route)


def to_partner(block):
    return lax.ppermute(block, "tile", [(0, 2), (1, 3), (2, 0), (3, 1)])


def to_core(block):
    return lax.ppermute(block, "tile", [(0, 1), (1, 0), (2, 3), (3, 2)])


def shards(queries, key_vectors, value_vectors, out_weight, cotangent):
    q, k, v, cot = queries[0], key_vectors[0], value_vectors[0], cotangent[0]
    tokens, feats = q.shape
    model = cot.shape[1]
    place = lax.axis_index("tile")
    y, core = place // 2, place % 2
    quarter = model // 4

    left = along_tile(jnp.concatenate([k[tokens - TILE :], v[tokens - TILE :]], axis=1), 1)
    right = along_tile(jnp.concatenate([k[:TILE], v[:TILE]], axis=1), -1)
    w_own = gather_weight(out_weight)
    w_other = to_core(w_own)
    cot_partner = to_partner(lax.dynamic_slice_in_dim(cot, (1 - y) * (model // 2), model // 2, axis=1))

    att, probs, probs_halo = attention_forward(q, k, v, left, right)
    att_partner = to_partner(att)

    grad_partner = grad_attention_part(cot_partner, w_own, w_other, BF16, False)
    grad_recv = to_partner(grad_partner)
    grad_own = grad_attention_part(cot, w_own, w_other, F32, True)

    my_at = (2 * y + core) * quarter
    sib_at = (2 * y + 1 - core) * quarter
    c_own = lax.dynamic_slice_in_dim(cot, my_at, quarter, axis=1)
    c_sib = to_core(lax.dynamic_slice_in_dim(cot, sib_at, quarter, axis=1))
    c_par = lax.dynamic_slice_in_dim(cot_partner, core * quarter, quarter, axis=1)
    c_sibpar = to_core(
        lax.dynamic_slice_in_dim(cot_partner, (1 - core) * quarter, quarter, axis=1)
    )
    a_sib = to_core(att)
    a_sibpar = to_core(att_partner)
    weight_grad = weight_grad_sum(
        (att, a_sib, att_partner, a_sibpar), (c_own, c_sib, c_par, c_sibpar)
    )

    proj_partner = project_half(att_partner, w_own, w_other)
    proj_recv = to_partner(proj_partner)
    proj_own = project_half(att, w_own, w_other)
    projected = project_out(proj_own, proj_recv)

    ga, ds_halo, kl, vl, kr, vr = halo_backward(
        grad_own, grad_recv, att, q, left, right, probs_halo
    )
    lk, lv = along_tile(kr, 1), along_tile(vr, 1)
    rk, rv = along_tile(kl, -1), along_tile(vl, -1)
    dq, dk, dv = main_backward(ga, att, q, k, v, left, right, probs, ds_halo)
    dk, dv = add_rims(dk, dv, lk, lv, rk, rv)
    return projected[None], dq[None], dk[None], dv[None], weight_grad


def solution(mesh):
    tokens = P("dp", "tile", None)
    weight = P("dp", "tile")
    return jax.shard_map(
        shards,
        mesh=mesh,
        in_specs=(tokens, tokens, tokens, weight, tokens),
        out_specs=(tokens, tokens, tokens, tokens, weight),
        check_vma=False,
    )
```

time: 546 us -> 174 us (0.32)
  waiting for transfers between devices: 400 us -> 59.3 us
  Pallas kernels: 0 us -> 50.4 us
  matrix products: 46.2 us -> 0 us
  local copies, waits for them, and re-layouts: 52.5 us -> 15.2 us
  starting transfers between devices: 11.1 us -> 41.7 us
  other arithmetic: 21.2 us -> 4.43 us
  between operations: 14 us -> 0.96 us
    reduce_scatter x2 -> x0, waiting for transfers between devices: 303 us -> none  [the longest x1 303 us: shards(): lax.psum_scatter(contract_rows(attention, grad_rows), 'dp', scatter_dimen...]
    all_gather x2 -> x0, waiting for transfers between devices: 95.9 us -> none  [the longest x1 57 us: shards(): weight_rows = lax.all_gather(out_weight, 'dp', axis=0, tiled=True)]
    ppermute x4 -> x29, waiting for transfers between devices: 0.01 us -> 59.3 us  [the longest x4 36.1 us: to_partner(): return lax.ppermute(block, 'tile', [(0, 2), (1, 3), (2, 0), (3, 1)])]
    pallas_call x0 -> x14, Pallas kernels: none -> 50.4 us  [the longest x4 10.5 us: weight_grad_part(): pl.pallas_call(functools.partial(weight_grad_kernel, shift=shift), in_spe...]
    dot_general x8 -> x0, matrix products: 39.8 us -> none  [the longest x1 7.84 us: contract_rows(): lax.dot_general(left, right, (((0,), (0,)), ((), ())), preferred_element_...]
    ppermute x4 -> x29, starting transfers between devices: 10.7 us -> 41.7 us  [the longest x14 18.8 us: dp_shift(): return lax.ppermute(block, 'dp', route)]
    scatter-add x2 -> x0, local copies, waits for them, and re-layouts: 18.1 us -> none  [the longest x1 9.82 us: shards(): own_grads = own_grads.at[tokens - TILE:].add(from_right.astype(jnp.float32))]
    slice x6 -> x1, local copies, waits for them, and re-layouts: 10.7 us -> 1.44 us  [shards(): right = along_tile(jnp.concatenate([k[:TILE], v[:TILE]], axis=1), -1)]
  transfers between devices with their start and end apart: 8 -> 29, of which waited for: 3 -> 8; matrix products, arithmetic and copies ran while one was open for 18% -> 6% of each run, Pallas kernels for 0% -> 28%
where the time goes in v1:
time: 174 us; the launch traced here: 172 us
  waiting for transfers between devices  59.3 us (34%)
  Pallas kernels  50.4 us (29%)
  starting transfers between devices  41.7 us (24%)
  local copies, waits for them, and re-layouts  15.2 us (9%)
  other arithmetic  4.43 us (3%)
    ppermute x4, waiting for transfers between devices, to_partner(): return lax.ppermute(block, 'tile', [(0, 2), (1, 3), (2, 0), (3, 1)])  36.1 us
    ppermute x14, waiting for transfers between devices, dp_shift(): return lax.ppermute(block, 'dp', route)  21.9 us
    ppermute x14, starting transfers between devices, dp_shift(): return lax.ppermute(block, 'dp', route)  18.8 us
    ppermute x6, starting transfers between devices, along_tile(): return lax.ppermute(block, 'tile', route)  11.3 us
    pallas_call x4, Pallas kernels, weight_grad_part(): pl.pallas_call(functools.partial(weight_grad_kernel, shift=shift), in_spe...  10.5 us
    unnamed x32, local copies, waits for them, and re-layouts  9.82 us
    pallas_call x2, Pallas kernels, grad_attention_part(): pl.pallas_call(functools.partial(grad_attention_kernel, sliced=sliced), g...  8.38 us
    pallas_call x1, Pallas kernels, attention_forward(): pl.pallas_call(forward_kernel, grid=(groups,), in_specs=[col, col, col, h...  8.32 us
  transfers between devices with their start and end apart: 29, of which 8 were waited for; matrix products, arithmetic and copies ran while one was open for 6% of the time, Pallas kernels for 28%

profile of v1, /device:TPU:0, one launch (start us, length us, event | category | flops | bytes accessed | tf_op | source)
XLA Modules:
  0.0 172.0 jit_solution(17197694953148629774)
XLA Ops:
  0.6 3.1 %collective-permute-start.2 = (bf16[192,768]{1,0:T(8,128)(2,1)}, bf16[192,768]{1,0:T(8,128)(2,1)S(1)}, u32[]{:S(2)}, u32[]{:S(2)}) collective-permute-start(bf16[192,768]{1,0:T(8,128)(2,1)} %refs_0_.1), channel_id=1, source_target_pairs={{0,8},{4,12},{8,16},{12,20},{16,24},{20,28},{24,0},{28,4},{1,9},{5... | collective-permute-start | bytes 884744 | tf_op jit(solution)/shard_map/ppermute | solution.py:347
  3.7 2.1 %collective-permute-start.3 = (bf16[192,768]{1,0:T(8,128)(2,1)}, bf16[192,768]{1,0:T(8,128)(2,1)S(1)}, u32[]{:S(2)}, u32[]{:S(2)}) collective-permute-start(bf16[192,768]{1,0:T(8,128)(2,1)} %refs_0_.1), channel_id=1, source_target_pairs={{0,24},{4,28},{8,0},{12,4},{16,8},{20,12},{24,16},{28,20},{1,25},{... | collective-permute-start | bytes 884744 | tf_op jit(solution)/shard_map/ppermute | solution.py:347
  15.6 3.1 %collective-permute-done.3.refs_2_ = bf16[192,768]{1,0:T(8,128)(2,1)S(1)} collective-permute-done((bf16[192,768]{1,0:T(8,128)(2,1)}, bf16[192,768]{1,0:T(8,128)(2,1)S(1)}, u32[]{:S(2)}, u32[]{:S(2)}) %collective-permute-start.3) | collective-permute-done | bytes 294944 | tf_op jit(solution)/shard_map/ppermute | solution.py:347
  20.2 11.7 %collective-permute-done.4.refs_3_ = bf16[192,768]{1,0:T(8,128)(2,1)S(1)} collective-permute-done((bf16[192,768]{1,0:T(8,128)(2,1)}, bf16[192,768]{1,0:T(8,128)(2,1)S(1)}, u32[]{:S(2)}, u32[]{:S(2)}) %collective-permute-start.4) | collective-permute-done | bytes 294944 | tf_op jit(solution)/shard_map/ppermute | solution.py:347
  35.7 5.2 %collective-permute-done.8.refs_7_ = bf16[192,768]{1,0:T(8,128)(2,1)S(1)} collective-permute-done((bf16[192,768]{1,0:T(8,128)(2,1)S(1)}, bf16[192,768]{1,0:T(8,128)(2,1)S(1)}, u32[]{:S(2)}, u32[]{:S(2)}) %collective-permute-start.8) | collective-permute-done | bytes 294944 | tf_op jit(solution)/shard_map/ppermute | solution.py:347
  46.9 8.3 %attention_forward.1 = (bf16[240,1536]{1,0:T(8,128)(2,1)S(1)}, bf16[12,240,240]{2,1,0:T(8,128)(2,1)}, bf16[12,240,120]{2,1,0:T(8,128)(2,1)S(1)}) custom-call(bf16[240,1536]{1,0:T(8,128)(2,1)S(1)} %bitcast.23, bf16[240,1536]{1,0:T(8,128)(2,1)S(1)} %bitcast.26, bf16[240,1536]{1,0:T(8,128)(2,1)S(1)} %bitcast.28, bf16[120,3072]{1,0:T(8,128)(2,1)S(1)} %copy-done.10, ...), custom_call_target="tpu_custom_call" | custom-call | flops 1400000000 | bytes 8000000 | tf_op jit(solution)/shard_map/attention_forward/pallas_call | solution.py:94
  55.2 4.6 %collective-permute-start.10 = (bf16[240,1536]{1,0:T(8,128)(2,1)S(1)}, bf16[240,1536]{1,0:T(8,128)(2,1)}, u32[]{:S(2)}, u32[]{:S(2)}) collective-permute-start(bf16[240,1536]{1,0:T(8,128)(2,1)S(1)} %get-tuple-element.27.a_ref.a0), channel_id=1, source_target_pairs={{0,2},{1,3},{2,0},{3,1},{4,6},{5,7},{6,4},{7,5},{8,10},{9,11},{10,... | collective-permute-start | bytes 2211848 | tf_op jit(solution)/shard_map/ppermute | solution.py:419
  62.5 14.1 %collective-permute-done.10.a_ref.a2 = bf16[240,1536]{1,0:T(8,128)(2,1)} collective-permute-done((bf16[240,1536]{1,0:T(8,128)(2,1)S(1)}, bf16[240,1536]{1,0:T(8,128)(2,1)}, u32[]{:S(2)}, u32[]{:S(2)}) %collective-permute-start.10) | collective-permute-done | bytes 737312 | tf_op jit(solution)/shard_map/ppermute | solution.py:419
  76.6 2.1 %collective-permute-start.19 = (bf16[240,1536]{1,0:T(8,128)(2,1)}, bf16[240,1536]{1,0:T(8,128)(2,1)}, u32[]{:S(2)}, u32[]{:S(2)}) collective-permute-start(bf16[240,1536]{1,0:T(8,128)(2,1)} %collective-permute-done.10.a_ref.a2), channel_id=1, source_target_pairs={{0,1},{1,0},{2,3},{3,2},{4,5},{5,4},{6,7},{7,6},{8,9},{9,8},{10,11... | collective-permute-start | bytes 2211848 | tf_op jit(solution)/shard_map/ppermute | solution.py:423
  80.7 11.5 %collective-permute-done.12.c_ref = bf16[240,1536]{1,0:T(8,128)(2,1)} collective-permute-done((bf16[240,1536]{1,0:T(8,128)(2,1)}, bf16[240,1536]{1,0:T(8,128)(2,1)}, u32[]{:S(2)}, u32[]{:S(2)}) %collective-permute-start.12) | collective-permute-done | bytes 737312 | tf_op jit(solution)/shard_map/ppermute | solution.py:419
  95.5 2.6 %weight_grad_part.7 = (f32[192,768]{1,0:T(8,128)S(1)}, bf16[192,768]{1,0:T(8,128)(2,1)S(1)}) custom-call(bf16[240,1536]{1,0:T(8,128)(2,1)S(1)} %get-tuple-element.27.a_ref.a0, bf16[240,1536]{1,0:T(8,128)(2,1)} %collective-permute-done.18.a1, bf16[240,1536]{1,0:T(8,128)(2,1)} %collective-permute-done.10.a_ref.a2, ...), custom_call_target="tpu_custom_call" | custom-call | flops 566231040 | bytes 6000000 | tf_op jit(solution)/shard_map/weight_grad_part/pallas_call | solution.py:381
  98.7 2.6 %weight_grad_part.6 = (f32[192,768]{1,0:T(8,128)S(1)}, bf16[192,768]{1,0:T(8,128)(2,1)S(1)}) custom-call(bf16[240,1536]{1,0:T(8,128)(2,1)S(1)} %get-tuple-element.27.a_ref.a0, bf16[240,1536]{1,0:T(8,128)(2,1)} %collective-permute-done.18.a1, bf16[240,1536]{1,0:T(8,128)(2,1)} %collective-permute-done.10.a_ref.a2, ...), custom_call_target="tpu_custom_call" | custom-call | flops 566231040 | bytes 6000000 | tf_op jit(solution)/shard_map/weight_grad_part/pallas_call | solution.py:381
  102.9 2.6 %weight_grad_part.5 = (f32[192,768]{1,0:T(8,128)S(1)}, bf16[192,768]{1,0:T(8,128)(2,1)S(1)}) custom-call(bf16[240,1536]{1,0:T(8,128)(2,1)S(1)} %get-tuple-element.27.a_ref.a0, bf16[240,1536]{1,0:T(8,128)(2,1)} %collective-permute-done.18.a1, bf16[240,1536]{1,0:T(8,128)(2,1)} %collective-permute-done.10.a_ref.a2, ...), custom_call_target="tpu_custom_call" | custom-call | flops 566231040 | bytes 6000000 | tf_op jit(solution)/shard_map/weight_grad_part/pallas_call | solution.py:381
  106.1 2.6 %weight_grad_part.4 = (f32[192,768]{1,0:T(8,128)S(1)}, bf16[192,768]{1,0:T(8,128)(2,1)S(1)}) custom-call(bf16[240,1536]{1,0:T(8,128)(2,1)S(1)} %get-tuple-element.27.a_ref.a0, bf16[240,1536]{1,0:T(8,128)(2,1)} %collective-permute-done.18.a1, bf16[240,1536]{1,0:T(8,128)(2,1)} %collective-permute-done.10.a_ref.a2, ...), custom_call_target="tpu_custom_call" | custom-call | flops 566231040 | bytes 6000000 | tf_op jit(solution)/shard_map/weight_grad_part/pallas_call | solution.py:381
  110.3 4.3 %grad_attention_part.3 = bf16[240,1536]{1,0:T(8,128)(2,1)S(1)} custom-call(bf16[240,1536]{1,0:T(8,128)(2,1)} %collective-permute-done.12.c_ref, bf16[1536,768]{1,0:T(8,128)(2,1)S(1)} %assemble_weight.1.w_own, bf16[1536,768]{1,0:T(8,128)(2,1)} %collective-permute-done.9.w_other), custom_call_target="tpu_custom_call" | custom-call | flops 1132462080 | bytes 7000000 | tf_op jit(solution)/shard_map/grad_attention_part/pallas_call | solution.py:254
  114.6 2.2 %collective-permute-start.13 = (bf16[240,1536]{1,0:T(8,128)(2,1)S(1)}, bf16[240,1536]{1,0:T(8,128)(2,1)S(1)}, u32[]{:S(2)}, u32[]{:S(2)}) collective-permute-start(bf16[240,1536]{1,0:T(8,128)(2,1)S(1)} %grad_attention_part.3), channel_id=1, source_target_pairs={{0,2},{1,3},{2,0},{3,1},{4,6},{5,7},{6,4},{7,5},{8,10},{9,11},{10,... | collective-permute-start | bytes 2211848 | tf_op jit(solution)/shard_map/ppermute | solution.py:419
  120.3 3.3 %project_half.3 = bf16[240,1536]{1,0:T(8,128)(2,1)S(1)} custom-call(bf16[240,1536]{1,0:T(8,128)(2,1)} %collective-permute-done.10.a_ref.a2, bf16[1536,768]{1,0:T(8,128)(2,1)S(1)} %assemble_weight.1.w_own, bf16[1536,768]{1,0:T(8,128)(2,1)} %collective-permute-done.9.w_other), custom_call_target="tpu_custom_call" | custom-call | flops 1132462080 | bytes 7000000 | tf_op jit(solution)/shard_map/project_half/pallas_call | solution.py:279
  123.8 10.4 %collective-permute-done.13.gr_ref = bf16[240,1536]{1,0:T(8,128)(2,1)S(1)} collective-permute-done((bf16[240,1536]{1,0:T(8,128)(2,1)S(1)}, bf16[240,1536]{1,0:T(8,128)(2,1)S(1)}, u32[]{:S(2)}, u32[]{:S(2)}) %collective-permute-start.13) | collective-permute-done | bytes 737312 | tf_op jit(solution)/shard_map/ppermute | solution.py:419
  134.3 4.1 %grad_attention_part.2.go_ref = f32[240,1536]{1,0:T(8,128)S(1)} custom-call(bf16[240,3072]{1,0:T(8,128)(2,1)S(1)} %bitcast.22, bf16[1536,768]{1,0:T(8,128)(2,1)S(1)} %assemble_weight.1.w_own, bf16[1536,768]{1,0:T(8,128)(2,1)} %collective-permute-done.9.w_other), custom_call_target="tpu_custom_call" | custom-call | flops 1132462080 | bytes 7000000 | tf_op jit(solution)/shard_map/grad_attention_part/pallas_call | solution.py:254
  139.5 5.9 %halo_backward.1 = (bf16[240,1536]{1,0:T(8,128)(2,1)S(1)}, bf16[12,240,120]{2,1,0:T(8,128)(2,1)S(1)}, bf16[120,1536]{1,0:T(8,128)(2,1)S(1)}, bf16[120,1536]{1,0:...) custom-call(f32[240,1536]{1,0:T(8,128)} %copy-done.2, ...), custom_call_target="tpu_custom_call" | custom-call | flops 1000000000 | bytes 8000000 | tf_op jit(solution)/shard_map/halo_backward/pallas_call | solution.py:143
  146.8 4.6 %collective-permute-start.15 = (bf16[120,1536]{1,0:T(8,128)(2,1)S(1)}, bf16[120,1536]{1,0:T(8,128)(2,1)S(1)}, u32[]{:S(2)}, u32[]{:S(2)}) collective-permute-start(bf16[120,1536]{1,0:T(8,128)(2,1)S(1)} %get-tuple-element.36), channel_id=1, source_target_pairs={{0,1},{1,2},{2,3},{4,5},{5,6},{6,7},{8,9},{9,10},{10,11},{12,13},{... | collective-permute-start | bytes 1105928 | tf_op jit(solution)/shard_map/ppermute | solution.py:415
  155.2 3.0 %project_half.2.mine = bf16[240,1536]{1,0:T(8,128)(2,1)S(1)} custom-call(bf16[240,1536]{1,0:T(8,128)(2,1)S(1)} %get-tuple-element.27.a_ref.a0, bf16[1536,768]{1,0:T(8,128)(2,1)S(1)} %assemble_weight.1.w_own, bf16[1536,768]{1,0:T(8,128)(2,1)} %collective-permute-done.9.w_other), custom_call_target="tpu_custom_call" | custom-call | flops 1132462080 | bytes 7000000 | tf_op jit(solution)/shard_map/project_half/pallas_call | solution.py:279
  160.0 7.2 %main_backward.1 = (bf16[240,1536]{1,0:T(8,128)(2,1)}, f32[240,1536]{1,0:T(8,128)}, f32[240,1536]{1,0:T(8,128)}) custom-call(bf16[240,1536]{1,0:T(8,128)(2,1)S(1)} %get-tuple-element.29.ga_ref, bf16[240,1536]{1,0:T(8,128)(2,1)S(1)} %get-tuple-element.27.a_ref.a0, bf16[240,1536]{1,0:T(8,128)(2,1)S(1)} %bitcast.25, bf16[240,1536]{1,0:T(8,128)(2,1)S(1)} %bitcast.27, ...), custom_call_target="tpu_custom_call" | custom-call | flops 1500000000 | bytes 10000000 | tf_op jit(solution)/shard_map/main_backward/pallas_call | solution.py:186
  170.0 2.0 %add_rims.1 = (bf16[240,1536]{1,0:T(8,128)(2,1)}, bf16[240,1536]{1,0:T(8,128)(2,1)}) custom-call(f32[240,1536]{1,0:T(8,128)S(1)} %copy-done.12, f32[240,1536]{1,0:T(8,128)S(1)} %copy-done.13, bf16[120,1536]{1,0:T(8,128)(2,1)S(1)} %collective-permute-done.14.lk, bf16[120,1536]{1,0:T(8,128)(2,1)S(1)} %collective-permute-done.15.lv, ...), custom_call_target="tpu_custom_call" | custom-call | flops 1000000 | bytes 6000000 | tf_op jit(solution)/shard_map/add_rims/pallas_call | solution.py:224
  (90 shorter events, 47.6 us)
Async XLA Ops:
  3.7 15.0 %collective-permute-start.3 = (bf16[192,768]{1,0:T(8,128)(2,1)}, bf16[192,768]{1,0:T(8,128)(2,1)S(1)}, u32[]{:S(2)}, u32[]{:S(2)}) collective-permute-start(bf16[192,768]{1,0:T(8,128)(2,1)} %refs_0_.1), channel_id=1, source_target_pairs={{0,24},{4,28},{8,0},{12,4},{16,8},{20,12},{24,16},{28,20},{1,25},{... | collective-permute-start | bytes 884744 | tf_op jit(solution)/shard_map/ppermute | solution.py:347
  5.8 26.1 %collective-permute-start.4 = (bf16[192,768]{1,0:T(8,128)(2,1)}, bf16[192,768]{1,0:T(8,128)(2,1)S(1)}, u32[]{:S(2)}, u32[]{:S(2)}) collective-permute-start(bf16[192,768]{1,0:T(8,128)(2,1)} %refs_0_.1), channel_id=1, source_target_pairs={{0,16},{4,20},{8,24},{12,28},{16,0},{20,4},{24,8},{28,12},{1,17},{... | collective-permute-start | bytes 884744 | tf_op jit(solution)/shard_map/ppermute | solution.py:347
  6.7 27.6 %collective-permute-start.5 = (bf16[192,768]{1,0:T(8,128)(2,1)}, bf16[192,768]{1,0:T(8,128)(2,1)S(1)}, u32[]{:S(2)}, u32[]{:S(2)}) collective-permute-start(bf16[192,768]{1,0:T(8,128)(2,1)} %refs_0_.1), channel_id=1, source_target_pairs={{0,4},{4,0},{8,12},{12,8},{16,20},{20,16},{24,28},{28,24},{1,5},{5... | collective-permute-start | bytes 884744 | tf_op jit(solution)/shard_map/ppermute | solution.py:347
  10.6 30.9 %collective-permute-start = (bf16[120,3072]{1,0:T(8,128)(2,1)}, bf16[120,3072]{1,0:T(8,128)(2,1)S(1)}, u32[]{:S(2)}, u32[]{:S(2)}) collective-permute-start(bf16[120,3072]{1,0:T(8,128)(2,1)} %pad_maximum_fusion), channel_id=1, source_target_pairs={{0,1},{1,2},{2,3},{4,5},{5,6},{6,7},{8,9},{9,10},{10,11},{12,13},{... | collective-permute-start | bytes 2211848 | tf_op jit(solution)/shard_map/ppermute | solution.py:415
  13.8 21.8 %collective-permute-start.6 = (bf16[192,768]{1,0:T(8,128)(2,1)S(1)}, bf16[192,768]{1,0:T(8,128)(2,1)S(1)}, u32[]{:S(2)}, u32[]{:S(2)}) collective-permute-start(bf16[192,768]{1,0:T(8,128)(2,1)S(1)} %collective-permute-done.2.refs_1_), channel_id=1, source_target_pairs={{0,4},{4,0},{8,12},{12,8},{16,20},{20,16},{24,28},{28,24},{1,5},{5... | collective-permute-start | bytes 884744 | tf_op jit(solution)/shard_map/ppermute | solution.py:347
  18.7 16.9 %collective-permute-start.7 = (bf16[192,768]{1,0:T(8,128)(2,1)S(1)}, bf16[192,768]{1,0:T(8,128)(2,1)S(1)}, u32[]{:S(2)}, u32[]{:S(2)}) collective-permute-start(bf16[192,768]{1,0:T(8,128)(2,1)S(1)} %collective-permute-done.3.refs_2_), channel_id=1, source_target_pairs={{0,4},{4,0},{8,12},{12,8},{16,20},{20,16},{24,28},{28,24},{1,5},{5... | collective-permute-start | bytes 884744 | tf_op jit(solution)/shard_map/ppermute | solution.py:347
  41.4 68.9 %collective-permute-start.9 = (bf16[1536,768]{1,0:T(8,128)(2,1)S(1)}, bf16[1536,768]{1,0:T(8,128)(2,1)}, u32[]{:S(2)}, u32[]{:S(2)}) collective-permute-start(bf16[1536,768]{1,0:T(8,128)(2,1)S(1)} %assemble_weight.1.w_own), channel_id=1, source_target_pairs={{0,1},{1,0},{2,3},{3,2},{4,5},{5,4},{6,7},{7,6},{8,9},{9,8},{10,11... | collective-permute-start | bytes 7077896 | tf_op jit(solution)/shard_map/ppermute | solution.py:423
  55.2 21.4 %collective-permute-start.10 = (bf16[240,1536]{1,0:T(8,128)(2,1)S(1)}, bf16[240,1536]{1,0:T(8,128)(2,1)}, u32[]{:S(2)}, u32[]{:S(2)}) collective-permute-start(bf16[240,1536]{1,0:T(8,128)(2,1)S(1)} %get-tuple-element.27.a_ref.a0), channel_id=1, source_target_pairs={{0,2},{1,3},{2,0},{3,1},{4,6},{5,7},{6,4},{7,5},{8,10},{9,11},{10,... | collective-permute-start | bytes 2211848 | tf_op jit(solution)/shard_map/ppermute | solution.py:419
  60.8 31.5 %collective-permute-start.12 = (bf16[240,1536]{1,0:T(8,128)(2,1)}, bf16[240,1536]{1,0:T(8,128)(2,1)}, u32[]{:S(2)}, u32[]{:S(2)}) collective-permute-start(bf16[240,1536]{1,0:T(8,128)(2,1)} %dynamic-slice_bitcast_fusion), channel_id=1, source_target_pairs={{0,2},{1,3},{2,0},{3,1},{4,6},{5,7},{6,4},{7,5},{8,10},{9,11},{10,... | collective-permute-start | bytes 2211848 | tf_op jit(solution)/shard_map/ppermute | solution.py:419
  60.8 34.6 %collective-permute-start.18 = (bf16[240,1536]{1,0:T(8,128)(2,1)S(1)}, bf16[240,1536]{1,0:T(8,128)(2,1)}, u32[]{:S(2)}, u32[]{:S(2)}) collective-permute-start(bf16[240,1536]{1,0:T(8,128)(2,1)S(1)} %get-tuple-element.27.a_ref.a0), channel_id=1, source_target_pairs={{0,1},{1,0},{2,3},{3,2},{4,5},{5,4},{6,7},{7,6},{8,9},{9,8},{10,11... | collective-permute-start | bytes 2211848 | tf_op jit(solution)/shard_map/ppermute | solution.py:423
  76.6 18.8 %collective-permute-start.19 = (bf16[240,1536]{1,0:T(8,128)(2,1)}, bf16[240,1536]{1,0:T(8,128)(2,1)}, u32[]{:S(2)}, u32[]{:S(2)}) collective-permute-start(bf16[240,1536]{1,0:T(8,128)(2,1)} %collective-permute-done.10.a_ref.a2), channel_id=1, source_target_pairs={{0,1},{1,0},{2,3},{3,2},{4,5},{5,4},{6,7},{7,6},{8,9},{9,8},{10,11... | collective-permute-start | bytes 2211848 | tf_op jit(solution)/shard_map/ppermute | solution.py:423
  98.1 18.7 %collective-permute-start.27 = (bf16[192,768]{1,0:T(8,128)(2,1)S(1)}, bf16[192,768]{1,0:T(8,128)(2,1)S(1)}, u32[]{:S(2)}, u32[]{:S(2)}) collective-permute-start(bf16[192,768]{1,0:T(8,128)(2,1)S(1)} %get-tuple-element.48), channel_id=1, source_target_pairs={{0,4},{4,0},{8,12},{12,8},{16,20},{20,16},{24,28},{28,24},{1,5},{5... | collective-permute-start | bytes 884744 | tf_op jit(solution)/shard_map/ppermute | solution.py:347
  101.3 17.8 %collective-permute-start.25 = (bf16[192,768]{1,0:T(8,128)(2,1)S(1)}, bf16[192,768]{1,0:T(8,128)(2,1)S(1)}, u32[]{:S(2)}, u32[]{:S(2)}) collective-permute-start(bf16[192,768]{1,0:T(8,128)(2,1)S(1)} %get-tuple-element.46), channel_id=1, source_target_pairs={{0,4},{4,0},{8,12},{12,8},{16,20},{20,16},{24,28},{28,24},{1,5},{5... | collective-permute-start | bytes 884744 | tf_op jit(solution)/shard_map/ppermute | solution.py:347
  105.5 18.1 %collective-permute-start.23 = (bf16[192,768]{1,0:T(8,128)(2,1)S(1)}, bf16[192,768]{1,0:T(8,128)(2,1)S(1)}, u32[]{:S(2)}, u32[]{:S(2)}) collective-permute-start(bf16[192,768]{1,0:T(8,128)(2,1)S(1)} %get-tuple-element.44), channel_id=1, source_target_pairs={{0,4},{4,0},{8,12},{12,8},{16,20},{20,16},{24,28},{28,24},{1,5},{5... | collective-permute-start | bytes 884744 | tf_op jit(solution)/shard_map/ppermute | solution.py:347
  108.7 36.7 %collective-permute-start.22 = (bf16[192,768]{1,0:T(8,128)(2,1)S(1)}, bf16[192,768]{1,0:T(8,128)(2,1)S(1)}, u32[]{:S(2)}, u32[]{:S(2)}) collective-permute-start(bf16[192,768]{1,0:T(8,128)(2,1)S(1)} %get-tuple-element.42), channel_id=1, source_target_pairs={{0,4},{4,0},{8,12},{12,8},{16,20},{20,16},{24,28},{28,24},{1,5},{5... | collective-permute-start | bytes 884744 | tf_op jit(solution)/shard_map/ppermute | solution.py:347
  114.6 19.6 %collective-permute-start.13 = (bf16[240,1536]{1,0:T(8,128)(2,1)S(1)}, bf16[240,1536]{1,0:T(8,128)(2,1)S(1)}, u32[]{:S(2)}, u32[]{:S(2)}) collective-permute-start(bf16[240,1536]{1,0:T(8,128)(2,1)S(1)} %grad_attention_part.3), channel_id=1, source_target_pairs={{0,2},{1,3},{2,0},{3,1},{4,6},{5,7},{6,4},{7,5},{8,10},{9,11},{10,... | collective-permute-start | bytes 2211848 | tf_op jit(solution)/shard_map/ppermute | solution.py:419
  117.5 29.3 %collective-permute-start.28 = (bf16[192,768]{1,0:T(8,128)(2,1)}, bf16[192,768]{1,0:T(8,128)(2,1)S(1)}, u32[]{:S(2)}, u32[]{:S(2)}) collective-permute-start(bf16[192,768]{1,0:T(8,128)(2,1)} %add_convert_fusion), channel_id=1, source_target_pairs={{0,24},{4,28},{8,0},{12,4},{16,8},{20,12},{24,16},{28,20},{1,25},{... | collective-permute-start | bytes 884744 | tf_op jit(solution)/shard_map/ppermute | solution.py:347
  119.9 31.5 %collective-permute-start.26 = (bf16[192,768]{1,0:T(8,128)(2,1)}, bf16[192,768]{1,0:T(8,128)(2,1)S(1)}, u32[]{:S(2)}, u32[]{:S(2)}) collective-permute-start(bf16[192,768]{1,0:T(8,128)(2,1)} %add_convert_fusion.1), channel_id=1, source_target_pairs={{0,8},{4,12},{8,16},{12,20},{16,24},{20,28},{24,0},{28,4},{1,9},{5... | collective-permute-start | bytes 884744 | tf_op jit(solution)/shard_map/ppermute | solution.py:347
  123.7 34.5 %collective-permute-start.11 = (bf16[240,1536]{1,0:T(8,128)(2,1)S(1)}, bf16[240,1536]{1,0:T(8,128)(2,1)S(1)}, u32[]{:S(2)}, u32[]{:S(2)}) collective-permute-start(bf16[240,1536]{1,0:T(8,128)(2,1)S(1)} %project_half.3), channel_id=1, source_target_pairs={{0,2},{1,3},{2,0},{3,1},{4,6},{5,7},{6,4},{7,5},{8,10},{9,11},{10,... | collective-permute-start | bytes 2211848 | tf_op jit(solution)/shard_map/ppermute | solution.py:419
  134.2 18.5 %collective-permute-start.24 = (bf16[192,768]{1,0:T(8,128)(2,1)S(1)}, bf16[192,768]{1,0:T(8,128)(2,1)S(1)}, u32[]{:S(2)}, u32[]{:S(2)}) collective-permute-start(bf16[192,768]{1,0:T(8,128)(2,1)S(1)} %add_convert_fusion.2), channel_id=1, source_target_pairs={{0,16},{4,20},{8,24},{12,28},{16,0},{20,4},{24,8},{28,12},{1,17},{... | collective-permute-start | bytes 884744 | tf_op jit(solution)/shard_map/ppermute | solution.py:347
  145.5 21.7 %collective-permute-start.14 = (bf16[120,1536]{1,0:T(8,128)(2,1)S(1)}, bf16[120,1536]{1,0:T(8,128)(2,1)S(1)}, u32[]{:S(2)}, u32[]{:S(2)}) collective-permute-start(bf16[120,1536]{1,0:T(8,128)(2,1)S(1)} %get-tuple-element.35), channel_id=1, source_target_pairs={{0,1},{1,2},{2,3},{4,5},{5,6},{6,7},{8,9},{9,10},{10,11},{12,13},{... | collective-permute-start | bytes 1105928 | tf_op jit(solution)/shard_map/ppermute | solution.py:415
  146.8 20.4 %collective-permute-start.15 = (bf16[120,1536]{1,0:T(8,128)(2,1)S(1)}, bf16[120,1536]{1,0:T(8,128)(2,1)S(1)}, u32[]{:S(2)}, u32[]{:S(2)}) collective-permute-start(bf16[120,1536]{1,0:T(8,128)(2,1)S(1)} %get-tuple-element.36), channel_id=1, source_target_pairs={{0,1},{1,2},{2,3},{4,5},{5,6},{6,7},{8,9},{9,10},{10,11},{12,13},{... | collective-permute-start | bytes 1105928 | tf_op jit(solution)/shard_map/ppermute | solution.py:415
  151.4 15.8 %collective-permute-start.16 = (bf16[120,1536]{1,0:T(8,128)(2,1)S(1)}, bf16[120,1536]{1,0:T(8,128)(2,1)S(1)}, u32[]{:S(2)}, u32[]{:S(2)}) collective-permute-start(bf16[120,1536]{1,0:T(8,128)(2,1)S(1)} %get-tuple-element.37), channel_id=1, source_target_pairs={{1,0},{2,1},{3,2},{5,4},{6,5},{7,6},{9,8},{10,9},{11,10},{13,12},{... | collective-permute-start | bytes 1105928 | tf_op jit(solution)/shard_map/ppermute | solution.py:415
  152.7 14.5 %collective-permute-start.17 = (bf16[120,1536]{1,0:T(8,128)(2,1)S(1)}, bf16[120,1536]{1,0:T(8,128)(2,1)S(1)}, u32[]{:S(2)}, u32[]{:S(2)}) collective-permute-start(bf16[120,1536]{1,0:T(8,128)(2,1)S(1)} %get-tuple-element.38), channel_id=1, source_target_pairs={{1,0},{2,1},{3,2},{5,4},{6,5},{7,6},{9,8},{10,9},{11,10},{13,12},{... | collective-permute-start | bytes 1105928 | tf_op jit(solution)/shard_map/ppermute | solution.py:415
  (21 other events, 148.0 us)

commit v2 on v0

v2 whole, which is shorter than its diff:
```python
import functools

import jax
import jax.numpy as jnp
from jax import lax
from jax.experimental import pallas as pl
from jax.experimental.pallas import tpu as pltpu
from jax.sharding import PartitionSpec as P

HEADS = 12
HEAD = 128
TILE = 120
GROUP = 3
NEAR = (0, 1, 3)
FAR = 2
SCALE = HEAD**-0.5
VMEM = 32 * 1024 * 1024
FIRST = 60 * 1024 * 1024
BF16 = jnp.bfloat16
F32 = jnp.float32


def dot_nn(a, b):
    return lax.dot_general(a, b, (((1,), (0,)), ((), ())), preferred_element_type=F32)


def dot_nt(a, b):
    return lax.dot_general(a, b, (((1,), (1,)), ((), ())), preferred_element_type=F32)


def dot_tn(a, b):
    return lax.dot_general(a, b, (((0,), (0,)), ((), ())), preferred_element_type=F32)


WEIGHT = {}


def cost(name):
    return pl.CostEstimate(
        flops=int(WEIGHT.get(name, 3e10)), bytes_accessed=int(1e10), transcendentals=0
    )


def whole():
    return pl.BlockSpec(memory_space=pltpu.VMEM)


def anywhere():
    return pl.BlockSpec(memory_space=pl.ANY)


def shape(dims, dtype=BF16):
    return jax.ShapeDtypeStruct(dims, dtype)


def run(kernel, args, in_specs, out_specs, out_shape, name, after=(), grid=(), limit=VMEM, **extra):
    count, skipped = len(args), len(after)

    def body(*refs):
        kernel(*refs[:count], *refs[count + skipped :])

    return pl.pallas_call(
        body,
        grid=grid,
        in_specs=list(in_specs) + [anywhere()] * skipped,
        out_specs=out_specs,
        out_shape=out_shape,
        compiler_params=pltpu.CompilerParams(vmem_limit_bytes=limit),
        cost_estimate=cost(name),
        name=name,
        **extra,
    )(*args, *after)


def relay(block, after):
    def body(*refs):
        pass

    return pl.pallas_call(
        body,
        in_specs=[anywhere()] * (1 + len(after)),
        out_specs=anywhere(),
        out_shape=shape(block.shape, block.dtype),
        input_output_aliases={0: 0},
        cost_estimate=cost("relay"),
        name="relay",
    )(block, *after)


def facing_rows(rows, cols):
    y, core = place()
    top = lax.broadcasted_iota(jnp.int32, (rows, cols), 0) < TILE
    return top == (core == 0)


def place():
    tile = lax.axis_index("tile")
    return lax.div(tile, 2), lax.rem(tile, 2)


def columns(start, width):
    return pl.ds(pl.multiple_of(start, 128), width)


def rows_at(start, count):
    return pl.ds(pl.multiple_of(start, 16), count)


def forward_kernel(q_ref, k_ref, v_ref, kl_ref, vl_ref, kr_ref, vr_ref, a_ref, p_ref, ph_ref):
    rows = q_ref.shape[0]
    y, core = place()
    facing = facing_rows(rows, TILE)
    seen = jnp.logical_not(facing) | (y != core)
    for h in range(GROUP):
        at = pl.ds(h * HEAD, HEAD)
        q = q_ref[:, at]
        s = dot_nt(q, k_ref[:, at]) * SCALE
        sh = jnp.where(facing, dot_nt(q, kl_ref[:, at]), dot_nt(q, kr_ref[:, at])) * SCALE
        sh = jnp.where(seen, sh, -1e30)
        top_score = jnp.maximum(
            jnp.max(s, axis=-1, keepdims=True), jnp.max(sh, axis=-1, keepdims=True)
        )
        e = jnp.exp(s - top_score)
        eh = jnp.exp(sh - top_score)
        total = jnp.sum(e, axis=-1, keepdims=True) + jnp.sum(eh, axis=-1, keepdims=True)
        inverse = 1.0 / total
        p = (e * inverse).astype(BF16)
        ph = eh * inverse
        p_ref[h] = p
        ph_ref[h] = ph.astype(BF16)
        out = dot_nn(p, v_ref[:, at])
        out += dot_nn(jnp.where(facing, ph, 0.0).astype(BF16), vl_ref[:, at])
        out += dot_nn(jnp.where(facing, 0.0, ph).astype(BF16), vr_ref[:, at])
        a_ref[:, at] = out.astype(BF16)


def attention_specs(rows, feats):
    width = GROUP * HEAD
    groups = feats // width
    col = pl.BlockSpec((rows, width), lambda g: (0, g))
    halo_keys = pl.BlockSpec((TILE, width), lambda g: (0, g))
    halo_values = pl.BlockSpec((TILE, width), lambda g: (0, groups + g))
    own = pl.BlockSpec((GROUP, rows, rows), lambda g: (g, 0, 0))
    halo = pl.BlockSpec((GROUP, rows, TILE), lambda g: (g, 0, 0))
    return groups, col, halo_keys, halo_values, own, halo


def attention_forward(q, k, v, halo_chip, halo_core, after):
    rows, feats = q.shape
    groups, col, hk, hv, own, halo = attention_specs(rows, feats)
    return run(
        forward_kernel,
        (q, k, v, halo_chip, halo_chip, halo_core, halo_core),
        [col, col, col, hk, hv, hk, hv],
        [col, own, halo],
        [shape((rows, feats)), shape((HEADS, rows, rows)), shape((HEADS, rows, TILE))],
        "attention_forward",
        after,
        (groups,),
    )


def halo_backward_kernel(
    ga_ref, a_ref, q_ref, vl_ref, vr_ref, ph_ref, ds_ref, chip_ref, core_ref
):
    rows = q_ref.shape[0]
    feats = chip_ref.shape[1] // 2
    facing = facing_rows(rows, TILE)
    first = pl.program_id(0) * (GROUP * HEAD)
    for h in range(GROUP):
        at = pl.ds(h * HEAD, HEAD)
        to_key = columns(first + h * HEAD, HEAD)
        to_value = columns(first + feats + h * HEAD, HEAD)
        q = q_ref[:, at]
        ga = ga_ref[:, at]
        dots = jnp.sum(ga.astype(F32) * a_ref[:, at].astype(F32), axis=-1, keepdims=True)
        dp = jnp.where(facing, dot_nt(ga, vl_ref[:, at]), dot_nt(ga, vr_ref[:, at]))
        ph = ph_ref[h].astype(F32)
        ds = ph * (dp - dots)
        ds_ref[h] = ds.astype(BF16)
        chip_ref[:, to_key] = (dot_tn(jnp.where(facing, ds, 0.0).astype(BF16), q) * SCALE).astype(BF16)
        core_ref[:, to_key] = (dot_tn(jnp.where(facing, 0.0, ds).astype(BF16), q) * SCALE).astype(BF16)
        chip_ref[:, to_value] = dot_tn(jnp.where(facing, ph, 0.0).astype(BF16), ga).astype(BF16)
        core_ref[:, to_value] = dot_tn(jnp.where(facing, 0.0, ph).astype(BF16), ga).astype(BF16)


def halo_backward(ga, att, q, halo_chip, halo_core, probs_halo):
    rows, feats = q.shape
    groups, col, hk, hv, own, halo = attention_specs(rows, feats)
    rim = pl.BlockSpec((TILE, 2 * feats), lambda g: (0, 0))
    return run(
        halo_backward_kernel,
        (ga, att, q, halo_chip, halo_core, probs_halo),
        [col, col, col, hv, hv, halo],
        [halo, rim, rim],
        [shape((HEADS, rows, TILE))] + [shape((TILE, 2 * feats))] * 2,
        "halo_backward",
        (),
        (groups,),
    )


def main_backward_kernel(
    ga_ref, a_ref, q_ref, k_ref, v_ref, kl_ref, kr_ref, p_ref, dsh_ref, dq_ref, dk_ref, dv_ref
):
    rows = q_ref.shape[0]
    facing = facing_rows(rows, TILE)
    for h in range(GROUP):
        at = pl.ds(h * HEAD, HEAD)
        q = q_ref[:, at]
        ga = ga_ref[:, at]
        dots = jnp.sum(ga.astype(F32) * a_ref[:, at].astype(F32), axis=-1, keepdims=True)
        p = p_ref[h]
        ds = (p.astype(F32) * (dot_nt(ga, v_ref[:, at]) - dots)).astype(BF16)
        dsh = dsh_ref[h].astype(F32)
        dq = dot_nn(ds, k_ref[:, at])
        dq += dot_nn(jnp.where(facing, dsh, 0.0).astype(BF16), kl_ref[:, at])
        dq += dot_nn(jnp.where(facing, 0.0, dsh).astype(BF16), kr_ref[:, at])
        dq_ref[:, at] = (dq * SCALE).astype(BF16)
        dk_ref[:, at] = dot_tn(ds, q) * SCALE
        dv_ref[:, at] = dot_tn(p, ga)


def main_backward(ga, att, q, k, v, halo_chip, halo_core, probs, ds_halo, after):
    rows, feats = q.shape
    groups, col, hk, hv, own, halo = attention_specs(rows, feats)
    return run(
        main_backward_kernel,
        (ga, att, q, k, v, halo_chip, halo_core, probs, ds_halo),
        [col, col, col, col, col, hk, hk, own, halo],
        [col, col, col],
        [shape((rows, feats)), shape((rows, feats), F32), shape((rows, feats), F32)],
        "main_backward",
        after,
        (groups,),
    )


def add_rims_kernel(own_k, own_v, lk, lv, rk, rv, out_k, out_v):
    y, core = place()
    for own, chip, other, out in ((own_k, lk, rk, out_k), (own_v, lv, rv, out_v)):
        far, near = chip[...].astype(F32), other[...].astype(F32)
        low, high = jnp.where(core == 0, far, near), jnp.where(core == 0, near, far)
        extra = jnp.concatenate([low, high], axis=0)
        out[...] = (own[...] + extra).astype(BF16)


def add_rims(dk, dv, from_chip, from_core):
    rows, feats = dk.shape
    groups, col, hk, hv, own, halo = attention_specs(rows, feats)
    return run(
        add_rims_kernel,
        (dk, dv, from_chip, from_chip, from_core, from_core),
        [col, col, hk, hv, hk, hv],
        [col, col],
        [shape((rows, feats))] * 2,
        "add_rims",
        (),
        (groups,),
    )


def first_sends_kernel(k_ref, v_ref, w_ref, c_ref, chip_ref, core_ref, shard_ref, half_ref, held, sems):
    y, core = place()
    rows, feats = k_ref.shape
    parts = 4
    part = feats // parts
    copies = []
    for i, source in enumerate((k_ref, v_ref)):
        for j in range(parts):
            at = pl.ds(j * part, part)
            copies.append((source.at[:, at], held.at[i, :, at]))
    copies.append((w_ref, shard_ref))
    for j in range(parts):
        at = columns((1 - y) * feats + j * part, part)
        copies.append((c_ref.at[:, at], half_ref.at[:, pl.ds(j * part, part)]))
    copies = [pltpu.make_async_copy(*ends, sems.at[i]) for i, ends in enumerate(copies)]
    for copy in copies:
        copy.start()
    for copy in copies:
        copy.wait()
    for i in range(2):
        at = pl.ds(i * feats, feats)
        low, high = held[i, :TILE], held[i, rows - TILE :]
        chip_ref[:, at] = jnp.where(core == 0, low, high)
        core_ref[:, at] = jnp.where(core == 0, high, low)


def first_sends(k, v, w, cot):
    rows, feats = k.shape
    return run(
        first_sends_kernel,
        (k, v, w, cot),
        [pl.BlockSpec(memory_space=pltpu.HBM)] * 4,
        [whole()] * 4,
        [shape((TILE, 2 * feats))] * 2 + [shape(w.shape), shape((rows, cot.shape[1] // 2))],
        "first_sends",
        limit=FIRST,
        scratch_shapes=[pltpu.VMEM((2, rows, feats), BF16), pltpu.SemaphoreType.DMA((13,))],
    )


def quarters_for_core_kernel(cot_ref, partner_ref, out_ref):
    y, core = place()
    rows, width = out_ref.shape[0] // 2, out_ref.shape[1]
    out_ref[:rows] = cot_ref[:, columns((2 * y + 1 - core) * width, width)]
    out_ref[rows:] = partner_ref[:, columns((1 - core) * width, width)]


def quarters_for_core(cot, cot_partner, after):
    rows, model = cot.shape
    return run(
        quarters_for_core_kernel,
        (cot, cot_partner),
        [whole()] * 2,
        whole(),
        shape((2 * rows, model // 4)),
        "quarters_for_core",
        after,
    )


def block_at(shift):
    if not is_grid():
        return shift
    return lax.rem(lax.div(lax.axis_index("dp"), 2) + 4 - shift, 4)


def lay(pair, block):
    x = lax.rem(lax.axis_index("dp"), 2) if is_grid() else 0
    rows = pair[0].shape[0]
    block[rows_at(x * rows, rows), :] = pair[0][...]
    block[rows_at((1 - x) * rows, rows), :] = pair[1][...]


def half_product(c_ref, w_own, w_other, out_ref, sliced):
    y, core = place()
    half = y if sliced else 0
    width = w_own.shape[1]
    total = dot_nt(c_ref[:, columns((2 * half + core) * width, width)], w_own[...])
    total += dot_nt(c_ref[:, columns((2 * half + 1 - core) * width, width)], w_other[...])
    out_ref[...] = total.astype(out_ref.dtype)


def near_kernel(c_ref, w_own, w_other, out_ref, *, sliced):
    half_product(c_ref, w_own, w_other, out_ref, sliced)


def far_kernel(c_ref, own0, own1, other0, other1, out_ref, w_own, w_other, *, sliced):
    lay((own0, own1), w_own)
    lay((other0, other1), w_other)
    half_product(c_ref, w_own, w_other, out_ref, sliced)


def grad_attention_near(cot, near, dtype, sliced, after):
    rows = cot.shape[0]
    return run(
        functools.partial(near_kernel, sliced=sliced),
        (cot, *near),
        [whole()] * 3,
        whole(),
        shape((rows, near[0].shape[0]), dtype),
        "grad_attention_near",
        after,
    )


def grad_attention_far(cot, far, dtype, sliced, after):
    rows = cot.shape[0]
    feats, width = 2 * far[0].shape[0], far[0].shape[1]
    return run(
        functools.partial(far_kernel, sliced=sliced),
        (cot, *far),
        [whole()] * 5,
        whole(),
        shape((rows, feats), dtype),
        "grad_attention_far",
        after,
        scratch_shapes=[pltpu.VMEM((feats, width), BF16)] * 2,
    )


def merge_kernel(own_near, own_far, recv_near, recv_far, out_ref):
    rows, width = own_far.shape
    for i, shift in enumerate((*NEAR, FAR)):
        own, recv = (own_near, recv_near) if i < 3 else (own_far, recv_far)
        at = pl.ds(i * width if i < 3 else 0, width)
        total = own[:, at] + recv[:, at].astype(F32)
        out_ref[:, columns(block_at(shift) * width, width)] = total.astype(BF16)


def merge(own_near, own_far, recv_near, recv_far, after):
    rows, width = own_far.shape
    return run(
        merge_kernel,
        (own_near, own_far, recv_near, recv_far),
        [whole()] * 4,
        whole(),
        shape((rows, 4 * width)),
        "merge",
        after,
    )


def project_kernel(
    a_ref, near_own, near_other, own0, own1, other0, other1, out_ref, far_own, far_other
):
    y, core = place()
    rows, width = far_own.shape
    lay((own0, own1), far_own)
    lay((other0, other1), far_other)
    for quarter, near, far in ((core, near_own, far_own), (1 - core, near_other, far_other)):
        total = dot_nn(a_ref[:, columns(block_at(FAR) * rows, rows)], far[...])
        for i, shift in enumerate(NEAR):
            a = a_ref[:, columns(block_at(shift) * rows, rows)]
            total += dot_nn(a, near[i * rows : (i + 1) * rows])
        out_ref[:, columns(quarter * width, width)] = total.astype(BF16)


def project_half(att, near, far, after):
    rows = att.shape[0]
    feats, width = 2 * far[0].shape[0], far[0].shape[1]
    return run(
        project_kernel,
        (att, *near, *far),
        [whole()] * 7,
        whole(),
        shape((rows, 2 * width)),
        "project_half",
        after,
        scratch_shapes=[pltpu.VMEM((feats, width), BF16)] * 2,
    )


def join_halves_kernel(mine, theirs, out_ref):
    y, core = place()
    width = mine.shape[1]
    out_ref[:, columns(y * width, width)] = mine[...]
    out_ref[:, columns((1 - y) * width, width)] = theirs[...]


def join_halves(mine, theirs):
    rows, width = mine.shape
    return run(
        join_halves_kernel,
        (mine, theirs),
        [whole()] * 2,
        whole(),
        shape((rows, 2 * width)),
        "join_halves",
    )


def assemble_kernel(*refs):
    *pieces, out, sems = refs
    x = lax.rem(lax.axis_index("dp"), 2)
    rows = pieces[0].shape[0]
    copies = []
    for i, piece in enumerate(pieces):
        block = 2 * (i // 2) + (x if i % 2 == 0 else 1 - x)
        copies.append(pltpu.make_async_copy(piece, out.at[rows_at(block * rows, rows)], sems.at[i]))
    for copy in copies:
        copy.start()
    for copy in copies:
        copy.wait()


def assemble(pieces, after):
    rows, width = pieces[0].shape
    n = len(pieces)
    return run(
        assemble_kernel,
        pieces,
        [anywhere()] * n,
        whole(),
        shape((n * rows, width)),
        "assemble_weight",
        after,
        scratch_shapes=[pltpu.SemaphoreType.DMA((n,))],
    )


def along_z(block, shift):
    return lax.ppermute(
        block, "dp", [(2 * z + x, 2 * ((z + shift) % 4) + x) for z in range(4) for x in range(2)]
    )


def across_x(block):
    return lax.ppermute(block, "dp", [(i, i ^ 1) for i in range(8)])


def is_grid():
    return lax.axis_size("dp") == 8


def weight_grad_kernel(
    a_own, a_par, a_sib, a_sibpar, c_own, c_par, c_sib, c_sibpar, *outs_and_total
):
    *outs, total = outs_and_total
    x = lax.rem(lax.axis_index("dp"), 2)
    step = pl.program_id(0)
    half = total.shape[0] // 2
    acc = dot_tn(a_own[...], c_own[...])
    acc += dot_tn(a_par[...], c_par[...])
    acc += dot_tn(a_sib[...], c_sib[...])
    acc += dot_tn(a_sibpar[...], c_sibpar[...])
    total[...] = acc
    keeps, sends = outs[:3], outs[3:]
    for at, (part, row) in enumerate(((0, 0), (1, 0), (1, half), (2, 0))):

        @pl.when(step == at)
        def _():
            keeps[part][row : row + half] = total[rows_at(x * half, half), :]
            sends[part][row : row + half] = total[rows_at((1 - x) * half, half), :].astype(BF16)


def weight_grad_parts(operands, after):
    a_own, a_par, a_sib, a_sibpar, cot, cot_par, c_sib = operands
    tokens, feats = a_own.shape
    width = cot.shape[1] // 4
    part = feats // 4

    def rows_of(g):
        shift = jnp.where(g == 0, 2, jnp.where(g == 1, 1, jnp.where(g == 2, 3, 0)))
        return lax.rem(lax.div(lax.axis_index("dp"), 2) + shift, 4)

    a_spec = pl.BlockSpec((tokens, part), lambda g: (0, rows_of(g)))
    c_specs = [
        pl.BlockSpec((tokens, width), lambda g: (0, lax.axis_index("tile"))),
        pl.BlockSpec((tokens, width), lambda g: (0, lax.rem(lax.axis_index("tile"), 2))),
        pl.BlockSpec((tokens, width), lambda g: (0, 0)),
        pl.BlockSpec((tokens, width), lambda g: (1, 0)),
    ]
    dims = [(part // 2, width), (part, width), (part // 2, width)]
    return run(
        weight_grad_kernel,
        (a_own, a_par, a_sib, a_sibpar, cot, cot_par, c_sib, c_sib),
        [a_spec] * 4 + c_specs,
        [pl.BlockSpec(d, lambda g: (0, 0)) for d in dims * 2],
        [shape(d, F32) for d in dims] + [shape(d) for d in dims],
        "weight_grad_parts",
        after,
        (4,),
        scratch_shapes=[pltpu.VMEM((part, width), F32)],
    )


def weight_grad_sum(operands, after):
    if not is_grid():
        a_own, a_par, a_sib, a_sibpar, cot, cot_par, c_sib = operands
        y, core = place()
        tokens, width = c_sib.shape[0] // 2, c_sib.shape[1]
        c_own = lax.dynamic_slice_in_dim(cot, (2 * y + core) * width, width, axis=1)
        c_par = lax.dynamic_slice_in_dim(cot_par, core * width, width, axis=1)
        total = dot_tn(a_own, c_own) + dot_tn(a_par, c_par)
        total += dot_tn(a_sib, c_sib[:tokens]) + dot_tn(a_sibpar, c_sib[tokens:])
        return lax.psum_scatter(total, "dp", scatter_dimension=0, tiled=True)
    parts = weight_grad_parts(operands, after)
    return [(keep, across_x(send)) for keep, send in zip(parts[:3], parts[3:])]


def add_kernel(*refs):
    *terms, out = refs
    total = terms[0][...].astype(F32)
    for term in terms[1:]:
        total += term[...].astype(F32)
    out[...] = total.astype(out.dtype)


def add(terms, dtype, after=()):
    return run(
        add_kernel,
        terms,
        [whole()] * len(terms),
        whole(),
        shape(terms[0].shape, dtype),
        "add",
        after,
    )


def split_add_kernel(keep, recv, one, three):
    half = one.shape[0]
    one[...] = keep[:half] + recv[:half].astype(F32)
    three[...] = (keep[half:] + recv[half:].astype(F32)).astype(BF16)


def split_add(keep, recv, after=()):
    dims = (keep.shape[0] // 2, keep.shape[1])
    return run(
        split_add_kernel,
        (keep, recv),
        [whole()] * 2,
        [whole()] * 2,
        [shape(dims, F32), shape(dims)],
        "split_add",
        after,
    )


def between_chips(block):
    return lax.ppermute(block, "tile", [(1, 2), (2, 1)])


def to_partner(block):
    return lax.ppermute(block, "tile", [(0, 2), (1, 3), (2, 0), (3, 1)])


def to_core(block):
    return lax.ppermute(block, "tile", [(0, 1), (1, 0), (2, 3), (3, 2)])


def shards(queries, key_vectors, value_vectors, out_weight, cotangent):
    q, k, v, cot = queries[0], key_vectors[0], value_vectors[0], cotangent[0]
    tokens = q.shape[0]
    y, core = place()

    rim_chip, rim_core, shard, cot_send = first_sends(k, v, out_weight, cot)
    halo_chip, halo_core = between_chips(rim_chip), to_core(rim_core)
    if is_grid():
        z1, z3 = along_z(shard, 1), along_z(shard, 3)
        x0 = across_x(shard)
    cot_partner = to_partner(cot_send)
    att, probs, probs_halo = attention_forward(q, k, v, halo_chip, halo_core, ())
    att_partner = to_partner(att)
    att_core = to_core(att)
    if is_grid():
        z1 = relay(z1, (att,))
        z3 = relay(z3, (z1,))
        z2 = relay(along_z(z1, 1), (z3,))
        near_own = assemble(
            (shard, x0, z1, across_x(z1), z3, across_x(z3)), (att, cot_partner)
        )
        far_own = (z2, across_x(z2))
    else:
        w_own = lax.all_gather(out_weight, "dp", axis=0, tiled=True)
        cut = w_own.shape[0] * 3 // 4
        near_own = w_own[:cut]
        far_own = (w_own[cut : cut + cut // 6], w_own[cut + cut // 6 :])
    near = (near_own, to_core(near_own))
    far = (*far_own, to_core(far_own[0]), to_core(far_own[1]))
    cot_send_core = quarters_for_core(cot, cot_partner, ())
    cot_core = to_core(cot_send_core)

    send_near = grad_attention_near(cot_partner, near, BF16, False, (cot_send_core,))
    recv_near = to_partner(send_near)
    send_far = grad_attention_far(cot_partner, far, BF16, False, (send_near,))
    recv_far = to_partner(send_far)

    att_partner = relay(att_partner, (send_far,))
    att_core_partner = to_core(att_partner)
    mine_near = grad_attention_near(cot, near, F32, True, (send_far,))
    parts = weight_grad_sum(
        (att, att_partner, att_core, att_core_partner, cot, cot_partner, cot_core), (mine_near,)
    )
    grid = is_grid()
    mine_far = grad_attention_far(
        cot, far, F32, True, (mine_near, parts[2][0]) if grid else (mine_near,)
    )
    if grid:
        far_sum = add(parts[0], BF16, (mine_far,))
        from_two = along_z(far_sum, 1)
    proj_partner = project_half(att_partner, near, far, (far_sum,) if grid else (mine_far,))
    proj_recv = to_partner(proj_partner)

    ga = merge(mine_near, mine_far, recv_near, recv_far, (far_sum,) if grid else ())
    ds_halo, back_chip, back_core = halo_backward(ga, att, q, halo_chip, halo_core, probs_halo)
    from_chip, from_core = between_chips(back_chip), to_core(back_core)
    if grid:
        one, three = split_add(*parts[1], (ds_halo,))
        from_three = along_z(three, 3)
        one_sum = add((one, from_two), BF16, (three,))
        from_one = along_z(one_sum, 1)
    proj_own = project_half(att, near, far, (one_sum,) if grid else (proj_partner,))
    dq, dk, dv = main_backward(
        ga, att, q, k, v, halo_chip, halo_core, probs, ds_halo, (proj_own,)
    )
    projected = join_halves(proj_own, proj_recv)
    dk, dv = add_rims(dk, dv, from_chip, from_core)
    weight_grad = add((*parts[2], from_three, from_one), F32) if grid else parts
    return projected[None], dq[None], dk[None], dv[None], weight_grad


def solution(mesh):
    tokens = P("dp", "tile", None)
    weight = P("dp", "tile")
    return jax.shard_map(
        shards,
        mesh=mesh,
        in_specs=(tokens, tokens, tokens, weight, tokens),
        out_specs=(tokens, tokens, tokens, tokens, weight),
        check_vma=False,
    )
```

time: 546 us -> 126 us (0.23)
  waiting for transfers between devices: 400 us -> 23.7 us
  Pallas kernels: 0 us -> 55.2 us
  matrix products: 46.2 us -> 0 us
  local copies, waits for them, and re-layouts: 52.5 us -> 9.5 us
  starting transfers between devices: 11.1 us -> 36.3 us
  other arithmetic: 21.2 us -> 0 us
  between operations: 14 us -> 0.98 us
    reduce_scatter x2 -> x0, waiting for transfers between devices: 303 us -> none  [the longest x1 303 us: shards(): lax.psum_scatter(contract_rows(attention, grad_rows), 'dp', scatter_dimen...]
    all_gather x2 -> x0, waiting for transfers between devices: 95.9 us -> none  [the longest x1 57 us: shards(): weight_rows = lax.all_gather(out_weight, 'dp', axis=0, tiled=True)]
    pallas_call x0 -> x24, Pallas kernels: none -> 55.2 us  [the longest x20 55.2 us: run(): pl.pallas_call(body, grid=grid, in_specs=list(in_specs) + [anywhere()] *...]
    dot_general x8 -> x0, matrix products: 39.8 us -> none  [the longest x1 7.84 us: contract_rows(): lax.dot_general(left, right, (((0,), (0,)), ((), ())), preferred_element_...]
    ppermute x4 -> x28, starting transfers between devices: 10.7 us -> 36.3 us  [the longest x5 12.6 us: to_partner(): return lax.ppermute(block, 'tile', [(0, 2), (1, 3), (2, 0), (3, 1)])]
    ppermute x4 -> x28, waiting for transfers between devices: 0.01 us -> 23.7 us  [the longest x7 13.8 us: across_x(): return lax.ppermute(block, 'dp', [(i, i ^ 1) for i in range(8)])]
    scatter-add x2 -> x0, local copies, waits for them, and re-layouts: 18.1 us -> none  [the longest x1 9.82 us: shards(): own_grads = own_grads.at[tokens - TILE:].add(from_right.astype(jnp.float32))]
    slice x6 -> x0, local copies, waits for them, and re-layouts: 10.7 us -> none  [the longest x2 3.88 us: shards(): right_rim = both_grads[-TILE:].astype(jnp.bfloat16)]
  transfers between devices with their start and end apart: 8 -> 28, of which waited for: 3 -> 6; matrix products, arithmetic and copies ran while one was open for 18% -> 0% of each run, Pallas kernels for 0% -> 38%
where the time goes in v2:
time: 126 us
  Pallas kernels  55.2 us (44%)
  starting transfers between devices  36.3 us (29%)
  waiting for transfers between devices  23.7 us (19%)
  local copies, waits for them, and re-layouts  9.5 us (8%)
    pallas_call x20, Pallas kernels, run(): pl.pallas_call(body, grid=grid, in_specs=list(in_specs) + [anywhere()] *...  55.2 us
    ppermute x7, waiting for transfers between devices, across_x(): return lax.ppermute(block, 'dp', [(i, i ^ 1) for i in range(8)])  13.8 us
    ppermute x5, starting transfers between devices, to_partner(): return lax.ppermute(block, 'tile', [(0, 2), (1, 3), (2, 0), (3, 1)])  12.6 us
    unnamed x74, local copies, waits for them, and re-layouts  9.5 us
    ppermute x6, waiting for transfers between devices, along_z(): lax.ppermute(block, 'dp', [(2 * z + x, 2 * ((z + shift) % 4) + x) for z i...  8.78 us
    ppermute x7, starting transfers between devices, across_x(): return lax.ppermute(block, 'dp', [(i, i ^ 1) for i in range(8)])  8.63 us
    ppermute x6, starting transfers between devices, along_z(): lax.ppermute(block, 'dp', [(2 * z + x, 2 * ((z + shift) % 4) + x) for z i...  7.55 us
    ppermute x8, starting transfers between devices, to_core(): return lax.ppermute(block, 'tile', [(0, 1), (1, 0), (2, 3), (3, 2)])  5.22 us
  transfers between devices with their start and end apart: 28, of which 6 were waited for; matrix products, arithmetic and copies ran while one was open for 0% of the time, Pallas kernels for 38%

profile of v2, /device:TPU:0, one launch (start us, length us, event | category | flops | bytes accessed | tf_op | source)
XLA Modules:
  0.0 125.6 jit_solution(4523523177661739366)
XLA Ops:
  0.7 3.5 %first_sends.1 = (bf16[120,3072]{1,0:T(8,128)(2,1)}, bf16[120,3072]{1,0:T(8,128)(2,1)}, bf16[192,768]{1,0:T(8,128)(2,1)}, bf16[240,1536]{1,0:T(8,128)(2,1)}) custom-call(bf16[240,1536]{1,0:T(8,128)(2,1)} %bitcast.16, bf16[240,1536]{1,0:T(8,128)(2,1)} %bitcast.19, bf16[192,768]{1,0:T(8,128)(2,1)} %refs_2_.1, bf16[240,3072]{1,0:T(8,128)(2,1)} %bitcast.8), custom_call_target="tpu_custom_call" | custom-call | flops 30000001024 | bytes 10000000000 | tf_op jit(solution)/shard_map/first_sends/pallas_call | solution.py:62
  4.8 4.3 %collective-permute-start.1 = (bf16[120,3072]{1,0:T(8,128)(2,1)}, bf16[120,3072]{1,0:T(8,128)(2,1)S(1)}, u32[]{:S(2)}, u32[]{:S(2)}) collective-permute-start(bf16[120,3072]{1,0:T(8,128)(2,1)} %get-tuple-element.29), channel_id=1, source_target_pairs={{0,1},{1,0},{2,3},{3,2},{4,5},{5,4},{6,7},{7,6},{8,9},{9,8},{10,11... | collective-permute-start | bytes 2211848 | tf_op jit(solution)/shard_map/ppermute | solution.py:611
  9.2 3.6 %collective-permute-start.5 = (bf16[192,768]{1,0:T(8,128)(2,1)}, bf16[192,768]{1,0:T(8,128)(2,1)S(1)}, u32[]{:S(2)}, u32[]{:S(2)}) collective-permute-start(bf16[192,768]{1,0:T(8,128)(2,1)} %get-tuple-element.31.refs_0_), channel_id=1, source_target_pairs={{0,24},{4,28},{8,0},{12,4},{16,8},{20,12},{24,16},{28,20},{1,25},{... | collective-permute-start | bytes 884744 | tf_op jit(solution)/shard_map/ppermute | solution.py:484
  14.3 5.8 %collective-permute-start.7 = (bf16[240,1536]{1,0:T(8,128)(2,1)}, bf16[240,1536]{1,0:T(8,128)(2,1)S(1)}, u32[]{:S(2)}, u32[]{:S(2)}) collective-permute-start(bf16[240,1536]{1,0:T(8,128)(2,1)} %get-tuple-element.32), channel_id=1, source_target_pairs={{0,2},{1,3},{2,0},{3,1},{4,6},{5,7},{6,4},{7,5},{8,10},{9,11},{10,... | collective-permute-start | bytes 2211848 | tf_op jit(solution)/shard_map/ppermute | solution.py:607
  20.1 7.2 %attention_forward.1 = (bf16[240,1536]{1,0:T(8,128)(2,1)}, bf16[12,240,240]{2,1,0:T(8,128)(2,1)S(1)}, bf16[12,240,120]{2,1,0:T(8,128)(2,1)S(1)}) custom-call(bf16[240,1536]{1,0:T(8,128)(2,1)S(1)} %bitcast.13, bf16[240,1536]{1,0:T(8,128)(2,1)S(1)} %bitcast.17, bf16[240,1536]{1,0:T(8,128)(2,1)S(1)} %bitcast.20, ...), custom_call_target="tpu_custom_call" | custom-call | flops 30000001024 | bytes 10000000000 | tf_op jit(solution)/shard_map/attention_forward/pallas_call | solution.py:62
  29.3 1.6 %collective-permute-start.9 = (bf16[192,768]{1,0:T(8,128)(2,1)}, bf16[192,768]{1,0:T(8,128)(2,1)S(1)}, u32[]{:S(2)}, u32[]{:S(2)}) collective-permute-start(bf16[192,768]{1,0:T(8,128)(2,1)} %relay.4.refs_1_.refs_2_), channel_id=1, source_target_pairs={{0,8},{4,12},{8,16},{12,20},{16,24},{20,28},{24,0},{28,4},{1,9},{5... | collective-permute-start | bytes 884744 | tf_op jit(solution)/shard_map/ppermute | solution.py:484
  33.1 6.0 %collective-permute-done.9.refs_0_ = bf16[192,768]{1,0:T(8,128)(2,1)S(1)} collective-permute-done((bf16[192,768]{1,0:T(8,128)(2,1)}, bf16[192,768]{1,0:T(8,128)(2,1)S(1)}, u32[]{:S(2)}, u32[]{:S(2)}) %collective-permute-start.9) | collective-permute-done | bytes 294944 | tf_op jit(solution)/shard_map/ppermute | solution.py:484
  40.6 1.8 %collective-permute-start.13 = (bf16[240,1536]{1,0:T(8,128)(2,1)}, bf16[240,1536]{1,0:T(8,128)(2,1)}, u32[]{:S(2)}, u32[]{:S(2)}) collective-permute-start(bf16[240,1536]{1,0:T(8,128)(2,1)} %get-tuple-element.30.refs_1_.refs_6_.refs_0_), channel_id=1, source_target_pairs={{0,2},{1,3},{2,0},{3,1},{4,6},{5,7},{6,4},{7,5},{8,10},{9,11},{10,... | collective-permute-start | bytes 2211848 | tf_op jit(solution)/shard_map/ppermute | solution.py:607
  43.0 4.8 %collective-permute-done.6.refs_5_ = bf16[192,768]{1,0:T(8,128)(2,1)S(1)} collective-permute-done((bf16[192,768]{1,0:T(8,128)(2,1)}, bf16[192,768]{1,0:T(8,128)(2,1)S(1)}, u32[]{:S(2)}, u32[]{:S(2)}) %collective-permute-start.6) | collective-permute-done | bytes 294944 | tf_op jit(solution)/shard_map/ppermute | solution.py:490
  57.0 2.0 %grad_attention_near.2.refs_5_ = bf16[240,1152]{1,0:T(8,128)(2,1)} custom-call(bf16[240,1536]{1,0:T(8,128)(2,1)S(1)} %copy-done.13, bf16[1152,768]{1,0:T(8,128)(2,1)S(1)} %assemble_weight.1.refs_1_, bf16[1152,768]{1,0:T(8,128)(2,1)S(1)} %collective-permute-done.8.refs_2_, bf16[480,768]{1,0:T(8,128)(2,1)} %quarters_for_core.1.refs_3_), custom_call_target="tpu_custom_call" | custom-call | flops 30000001024 | bytes 10000000000 | tf_op jit(solution)/shard_map/grad_attention_near/pallas_call | solution.py:62
  59.0 3.1 %collective-permute-start.18 = (bf16[240,1152]{1,0:T(8,128)(2,1)}, bf16[240,1152]{1,0:T(8,128)(2,1)}, u32[]{:S(2)}, u32[]{:S(2)}) collective-permute-start(bf16[240,1152]{1,0:T(8,128)(2,1)} %grad_attention_near.2.refs_5_), channel_id=1, source_target_pairs={{0,2},{1,3},{2,0},{3,1},{4,6},{5,7},{6,4},{7,5},{8,10},{9,11},{10,... | collective-permute-start | bytes 1658888 | tf_op jit(solution)/shard_map/ppermute | solution.py:607
  66.4 6.7 %weight_grad_parts.1 = (f32[192,768]{1,0:T(8,128)S(1)}, f32[384,768]{1,0:T(8,128)S(1)}, f32[192,768]{1,0:T(8,128)S(1)}, bf16[192,768]{1,0:T(8,128)(2,1)S(1)}, bf...) custom-call(bf16[240,1536]{1,0:T(8,128)(2,1)} %get-tuple-element.30.refs_1_.refs_6_.refs_0_, ...), custom_call_target="tpu_custom_call" | custom-call | flops 30000001024 | bytes 10000000000 | tf_op jit(solution)/shard_map/weight_grad_parts/pallas_call | solution.py:62
  77.2 5.6 %collective-permute-done.20.refs_1_ = bf16[192,768]{1,0:T(8,128)(2,1)S(1)} collective-permute-done((bf16[192,768]{1,0:T(8,128)(2,1)S(1)}, bf16[192,768]{1,0:T(8,128)(2,1)S(1)}, u32[]{:S(2)}, u32[]{:S(2)}) %collective-permute-start.20) | collective-permute-done | bytes 294944 | tf_op jit(solution)/shard_map/ppermute | solution.py:490
  83.0 3.7 %project_half.3 = bf16[240,1536]{1,0:T(8,128)(2,1)} custom-call(bf16[240,1536]{1,0:T(8,128)(2,1)} %relay.7.refs_1_.refs_0_, bf16[1152,768]{1,0:T(8,128)(2,1)S(1)} %assemble_weight.1.refs_1_, bf16[1152,768]{1,0:T(8,128)(2,1)S(1)} %collective-permute-done.8.refs_2_, bf16[192,768]{1,0:T(8,128)(2,1)S(1)} %copy-done.30, bf16[192,768]{1,0:T(8,128)(2,1)S(1)} %copy-done.16, ...), custom_call_target="tpu_custom_call" | custom-call | flops 30000001024 | bytes 10000000000 | tf_op jit(solution)/shard_map/project_half/pallas_call | solution.py:62
  86.7 1.9 %collective-permute-start.22 = (bf16[240,1536]{1,0:T(8,128)(2,1)}, bf16[240,1536]{1,0:T(8,128)(2,1)}, u32[]{:S(2)}, u32[]{:S(2)}) collective-permute-start(bf16[240,1536]{1,0:T(8,128)(2,1)} %project_half.3), channel_id=1, source_target_pairs={{0,2},{1,3},{2,0},{3,1},{4,6},{5,7},{6,4},{7,5},{8,10},{9,11},{10,... | collective-permute-start | bytes 2211848 | tf_op jit(solution)/shard_map/ppermute | solution.py:607
  89.9 6.6 %halo_backward.1 = (bf16[12,240,120]{2,1,0:T(8,128)(2,1)S(1)}, bf16[120,3072]{1,0:T(8,128)(2,1)}, bf16[120,3072]{1,0:T(8,128)(2,1)S(1)}) custom-call(bf16[240,1536]{1,0:T(8,128)(2,1)S(1)} %merge.1.refs_0_, bf16[240,1536]{1,0:T(8,128)(2,1)} %get-tuple-element.30.refs_1_.refs_6_.refs_0_, bf16[240,1536]{1,0:T(8,128)(2,1)S(1)} %bitcast.14, ...), custom_call_target="tpu_custom_call" | custom-call | flops 30000001024 | bytes 10000000000 | tf_op jit(solution)/shard_map/halo_backward/pallas_call | solution.py:62
  98.1 3.4 %collective-permute-done.17.refs_1_ = bf16[384,768]{1,0:T(8,128)(2,1)} collective-permute-done((bf16[384,768]{1,0:T(8,128)(2,1)}, bf16[384,768]{1,0:T(8,128)(2,1)}, u32[]{:S(2)}, u32[]{:S(2)}) %collective-permute-start.17) | collective-permute-done | bytes 589856 | tf_op jit(solution)/shard_map/ppermute | solution.py:490
  102.7 1.8 %collective-permute-start.26 = (bf16[192,768]{1,0:T(8,128)(2,1)S(1)}, bf16[192,768]{1,0:T(8,128)(2,1)S(1)}, u32[]{:S(2)}, u32[]{:S(2)}) collective-permute-start(bf16[192,768]{1,0:T(8,128)(2,1)S(1)} %get-tuple-element.41.refs_2_), channel_id=1, source_target_pairs={{0,24},{4,28},{8,0},{12,4},{16,8},{20,12},{24,16},{28,20},{1,25},{... | collective-permute-start | bytes 884744 | tf_op jit(solution)/shard_map/ppermute | solution.py:484
  105.1 3.1 %project_half.2.refs_0_.refs_9_ = bf16[240,1536]{1,0:T(8,128)(2,1)S(1)} custom-call(bf16[240,1536]{1,0:T(8,128)(2,1)} %get-tuple-element.30.refs_1_.refs_6_.refs_0_, bf16[1152,768]{1,0:T(8,128)(2,1)S(1)} %assemble_weight.1.refs_1_, bf16[1152,768]{1,0:T(8,128)(2,1)S(1)} %collective-permute-done.8.refs_2_, bf16[192,768]{1,0:T(8,128)(2,1)S(1)} %copy-done.30, ...), custom_call_target="tpu_custom_call" | custom-call | flops 30000001024 | bytes 10000000000 | tf_op jit(solution)/shard_map/project_half/pallas_call | solution.py:62
  108.2 6.8 %main_backward.1 = (bf16[240,1536]{1,0:T(8,128)(2,1)}, f32[240,1536]{1,0:T(8,128)S(1)}, f32[240,1536]{1,0:T(8,128)S(1)}) custom-call(bf16[240,1536]{1,0:T(8,128)(2,1)S(1)} %merge.1.refs_0_, bf16[240,1536]{1,0:T(8,128)(2,1)} %get-tuple-element.30.refs_1_.refs_6_.refs_0_, bf16[240,1536]{1,0:T(8,128)(2,1)S(1)} %bitcast.15, bf16[240,1536]{1,0:T(8,128)(2,1)S(1)} %bitcast.18, ...), custom_call_target="tpu_custom_call" | custom-call | flops 30000001024 | bytes 10000000000 | tf_op jit(solution)/shard_map/main_backward/pallas_call | solution.py:62
  115.0 2.8 %collective-permute-done.27.refs_3_ = bf16[192,768]{1,0:T(8,128)(2,1)S(1)} collective-permute-done((bf16[192,768]{1,0:T(8,128)(2,1)S(1)}, bf16[192,768]{1,0:T(8,128)(2,1)S(1)}, u32[]{:S(2)}, u32[]{:S(2)}) %collective-permute-start.27) | collective-permute-done | bytes 294944 | tf_op jit(solution)/shard_map/ppermute | solution.py:484
  117.8 1.9 %add.5 = f32[192,768]{1,0:T(8,128)} custom-call(f32[192,768]{1,0:T(8,128)S(1)} %copy-done.36, bf16[192,768]{1,0:T(8,128)(2,1)} %collective-permute-done.25.refs_1_, bf16[192,768]{1,0:T(8,128)(2,1)S(1)} %collective-permute-done.26.refs_2_, bf16[192,768]{1,0:T(8,128)(2,1)S(1)} %collective-permute-done.27.refs_3_), custom_call_target="tpu_custom_call" | custom-call | flops 30000001024 | bytes 10000000000 | tf_op jit(solution)/shard_map/add/pallas_call | solution.py:62
  119.7 2.3 %join_halves.1 = bf16[240,3072]{1,0:T(8,128)(2,1)} custom-call(bf16[240,1536]{1,0:T(8,128)(2,1)S(1)} %project_half.2.refs_0_.refs_9_, bf16[240,1536]{1,0:T(8,128)(2,1)} %collective-permute-done.22.refs_1_), custom_call_target="tpu_custom_call" | custom-call | flops 30000001024 | bytes 10000000000 | tf_op jit(solution)/shard_map/join_halves/pallas_call | solution.py:62
  122.0 3.6 %add_rims.1 = (bf16[240,1536]{1,0:T(8,128)(2,1)}, bf16[240,1536]{1,0:T(8,128)(2,1)}) custom-call(f32[240,1536]{1,0:T(8,128)S(1)} %get-tuple-element.44.refs_0_, f32[240,1536]{1,0:T(8,128)S(1)} %get-tuple-element.45.refs_1_, bf16[120,3072]{1,0:T(8,128)(2,1)} %collective-permute-done.23.refs_2_.refs_3_, ...), custom_call_target="tpu_custom_call" | custom-call | flops 30000001024 | bytes 10000000000 | tf_op jit(solution)/shard_map/add_rims/pallas_call | solution.py:62
  (130 shorter events, 30.8 us)
Async XLA Ops:
  4.1 10.2 %collective-permute-start = (bf16[120,3072]{1,0:T(8,128)(2,1)}, bf16[120,3072]{1,0:T(8,128)(2,1)S(1)}, u32[]{:S(2)}, u32[]{:S(2)}) collective-permute-start(bf16[120,3072]{1,0:T(8,128)(2,1)} %get-tuple-element.28), channel_id=1, source_target_pairs={{1,2},{2,1},{5,6},{6,5},{9,10},{10,9},{13,14},{14,13},{17,18},{18,... | collective-permute-start | bytes 2211848 | tf_op jit(solution)/shard_map/ppermute | solution.py:603
  4.8 15.2 %collective-permute-start.1 = (bf16[120,3072]{1,0:T(8,128)(2,1)}, bf16[120,3072]{1,0:T(8,128)(2,1)S(1)}, u32[]{:S(2)}, u32[]{:S(2)}) collective-permute-start(bf16[120,3072]{1,0:T(8,128)(2,1)} %get-tuple-element.29), channel_id=1, source_target_pairs={{0,1},{1,0},{2,3},{3,2},{4,5},{5,4},{6,7},{7,6},{8,9},{9,8},{10,11... | collective-permute-start | bytes 2211848 | tf_op jit(solution)/shard_map/ppermute | solution.py:611
  9.2 23.2 %collective-permute-start.5 = (bf16[192,768]{1,0:T(8,128)(2,1)}, bf16[192,768]{1,0:T(8,128)(2,1)S(1)}, u32[]{:S(2)}, u32[]{:S(2)}) collective-permute-start(bf16[192,768]{1,0:T(8,128)(2,1)} %get-tuple-element.31.refs_0_), channel_id=1, source_target_pairs={{0,24},{4,28},{8,0},{12,4},{16,8},{20,12},{24,16},{28,20},{1,25},{... | collective-permute-start | bytes 884744 | tf_op jit(solution)/shard_map/ppermute | solution.py:484
  12.8 16.5 %collective-permute-start.3 = (bf16[192,768]{1,0:T(8,128)(2,1)}, bf16[192,768]{1,0:T(8,128)(2,1)}, u32[]{:S(2)}, u32[]{:S(2)}) collective-permute-start(bf16[192,768]{1,0:T(8,128)(2,1)} %get-tuple-element.31.refs_0_), channel_id=1, source_target_pairs={{0,8},{4,12},{8,16},{12,20},{16,24},{20,28},{24,0},{28,4},{1,9},{5... | collective-permute-start | bytes 884744 | tf_op jit(solution)/shard_map/ppermute | solution.py:484
  12.8 27.8 %collective-permute-start.2 = (bf16[192,768]{1,0:T(8,128)(2,1)}, bf16[192,768]{1,0:T(8,128)(2,1)S(1)}, u32[]{:S(2)}, u32[]{:S(2)}) collective-permute-start(bf16[192,768]{1,0:T(8,128)(2,1)} %get-tuple-element.31.refs_0_), channel_id=1, source_target_pairs={{0,4},{4,0},{8,12},{12,8},{16,20},{20,16},{24,28},{28,24},{1,5},{5... | collective-permute-start | bytes 884744 | tf_op jit(solution)/shard_map/ppermute | solution.py:490
  14.3 28.1 %collective-permute-start.7 = (bf16[240,1536]{1,0:T(8,128)(2,1)}, bf16[240,1536]{1,0:T(8,128)(2,1)S(1)}, u32[]{:S(2)}, u32[]{:S(2)}) collective-permute-start(bf16[240,1536]{1,0:T(8,128)(2,1)} %get-tuple-element.32), channel_id=1, source_target_pairs={{0,2},{1,3},{2,0},{3,1},{4,6},{5,7},{6,4},{7,5},{8,10},{9,11},{10,... | collective-permute-start | bytes 2211848 | tf_op jit(solution)/shard_map/ppermute | solution.py:607
  29.3 9.8 %collective-permute-start.9 = (bf16[192,768]{1,0:T(8,128)(2,1)}, bf16[192,768]{1,0:T(8,128)(2,1)S(1)}, u32[]{:S(2)}, u32[]{:S(2)}) collective-permute-start(bf16[192,768]{1,0:T(8,128)(2,1)} %relay.4.refs_1_.refs_2_), channel_id=1, source_target_pairs={{0,8},{4,12},{8,16},{12,20},{16,24},{20,28},{24,0},{28,4},{1,9},{5... | collective-permute-start | bytes 884744 | tf_op jit(solution)/shard_map/ppermute | solution.py:484
  30.9 17.7 %collective-permute-start.4 = (bf16[192,768]{1,0:T(8,128)(2,1)}, bf16[192,768]{1,0:T(8,128)(2,1)S(1)}, u32[]{:S(2)}, u32[]{:S(2)}) collective-permute-start(bf16[192,768]{1,0:T(8,128)(2,1)} %relay.4.refs_1_.refs_2_), channel_id=1, source_target_pairs={{0,4},{4,0},{8,12},{12,8},{16,20},{20,16},{24,28},{28,24},{1,5},{5... | collective-permute-start | bytes 884744 | tf_op jit(solution)/shard_map/ppermute | solution.py:490
  32.3 34.0 %collective-permute-start.14 = (bf16[240,1536]{1,0:T(8,128)(2,1)}, bf16[240,1536]{1,0:T(8,128)(2,1)}, u32[]{:S(2)}, u32[]{:S(2)}) collective-permute-start(bf16[240,1536]{1,0:T(8,128)(2,1)} %get-tuple-element.30.refs_1_.refs_6_.refs_0_), channel_id=1, source_target_pairs={{0,1},{1,0},{2,3},{3,2},{4,5},{5,4},{6,7},{7,6},{8,9},{9,8},{10,11... | collective-permute-start | bytes 2211848 | tf_op jit(solution)/shard_map/ppermute | solution.py:611
  39.1 8.7 %collective-permute-start.6 = (bf16[192,768]{1,0:T(8,128)(2,1)}, bf16[192,768]{1,0:T(8,128)(2,1)S(1)}, u32[]{:S(2)}, u32[]{:S(2)}) collective-permute-start(bf16[192,768]{1,0:T(8,128)(2,1)} %relay.5.refs_4_.refs_1_), channel_id=1, source_target_pairs={{0,4},{4,0},{8,12},{12,8},{16,20},{20,16},{24,28},{28,24},{1,5},{5... | collective-permute-start | bytes 884744 | tf_op jit(solution)/shard_map/ppermute | solution.py:490
  40.6 23.0 %collective-permute-start.13 = (bf16[240,1536]{1,0:T(8,128)(2,1)}, bf16[240,1536]{1,0:T(8,128)(2,1)}, u32[]{:S(2)}, u32[]{:S(2)}) collective-permute-start(bf16[240,1536]{1,0:T(8,128)(2,1)} %get-tuple-element.30.refs_1_.refs_6_.refs_0_), channel_id=1, source_target_pairs={{0,2},{1,3},{2,0},{3,1},{4,6},{5,7},{6,4},{7,5},{8,10},{9,11},{10,... | collective-permute-start | bytes 2211848 | tf_op jit(solution)/shard_map/ppermute | solution.py:607
  42.4 13.4 %collective-permute-start.10 = (bf16[192,768]{1,0:T(8,128)(2,1)}, bf16[192,768]{1,0:T(8,128)(2,1)S(1)}, u32[]{:S(2)}, u32[]{:S(2)}) collective-permute-start(bf16[192,768]{1,0:T(8,128)(2,1)} %relay.6.refs_1_.refs_3_), channel_id=1, source_target_pairs={{0,4},{4,0},{8,12},{12,8},{16,20},{20,16},{24,28},{28,24},{1,5},{5... | collective-permute-start | bytes 884744 | tf_op jit(solution)/shard_map/ppermute | solution.py:490
  55.2 11.1 %collective-permute-start.16 = (bf16[480,768]{1,0:T(8,128)(2,1)}, bf16[480,768]{1,0:T(8,128)(2,1)}, u32[]{:S(2)}, u32[]{:S(2)}) collective-permute-start(bf16[480,768]{1,0:T(8,128)(2,1)} %quarters_for_core.1.refs_3_), channel_id=1, source_target_pairs={{0,1},{1,0},{2,3},{3,2},{4,5},{5,4},{6,7},{7,6},{8,9},{9,8},{10,11... | collective-permute-start | bytes 2211848 | tf_op jit(solution)/shard_map/ppermute | solution.py:611
  59.0 29.6 %collective-permute-start.18 = (bf16[240,1152]{1,0:T(8,128)(2,1)}, bf16[240,1152]{1,0:T(8,128)(2,1)}, u32[]{:S(2)}, u32[]{:S(2)}) collective-permute-start(bf16[240,1152]{1,0:T(8,128)(2,1)} %grad_attention_near.2.refs_5_), channel_id=1, source_target_pairs={{0,2},{1,3},{2,0},{3,1},{4,6},{5,7},{6,4},{7,5},{8,10},{9,11},{10,... | collective-permute-start | bytes 1658888 | tf_op jit(solution)/shard_map/ppermute | solution.py:607
  63.5 23.2 %collective-permute-start.19 = (bf16[240,384]{1,0:T(8,128)(2,1)}, bf16[240,384]{1,0:T(8,128)(2,1)}, u32[]{:S(2)}, u32[]{:S(2)}) collective-permute-start(bf16[240,384]{1,0:T(8,128)(2,1)} %grad_attention_far.2.refs_1_.refs_3_), channel_id=1, source_target_pairs={{0,2},{1,3},{2,0},{3,1},{4,6},{5,7},{6,4},{7,5},{8,10},{9,11},{10,... | collective-permute-start | bytes 552968 | tf_op jit(solution)/shard_map/ppermute | solution.py:607
  73.0 9.8 %collective-permute-start.20 = (bf16[192,768]{1,0:T(8,128)(2,1)S(1)}, bf16[192,768]{1,0:T(8,128)(2,1)S(1)}, u32[]{:S(2)}, u32[]{:S(2)}) collective-permute-start(bf16[192,768]{1,0:T(8,128)(2,1)S(1)} %get-tuple-element.37), channel_id=1, source_target_pairs={{0,4},{4,0},{8,12},{12,8},{16,20},{20,16},{24,28},{28,24},{1,5},{5... | collective-permute-start | bytes 884744 | tf_op jit(solution)/shard_map/ppermute | solution.py:490
  74.5 40.5 %collective-permute-start.25 = (bf16[192,768]{1,0:T(8,128)(2,1)}, bf16[192,768]{1,0:T(8,128)(2,1)}, u32[]{:S(2)}, u32[]{:S(2)}) collective-permute-start(bf16[192,768]{1,0:T(8,128)(2,1)} %get-tuple-element.50), channel_id=1, source_target_pairs={{0,4},{4,0},{8,12},{12,8},{16,20},{20,16},{24,28},{28,24},{1,5},{5... | collective-permute-start | bytes 884744 | tf_op jit(solution)/shard_map/ppermute | solution.py:490
  75.1 26.4 %collective-permute-start.17 = (bf16[384,768]{1,0:T(8,128)(2,1)}, bf16[384,768]{1,0:T(8,128)(2,1)}, u32[]{:S(2)}, u32[]{:S(2)}) collective-permute-start(bf16[384,768]{1,0:T(8,128)(2,1)} %get-tuple-element.34), channel_id=1, source_target_pairs={{0,4},{4,0},{8,12},{12,8},{16,20},{20,16},{24,28},{28,24},{1,5},{5... | collective-permute-start | bytes 1769480 | tf_op jit(solution)/shard_map/ppermute | solution.py:490
  82.9 21.5 %collective-permute-start.21 = (bf16[192,768]{1,0:T(8,128)(2,1)S(1)}, bf16[192,768]{1,0:T(8,128)(2,1)S(1)}, u32[]{:S(2)}, u32[]{:S(2)}) collective-permute-start(bf16[192,768]{1,0:T(8,128)(2,1)S(1)} %add.3.refs_4_.refs_7_), channel_id=1, source_target_pairs={{0,8},{4,12},{8,16},{12,20},{16,24},{20,28},{24,0},{28,4},{1,9},{5... | collective-permute-start | bytes 884744 | tf_op jit(solution)/shard_map/ppermute | solution.py:484
  86.7 32.9 %collective-permute-start.22 = (bf16[240,1536]{1,0:T(8,128)(2,1)}, bf16[240,1536]{1,0:T(8,128)(2,1)}, u32[]{:S(2)}, u32[]{:S(2)}) collective-permute-start(bf16[240,1536]{1,0:T(8,128)(2,1)} %project_half.3), channel_id=1, source_target_pairs={{0,2},{1,3},{2,0},{3,1},{4,6},{5,7},{6,4},{7,5},{8,10},{9,11},{10,... | collective-permute-start | bytes 2211848 | tf_op jit(solution)/shard_map/ppermute | solution.py:607
  96.5 25.5 %collective-permute-start.23 = (bf16[120,3072]{1,0:T(8,128)(2,1)}, bf16[120,3072]{1,0:T(8,128)(2,1)}, u32[]{:S(2)}, u32[]{:S(2)}) collective-permute-start(bf16[120,3072]{1,0:T(8,128)(2,1)} %get-tuple-element.46), channel_id=1, source_target_pairs={{1,2},{2,1},{5,6},{6,5},{9,10},{10,9},{13,14},{14,13},{17,18},{18,... | collective-permute-start | bytes 2211848 | tf_op jit(solution)/shard_map/ppermute | solution.py:603
  102.7 12.3 %collective-permute-start.26 = (bf16[192,768]{1,0:T(8,128)(2,1)S(1)}, bf16[192,768]{1,0:T(8,128)(2,1)S(1)}, u32[]{:S(2)}, u32[]{:S(2)}) collective-permute-start(bf16[192,768]{1,0:T(8,128)(2,1)S(1)} %get-tuple-element.41.refs_2_), channel_id=1, source_target_pairs={{0,24},{4,28},{8,0},{12,4},{16,8},{20,12},{24,16},{28,20},{1,25},{... | collective-permute-start | bytes 884744 | tf_op jit(solution)/shard_map/ppermute | solution.py:484
  104.5 13.2 %collective-permute-start.27 = (bf16[192,768]{1,0:T(8,128)(2,1)S(1)}, bf16[192,768]{1,0:T(8,128)(2,1)S(1)}, u32[]{:S(2)}, u32[]{:S(2)}) collective-permute-start(bf16[192,768]{1,0:T(8,128)(2,1)S(1)} %add.4.refs_7_), channel_id=1, source_target_pairs={{0,8},{4,12},{8,16},{12,20},{16,24},{20,28},{24,0},{28,4},{1,9},{5... | collective-permute-start | bytes 884744 | tf_op jit(solution)/shard_map/ppermute | solution.py:484
  115.0 7.0 %collective-permute-start.24 = (bf16[120,3072]{1,0:T(8,128)(2,1)S(1)}, bf16[120,3072]{1,0:T(8,128)(2,1)S(1)}, u32[]{:S(2)}, u32[]{:S(2)}) collective-permute-start(bf16[120,3072]{1,0:T(8,128)(2,1)S(1)} %get-tuple-element.47), channel_id=1, source_target_pairs={{0,1},{1,0},{2,3},{3,2},{4,5},{5,4},{6,7},{7,6},{8,9},{9,8},{10,11... | collective-permute-start | bytes 2211848 | tf_op jit(solution)/shard_map/ppermute | solution.py:611
  (41 other events, 243.0 us)

commit v3 on v2

--- a/solution.py
+++ b/solution.py
@@ -153,7 +153,11 @@
         (q, k, v, halo_chip, halo_chip, halo_core, halo_core),
         [col, col, col, hk, hv, hk, hv],
         [col, own, halo],
-        [shape((rows, feats)), shape((HEADS, rows, rows)), shape((HEADS, rows, TILE))],
+        [
+            shape((rows, feats)),
+            pltpu.HBM((HEADS, rows, rows), BF16),
+            pltpu.HBM((HEADS, rows, TILE), BF16),
+        ],
         "attention_forward",
         after,
         (groups,),
@@ -201,10 +205,32 @@
 
 
 def main_backward_kernel(
-    ga_ref, a_ref, q_ref, k_ref, v_ref, kl_ref, kr_ref, p_ref, dsh_ref, dq_ref, dk_ref, dv_ref
+    ga_ref,
+    a_ref,
+    q_ref,
+    k_ref,
+    v_ref,
+    kl_ref,
+    kr_ref,
+    p_ref,
+    dsh_ref,
+    chip_k,
+    chip_v,
+    core_k,
+    core_v,
+    dq_ref,
+    dk_ref,
+    dv_ref,
 ):
     rows = q_ref.shape[0]
+    y, core = place()
     facing = facing_rows(rows, TILE)
+
+    def from_others(chip, other, at):
+        far, near = chip[:, at].astype(F32), other[:, at].astype(F32)
+        low, high = jnp.where(core == 0, far, near), jnp.where(core == 0, near, far)
+        return jnp.concatenate([low, high], axis=0)
+
     for h in range(GROUP):
         at = pl.ds(h * HEAD, HEAD)
         q = q_ref[:, at]
@@ -217,45 +243,24 @@
         dq += dot_nn(jnp.where(facing, dsh, 0.0).astype(BF16), kl_ref[:, at])
         dq += dot_nn(jnp.where(facing, 0.0, dsh).astype(BF16), kr_ref[:, at])
         dq_ref[:, at] = (dq * SCALE).astype(BF16)
-        dk_ref[:, at] = dot_tn(ds, q) * SCALE
-        dv_ref[:, at] = dot_tn(p, ga)
-
-
-def main_backward(ga, att, q, k, v, halo_chip, halo_core, probs, ds_halo, after):
+        dk_ref[:, at] = (dot_tn(ds, q) * SCALE + from_others(chip_k, core_k, at)).astype(BF16)
+        dv_ref[:, at] = (dot_tn(p, ga) + from_others(chip_v, core_v, at)).astype(BF16)
+
+
+def main_backward(
+    ga, att, q, k, v, halo_chip, halo_core, probs, ds_halo, from_chip, from_core, after
+):
     rows, feats = q.shape
     groups, col, hk, hv, own, halo = attention_specs(rows, feats)
     return run(
         main_backward_kernel,
-        (ga, att, q, k, v, halo_chip, halo_core, probs, ds_halo),
-        [col, col, col, col, col, hk, hk, own, halo],
+        (ga, att, q, k, v, halo_chip, halo_core, probs, ds_halo)
+        + (from_chip, from_chip, from_core, from_core),
+        [col, col, col, col, col, hk, hk, own, halo, hk, hv, hk, hv],
         [col, col, col],
-        [shape((rows, feats)), shape((rows, feats), F32), shape((rows, feats), F32)],
+        [shape((rows, feats))] * 3,
         "main_backward",
         after,
-        (groups,),
-    )
-
-
-def add_rims_kernel(own_k, own_v, lk, lv, rk, rv, out_k, out_v):
-    y, core = place()
-    for own, chip, other, out in ((own_k, lk, rk, out_k), (own_v, lv, rv, out_v)):
-        far, near = chip[...].astype(F32), other[...].astype(F32)
-        low, high = jnp.where(core == 0, far, near), jnp.where(core == 0, near, far)
-        extra = jnp.concatenate([low, high], axis=0)
-        out[...] = (own[...] + extra).astype(BF16)
-
-
-def add_rims(dk, dv, from_chip, from_core):
-    rows, feats = dk.shape
-    groups, col, hk, hv, own, halo = attention_specs(rows, feats)
-    return run(
-        add_rims_kernel,
-        (dk, dv, from_chip, from_chip, from_core, from_core),
-        [col, col, hk, hv, hk, hv],
-        [col, col],
-        [shape((rows, feats))] * 2,
-        "add_rims",
-        (),
         (groups,),
     )
 
@@ -300,22 +305,24 @@
     )
 
 
-def quarters_for_core_kernel(cot_ref, partner_ref, out_ref):
+def core_sends_kernel(cot_ref, partner_ref, att_ref, w_ref, out_ref, att_out, w_out):
     y, core = place()
     rows, width = out_ref.shape[0] // 2, out_ref.shape[1]
     out_ref[:rows] = cot_ref[:, columns((2 * y + 1 - core) * width, width)]
     out_ref[rows:] = partner_ref[:, columns((1 - core) * width, width)]
-
-
-def quarters_for_core(cot, cot_partner, after):
+    att_out[...] = att_ref[...]
+    w_out[...] = w_ref[...]
+
+
+def core_sends(cot, cot_partner, att, shard, after):
     rows, model = cot.shape
     return run(
-        quarters_for_core_kernel,
-        (cot, cot_partner),
-        [whole()] * 2,
-        whole(),
-        shape((2 * rows, model // 4)),
-        "quarters_for_core",
+        core_sends_kernel,
+        (cot, cot_partner, att, shard),
+        [whole()] * 4,
+        [whole()] * 3,
+        [shape((2 * rows, model // 4)), shape(att.shape), shape(shard.shape)],
+        "core_sends",
         after,
     )
 
@@ -557,7 +564,7 @@
         total += dot_tn(a_sib, c_sib[:tokens]) + dot_tn(a_sibpar, c_sib[tokens:])
         return lax.psum_scatter(total, "dp", scatter_dimension=0, tiled=True)
     parts = weight_grad_parts(operands, after)
-    return [(keep, across_x(send)) for keep, send in zip(parts[:3], parts[3:])]
+    return (parts[0], across_x(parts[3])), (parts[1], across_x(parts[4])), (parts[2], parts[5])
 
 
 def add_kernel(*refs):
@@ -580,21 +587,21 @@
     )
 
 
-def split_add_kernel(keep, recv, one, three):
+def middle_sums_kernel(keep, recv, from_two, one, three):
     half = one.shape[0]
-    one[...] = keep[:half] + recv[:half].astype(F32)
+    one[...] = (keep[:half] + recv[:half].astype(F32) + from_two[...].astype(F32)).astype(BF16)
     three[...] = (keep[half:] + recv[half:].astype(F32)).astype(BF16)
 
 
-def split_add(keep, recv, after=()):
+def middle_sums(keep, recv, from_two, after):
     dims = (keep.shape[0] // 2, keep.shape[1])
     return run(
-        split_add_kernel,
-        (keep, recv),
+        middle_sums_kernel,
+        (keep, recv, from_two),
+        [whole()] * 3,
         [whole()] * 2,
-        [whole()] * 2,
-        [shape(dims, F32), shape(dims)],
-        "split_add",
+        [shape(dims)] * 2,
+        "middle_sums",
         after,
     )
 
@@ -622,16 +629,12 @@
         z1, z3 = along_z(shard, 1), along_z(shard, 3)
         x0 = across_x(shard)
     cot_partner = to_partner(cot_send)
-    att, probs, probs_halo = attention_forward(q, k, v, halo_chip, halo_core, ())
+    att, probs, probs_halo = attention_forward(q, k, v, halo_chip, halo_core, (z1, z3) if is_grid() else ())
     att_partner = to_partner(att)
-    att_core = to_core(att)
     if is_grid():
-        z1 = relay(z1, (att,))
-        z3 = relay(z3, (z1,))
-        z2 = relay(along_z(z1, 1), (z3,))
-        near_own = assemble(
-            (shard, x0, z1, across_x(z1), z3, across_x(z3)), (att, cot_partner)
-        )
+        x1, x3 = across_x(z1), across_x(z3)
+        z2 = relay(along_z(z1, 1), (att,))
+        near_own = assemble((shard, x0, z1, x1, z3, x3), (att, cot_partner))
         far_own = (z2, across_x(z2))
     else:
         w_own = lax.all_gather(out_weight, "dp", axis=0, tiled=True)
@@ -639,9 +642,9 @@
         near_own = w_own[:cut]
         far_own = (w_own[cut : cut + cut // 6], w_own[cut + cut // 6 :])
     near = (near_own, to_core(near_own))
-    far = (*far_own, to_core(far_own[0]), to_core(far_own[1]))
-    cot_send_core = quarters_for_core(cot, cot_partner, ())
-    cot_core = to_core(cot_send_core)
+    cot_send_core, att_send, far_send = core_sends(cot, cot_partner, att, far_own[0], (near_own,))
+    cot_core, att_core = to_core(cot_send_core), to_core(att_send)
+    far = (*far_own, to_core(far_send), to_core(far_own[1]))
 
     send_near = grad_attention_near(cot_partner, near, BF16, False, (cot_send_core,))
     recv_near = to_partner(send_near)
@@ -658,27 +661,25 @@
     mine_far = grad_attention_far(
         cot, far, F32, True, (mine_near, parts[2][0]) if grid else (mine_near,)
     )
+    proj_partner = project_half(att_partner, near, far, (mine_far,))
+    proj_recv = to_partner(proj_partner)
     if grid:
-        far_sum = add(parts[0], BF16, (mine_far,))
+        far_sum = add(parts[0], BF16, (proj_partner,))
         from_two = along_z(far_sum, 1)
-    proj_partner = project_half(att_partner, near, far, (far_sum,) if grid else (mine_far,))
-    proj_recv = to_partner(proj_partner)
+        recv = across_x(relay(parts[2][1], (far_sum,)))
 
     ga = merge(mine_near, mine_far, recv_near, recv_far, (far_sum,) if grid else ())
     ds_halo, back_chip, back_core = halo_backward(ga, att, q, halo_chip, halo_core, probs_halo)
     from_chip, from_core = between_chips(back_chip), to_core(back_core)
     if grid:
-        one, three = split_add(*parts[1], (ds_halo,))
-        from_three = along_z(three, 3)
-        one_sum = add((one, from_two), BF16, (three,))
-        from_one = along_z(one_sum, 1)
-    proj_own = project_half(att, near, far, (one_sum,) if grid else (proj_partner,))
+        one, three = middle_sums(*parts[1], from_two, (ds_halo,))
+        from_one, from_three = along_z(one, 1), along_z(three, 3)
+    proj_own = project_half(att, near, far, (one,) if grid else (proj_partner,))
     dq, dk, dv = main_backward(
-        ga, att, q, k, v, halo_chip, halo_core, probs, ds_halo, (proj_own,)
+        ga, att, q, k, v, halo_chip, halo_core, probs, ds_halo, from_chip, from_core, (proj_own,)
     )
     projected = join_halves(proj_own, proj_recv)
-    dk, dv = add_rims(dk, dv, from_chip, from_core)
-    weight_grad = add((*parts[2], from_three, from_one), F32) if grid else parts
+    weight_grad = add((parts[2][0], recv, from_three, from_one), F32, (dq,)) if grid else parts
     return projected[None], dq[None], dk[None], dv[None], weight_grad
 
 

time: 126 us -> 113 us (0.90)
  starting transfers between devices: 36.3 us -> 29.4 us
  waiting for transfers between devices: 23.7 us -> 21.2 us
  local copies, waits for them, and re-layouts: 9.5 us -> 7.54 us
  Pallas kernels: 55.2 us -> 53.6 us
    ppermute x5, starting transfers between devices: 12.6 us -> 2.73 us  [to_partner(): return lax.ppermute(block, 'tile', [(0, 2), (1, 3), (2, 0), (3, 1)])]
    ppermute x7, waiting for transfers between devices: 13.8 us -> 7.41 us  [across_x(): return lax.ppermute(block, 'dp', [(i, i ^ 1) for i in range(8)])]
    ppermute x6, waiting for transfers between devices: 8.78 us -> 13.7 us  [along_z(): lax.ppermute(block, 'dp', [(2 * z + x, 2 * ((z + shift) % 4) + x) for z i...]
    unnamed x74 -> x84, local copies, waits for them, and re-layouts: 9.5 us -> 7.54 us
    ppermute x8, starting transfers between devices: 5.22 us -> 7.13 us  [to_core(): return lax.ppermute(block, 'tile', [(0, 1), (1, 0), (2, 3), (3, 2)])]
    ppermute x6, starting transfers between devices: 7.55 us -> 9.41 us  [along_z(): lax.ppermute(block, 'dp', [(2 * z + x, 2 * ((z + shift) % 4) + x) for z i...]
    pallas_call x20 -> x18, Pallas kernels: 55.2 us -> 53.6 us  [run(): pl.pallas_call(body, grid=grid, in_specs=list(in_specs) + [anywhere()] *...]
  transfers between devices with their start and end apart: 28 -> 28, of which waited for: 6 -> 7; matrix products, arithmetic and copies ran while one was open for 0% -> 0% of each run, Pallas kernels for 38% -> 43%
where the time goes in v3:
time: 113 us
  Pallas kernels  53.6 us (47%)
  starting transfers between devices  29.4 us (26%)
  waiting for transfers between devices  21.2 us (19%)
  local copies, waits for them, and re-layouts  7.54 us (7%)
    pallas_call x18, Pallas kernels, run(): pl.pallas_call(body, grid=grid, in_specs=list(in_specs) + [anywhere()] *...  53.6 us
    ppermute x6, waiting for transfers between devices, along_z(): lax.ppermute(block, 'dp', [(2 * z + x, 2 * ((z + shift) % 4) + x) for z i...  13.7 us
    ppermute x6, starting transfers between devices, along_z(): lax.ppermute(block, 'dp', [(2 * z + x, 2 * ((z + shift) % 4) + x) for z i...  9.41 us
    ppermute x7, starting transfers between devices, across_x(): return lax.ppermute(block, 'dp', [(i, i ^ 1) for i in range(8)])  8.72 us
    unnamed x84, local copies, waits for them, and re-layouts  7.54 us
    ppermute x7, waiting for transfers between devices, across_x(): return lax.ppermute(block, 'dp', [(i, i ^ 1) for i in range(8)])  7.41 us
    ppermute x8, starting transfers between devices, to_core(): return lax.ppermute(block, 'tile', [(0, 1), (1, 0), (2, 3), (3, 2)])  7.13 us
    ppermute x5, starting transfers between devices, to_partner(): return lax.ppermute(block, 'tile', [(0, 2), (1, 3), (2, 0), (3, 1)])  2.73 us
  transfers between devices with their start and end apart: 28, of which 7 were waited for; matrix products, arithmetic and copies ran while one was open for 0% of the time, Pallas kernels for 43%

profile of v3, /device:TPU:0, one launch (start us, length us, event | category | flops | bytes accessed | tf_op | source)
XLA Modules:
  0.0 112.8 jit_solution(6667602872453157180)
XLA Ops:
  0.7 3.5 %first_sends.1 = (bf16[120,3072]{1,0:T(8,128)(2,1)}, bf16[120,3072]{1,0:T(8,128)(2,1)}, bf16[192,768]{1,0:T(8,128)(2,1)}, bf16[240,1536]{1,0:T(8,128)(2,1)}) custom-call(bf16[240,1536]{1,0:T(8,128)(2,1)} %bitcast.16, bf16[240,1536]{1,0:T(8,128)(2,1)} %bitcast.19, bf16[192,768]{1,0:T(8,128)(2,1)} %refs_2_.1, bf16[240,3072]{1,0:T(8,128)(2,1)} %bitcast.8), custom_call_target="tpu_custom_call" | custom-call | flops 30000001024 | bytes 10000000000 | tf_op jit(solution)/shard_map/first_sends/pallas_call | solution.py:62
  4.8 4.3 %collective-permute-start.1 = (bf16[120,3072]{1,0:T(8,128)(2,1)}, bf16[120,3072]{1,0:T(8,128)(2,1)S(1)}, u32[]{:S(2)}, u32[]{:S(2)}) collective-permute-start(bf16[120,3072]{1,0:T(8,128)(2,1)} %get-tuple-element.30), channel_id=1, source_target_pairs={{0,1},{1,0},{2,3},{3,2},{4,5},{5,4},{6,7},{7,6},{8,9},{9,8},{10,11... | collective-permute-start | bytes 2211848 | tf_op jit(solution)/shard_map/ppermute | solution.py:618
  9.2 3.6 %collective-permute-start.3 = (bf16[192,768]{1,0:T(8,128)(2,1)}, bf16[192,768]{1,0:T(8,128)(2,1)S(1)}, u32[]{:S(2)}, u32[]{:S(2)}) collective-permute-start(bf16[192,768]{1,0:T(8,128)(2,1)} %get-tuple-element.31.refs_0_), channel_id=1, source_target_pairs={{0,24},{4,28},{8,0},{12,4},{16,8},{20,12},{24,16},{28,20},{1,25},{... | collective-permute-start | bytes 884744 | tf_op jit(solution)/shard_map/ppermute | solution.py:491
  14.3 6.2 %collective-permute-done.3.refs_8_.refs_4_ = bf16[192,768]{1,0:T(8,128)(2,1)S(1)} collective-permute-done((bf16[192,768]{1,0:T(8,128)(2,1)}, bf16[192,768]{1,0:T(8,128)(2,1)S(1)}, u32[]{:S(2)}, u32[]{:S(2)}) %collective-permute-start.3) | collective-permute-done | bytes 294944 | tf_op jit(solution)/shard_map/ppermute | solution.py:491
  20.5 6.2 %collective-permute-done.2.refs_7_.refs_2_ = bf16[192,768]{1,0:T(8,128)(2,1)S(1)} collective-permute-done((bf16[192,768]{1,0:T(8,128)(2,1)}, bf16[192,768]{1,0:T(8,128)(2,1)S(1)}, u32[]{:S(2)}, u32[]{:S(2)}) %collective-permute-start.2) | collective-permute-done | bytes 294944 | tf_op jit(solution)/shard_map/ppermute | solution.py:491
  26.7 1.6 %collective-permute-start.9 = (bf16[192,768]{1,0:T(8,128)(2,1)S(1)}, bf16[192,768]{1,0:T(8,128)(2,1)S(1)}, u32[]{:S(2)}, u32[]{:S(2)}) collective-permute-start(bf16[192,768]{1,0:T(8,128)(2,1)S(1)} %collective-permute-done.2.refs_7_.refs_2_), channel_id=1, source_target_pairs={{0,8},{4,12},{8,16},{12,20},{16,24},{20,28},{24,0},{28,4},{1,9},{5... | collective-permute-start | bytes 884744 | tf_op jit(solution)/shard_map/ppermute | solution.py:491
  30.4 7.2 %attention_forward.1 = (bf16[240,1536]{1,0:T(8,128)(2,1)}, bf16[12,240,240]{2,1,0:T(8,128)(2,1)}, bf16[12,240,120]{2,1,0:T(8,128)(2,1)}) custom-call(bf16[240,1536]{1,0:T(8,128)(2,1)S(1)} %bitcast.13, bf16[240,1536]{1,0:T(8,128)(2,1)S(1)} %bitcast.17, bf16[240,1536]{1,0:T(8,128)(2,1)S(1)} %bitcast.20, ...), custom_call_target="tpu_custom_call" | custom-call | flops 30000001024 | bytes 10000000000 | tf_op jit(solution)/shard_map/attention_forward/pallas_call | solution.py:62
  38.7 1.6 %collective-permute-start.10 = (bf16[192,768]{1,0:T(8,128)(2,1)}, bf16[192,768]{1,0:T(8,128)(2,1)S(1)}, u32[]{:S(2)}, u32[]{:S(2)}) collective-permute-start(bf16[192,768]{1,0:T(8,128)(2,1)} %relay.3.refs_3_.refs_1_), channel_id=1, source_target_pairs={{0,4},{4,0},{8,12},{12,8},{16,20},{20,16},{24,28},{28,24},{1,5},{5... | collective-permute-start | bytes 884744 | tf_op jit(solution)/shard_map/ppermute | solution.py:497
  40.2 4.5 %collective-permute-done.6.refs_5_ = bf16[192,768]{1,0:T(8,128)(2,1)} collective-permute-done((bf16[192,768]{1,0:T(8,128)(2,1)S(1)}, bf16[192,768]{1,0:T(8,128)(2,1)}, u32[]{:S(2)}, u32[]{:S(2)}) %collective-permute-start.6) | collective-permute-done | bytes 294944 | tf_op jit(solution)/shard_map/ppermute | solution.py:497
  48.0 2.4 %core_sends.1 = (bf16[480,768]{1,0:T(8,128)(2,1)}, bf16[240,1536]{1,0:T(8,128)(2,1)}, bf16[192,768]{1,0:T(8,128)(2,1)S(1)}) custom-call(bf16[240,3072]{1,0:T(8,128)(2,1)S(1)} %bitcast.9, bf16[240,1536]{1,0:T(8,128)(2,1)S(1)} %copy-done.13, bf16[240,1536]{1,0:T(8,128)(2,1)} %get-tuple-element.32.refs_6_.refs_1_.refs_2_.refs_0_, ...), custom_call_target="tpu_custom_call" | custom-call | flops 30000001024 | bytes 10000000000 | tf_op jit(solution)/shard_map/core_sends/pallas_call | solution.py:62
  51.5 2.0 %grad_attention_near.2.refs_5_ = bf16[240,1152]{1,0:T(8,128)(2,1)} custom-call(bf16[240,1536]{1,0:T(8,128)(2,1)S(1)} %copy-done.14, bf16[1152,768]{1,0:T(8,128)(2,1)S(1)} %assemble_weight.1.refs_4_.refs_1_, bf16[1152,768]{1,0:T(8,128)(2,1)S(1)} %collective-permute-done.8.refs_2_, bf16[480,768]{1,0:T(8,128)(2,1)} %get-tuple-element.35.refs_3_), custom_call_target="tpu_custom_call" | custom-call | flops 30000001024 | bytes 10000000000 | tf_op jit(solution)/shard_map/grad_attention_near/pallas_call | solution.py:62
  55.3 1.6 %collective-permute-start.21 = (bf16[240,384]{1,0:T(8,128)(2,1)}, bf16[240,384]{1,0:T(8,128)(2,1)}, u32[]{:S(2)}, u32[]{:S(2)}) collective-permute-start(bf16[240,384]{1,0:T(8,128)(2,1)} %grad_attention_far.2.refs_1_.refs_3_), channel_id=1, source_target_pairs={{0,2},{1,3},{2,0},{3,1},{4,6},{5,7},{6,4},{7,5},{8,10},{9,11},{10,... | collective-permute-start | bytes 552968 | tf_op jit(solution)/shard_map/ppermute | solution.py:614
  59.6 6.9 %weight_grad_parts.1 = (f32[192,768]{1,0:T(8,128)S(1)}, f32[384,768]{1,0:T(8,128)S(1)}, f32[192,768]{1,0:T(8,128)S(1)}, bf16[192,768]{1,0:T(8,128)(2,1)S(1)}, bf...) custom-call(bf16[240,1536]{1,0:T(8,128)(2,1)} %get-tuple-element.32.refs_6_.refs_1_.refs_2_.refs_0_, ...), custom_call_target="tpu_custom_call" | custom-call | flops 30000001024 | bytes 10000000000 | tf_op jit(solution)/shard_map/weight_grad_parts/pallas_call | solution.py:62
  66.5 1.6 %collective-permute-start.18 = (bf16[192,768]{1,0:T(8,128)(2,1)S(1)}, bf16[192,768]{1,0:T(8,128)(2,1)S(1)}, u32[]{:S(2)}, u32[]{:S(2)}) collective-permute-start(bf16[192,768]{1,0:T(8,128)(2,1)S(1)} %get-tuple-element.40), channel_id=1, source_target_pairs={{0,4},{4,0},{8,12},{12,8},{16,20},{20,16},{24,28},{28,24},{1,5},{5... | collective-permute-start | bytes 884744 | tf_op jit(solution)/shard_map/ppermute | solution.py:497
  69.4 3.8 %project_half.2.refs_2_ = bf16[240,1536]{1,0:T(8,128)(2,1)} custom-call(bf16[240,1536]{1,0:T(8,128)(2,1)} %relay.4.refs_1_.refs_0_, bf16[1152,768]{1,0:T(8,128)(2,1)S(1)} %assemble_weight.1.refs_4_.refs_1_, bf16[1152,768]{1,0:T(8,128)(2,1)S(1)} %collective-permute-done.8.refs_2_, bf16[192,768]{1,0:T(8,128)(2,1)S(1)} %copy-done.29, ...), custom_call_target="tpu_custom_call" | custom-call | flops 30000001024 | bytes 10000000000 | tf_op jit(solution)/shard_map/project_half/pallas_call | solution.py:62
  73.6 2.8 %collective-permute-done.18.refs_1_ = bf16[192,768]{1,0:T(8,128)(2,1)S(1)} collective-permute-done((bf16[192,768]{1,0:T(8,128)(2,1)S(1)}, bf16[192,768]{1,0:T(8,128)(2,1)S(1)}, u32[]{:S(2)}, u32[]{:S(2)}) %collective-permute-start.18) | collective-permute-done | bytes 294944 | tf_op jit(solution)/shard_map/ppermute | solution.py:497
  77.3 1.6 %collective-permute-start.25 = (bf16[192,768]{1,0:T(8,128)(2,1)}, bf16[192,768]{1,0:T(8,128)(2,1)}, u32[]{:S(2)}, u32[]{:S(2)}) collective-permute-start(bf16[192,768]{1,0:T(8,128)(2,1)} %relay.5), channel_id=1, source_target_pairs={{0,4},{4,0},{8,12},{12,8},{16,20},{20,16},{24,28},{28,24},{1,5},{5... | collective-permute-start | bytes 884744 | tf_op jit(solution)/shard_map/ppermute | solution.py:497
  82.4 5.9 %halo_backward.1 = (bf16[12,240,120]{2,1,0:T(8,128)(2,1)S(1)}, bf16[120,3072]{1,0:T(8,128)(2,1)S(1)}, bf16[120,3072]{1,0:T(8,128)(2,1)S(1)}) custom-call(bf16[240,1536]{1,0:T(8,128)(2,1)S(1)} %merge.1.refs_0_, bf16[240,1536]{1,0:T(8,128)(2,1)} %get-tuple-element.32.refs_6_.refs_1_.refs_2_.refs_0_, bf16[240,1536]{1,0:T(8,128)(2,1)S(1)} %bitcast.14, ...), custom_call_target="tpu_custom_call" | custom-call | flops 30000001024 | bytes 10000000000 | tf_op jit(solution)/shard_map/halo_backward/pallas_call | solution.py:62
  89.2 1.7 %collective-permute-start.24 = (bf16[120,3072]{1,0:T(8,128)(2,1)S(1)}, bf16[120,3072]{1,0:T(8,128)(2,1)S(1)}, u32[]{:S(2)}, u32[]{:S(2)}) collective-permute-start(bf16[120,3072]{1,0:T(8,128)(2,1)S(1)} %get-tuple-element.47), channel_id=1, source_target_pairs={{0,1},{1,0},{2,3},{3,2},{4,5},{5,4},{6,7},{7,6},{8,9},{9,8},{10,11... | collective-permute-start | bytes 2211848 | tf_op jit(solution)/shard_map/ppermute | solution.py:618
  93.7 2.8 %project_half.3.refs_0_.refs_13_ = bf16[240,1536]{1,0:T(8,128)(2,1)S(1)} custom-call(bf16[240,1536]{1,0:T(8,128)(2,1)} %get-tuple-element.32.refs_6_.refs_1_.refs_2_.refs_0_, bf16[1152,768]{1,0:T(8,128)(2,1)S(1)} %assemble_weight.1.refs_4_.refs_1_, bf16[1152,768]{1,0:T(8,128)(2,1)S(1)} %collective-permute-done.8.refs_2_, bf16[192,768]{1,0:T(8,128)(2,1)S(1)} %copy-done.30, ...), custom_call_target="tpu_custom_call" | custom-call | flops 30000001024 | bytes 10000000000 | tf_op jit(solution)/shard_map/project_half/pallas_call | solution.py:62
  96.6 2.7 %collective-permute-start.26 = (bf16[192,768]{1,0:T(8,128)(2,1)S(1)}, bf16[192,768]{1,0:T(8,128)(2,1)S(1)}, u32[]{:S(2)}, u32[]{:S(2)}) collective-permute-start(bf16[192,768]{1,0:T(8,128)(2,1)S(1)} %get-tuple-element.52), channel_id=1, source_target_pairs={{0,24},{4,28},{8,0},{12,4},{16,8},{20,12},{24,16},{28,20},{1,25},{... | collective-permute-start | bytes 884744 | tf_op jit(solution)/shard_map/ppermute | solution.py:491
  99.2 2.3 %join_halves.1 = bf16[240,3072]{1,0:T(8,128)(2,1)} custom-call(bf16[240,1536]{1,0:T(8,128)(2,1)S(1)} %project_half.3.refs_0_.refs_13_, bf16[240,1536]{1,0:T(8,128)(2,1)} %collective-permute-done.22.refs_1_), custom_call_target="tpu_custom_call" | custom-call | flops 30000001024 | bytes 10000000000 | tf_op jit(solution)/shard_map/join_halves/pallas_call | solution.py:62
  101.6 6.9 %main_backward.1 = (bf16[240,1536]{1,0:T(8,128)(2,1)}, bf16[240,1536]{1,0:T(8,128)(2,1)}, bf16[240,1536]{1,0:T(8,128)(2,1)}) custom-call(bf16[240,1536]{1,0:T(8,128)(2,1)S(1)} %merge.1.refs_0_, bf16[240,1536]{1,0:T(8,128)(2,1)} %get-tuple-element.32.refs_6_.refs_1_.refs_2_.refs_0_, bf16[240,1536]{1,0:T(8,128)(2,1)S(1)} %bitcast.15, ...), custom_call_target="tpu_custom_call" | custom-call | flops 30000001024 | bytes 10000000000 | tf_op jit(solution)/shard_map/main_backward/pallas_call | solution.py:62
  110.9 1.9 %add.3 = f32[192,768]{1,0:T(8,128)} custom-call(f32[192,768]{1,0:T(8,128)S(1)} %copy-done.39, bf16[192,768]{1,0:T(8,128)(2,1)} %collective-permute-done.25.refs_1_, bf16[192,768]{1,0:T(8,128)(2,1)S(1)} %collective-permute-done.26.refs_2_, bf16[192,768]{1,0:T(8,128)(2,1)S(1)} %collective-permute-done.27.refs_3_, bf16[240,1536]{1,0:T(8,128)(2,1)S(1)} %copy-done.31), custom_call_target="tpu_custom_call" | custom-call | flops 30000001024 | bytes 10000000000 | tf_op jit(solution)/shard_map/add/pallas_call | solution.py:62
  (137 shorter events, 26.2 us)
Async XLA Ops:
  4.1 24.2 %collective-permute-start = (bf16[120,3072]{1,0:T(8,128)(2,1)}, bf16[120,3072]{1,0:T(8,128)(2,1)S(1)}, u32[]{:S(2)}, u32[]{:S(2)}) collective-permute-start(bf16[120,3072]{1,0:T(8,128)(2,1)} %get-tuple-element.29), channel_id=1, source_target_pairs={{1,2},{2,1},{5,6},{6,5},{9,10},{10,9},{13,14},{14,13},{17,18},{18,... | collective-permute-start | bytes 2211848 | tf_op jit(solution)/shard_map/ppermute | solution.py:610
  4.8 25.0 %collective-permute-start.1 = (bf16[120,3072]{1,0:T(8,128)(2,1)}, bf16[120,3072]{1,0:T(8,128)(2,1)S(1)}, u32[]{:S(2)}, u32[]{:S(2)}) collective-permute-start(bf16[120,3072]{1,0:T(8,128)(2,1)} %get-tuple-element.30), channel_id=1, source_target_pairs={{0,1},{1,0},{2,3},{3,2},{4,5},{5,4},{6,7},{7,6},{8,9},{9,8},{10,11... | collective-permute-start | bytes 2211848 | tf_op jit(solution)/shard_map/ppermute | solution.py:618
  9.2 11.3 %collective-permute-start.3 = (bf16[192,768]{1,0:T(8,128)(2,1)}, bf16[192,768]{1,0:T(8,128)(2,1)S(1)}, u32[]{:S(2)}, u32[]{:S(2)}) collective-permute-start(bf16[192,768]{1,0:T(8,128)(2,1)} %get-tuple-element.31.refs_0_), channel_id=1, source_target_pairs={{0,24},{4,28},{8,0},{12,4},{16,8},{20,12},{24,16},{28,20},{1,25},{... | collective-permute-start | bytes 884744 | tf_op jit(solution)/shard_map/ppermute | solution.py:491
  12.8 13.9 %collective-permute-start.2 = (bf16[192,768]{1,0:T(8,128)(2,1)}, bf16[192,768]{1,0:T(8,128)(2,1)S(1)}, u32[]{:S(2)}, u32[]{:S(2)}) collective-permute-start(bf16[192,768]{1,0:T(8,128)(2,1)} %get-tuple-element.31.refs_0_), channel_id=1, source_target_pairs={{0,8},{4,12},{8,16},{12,20},{16,24},{20,28},{24,0},{28,4},{1,9},{5... | collective-permute-start | bytes 884744 | tf_op jit(solution)/shard_map/ppermute | solution.py:491
  12.8 25.9 %collective-permute-start.4 = (bf16[192,768]{1,0:T(8,128)(2,1)}, bf16[192,768]{1,0:T(8,128)(2,1)}, u32[]{:S(2)}, u32[]{:S(2)}) collective-permute-start(bf16[192,768]{1,0:T(8,128)(2,1)} %get-tuple-element.31.refs_0_), channel_id=1, source_target_pairs={{0,4},{4,0},{8,12},{12,8},{16,20},{20,16},{24,28},{28,24},{1,5},{5... | collective-permute-start | bytes 884744 | tf_op jit(solution)/shard_map/ppermute | solution.py:497
  20.5 24.2 %collective-permute-start.7 = (bf16[240,1536]{1,0:T(8,128)(2,1)}, bf16[240,1536]{1,0:T(8,128)(2,1)S(1)}, u32[]{:S(2)}, u32[]{:S(2)}) collective-permute-start(bf16[240,1536]{1,0:T(8,128)(2,1)} %get-tuple-element.33), channel_id=1, source_target_pairs={{0,2},{1,3},{2,0},{3,1},{4,6},{5,7},{6,4},{7,5},{8,10},{9,11},{10,... | collective-permute-start | bytes 2211848 | tf_op jit(solution)/shard_map/ppermute | solution.py:614
  26.7 10.9 %collective-permute-start.9 = (bf16[192,768]{1,0:T(8,128)(2,1)S(1)}, bf16[192,768]{1,0:T(8,128)(2,1)S(1)}, u32[]{:S(2)}, u32[]{:S(2)}) collective-permute-start(bf16[192,768]{1,0:T(8,128)(2,1)S(1)} %collective-permute-done.2.refs_7_.refs_2_), channel_id=1, source_target_pairs={{0,8},{4,12},{8,16},{12,20},{16,24},{20,28},{24,0},{28,4},{1,9},{5... | collective-permute-start | bytes 884744 | tf_op jit(solution)/shard_map/ppermute | solution.py:491
  28.4 16.4 %collective-permute-start.5 = (bf16[192,768]{1,0:T(8,128)(2,1)S(1)}, bf16[192,768]{1,0:T(8,128)(2,1)}, u32[]{:S(2)}, u32[]{:S(2)}) collective-permute-start(bf16[192,768]{1,0:T(8,128)(2,1)S(1)} %collective-permute-done.2.refs_7_.refs_2_), channel_id=1, source_target_pairs={{0,4},{4,0},{8,12},{12,8},{16,20},{20,16},{24,28},{28,24},{1,5},{5... | collective-permute-start | bytes 884744 | tf_op jit(solution)/shard_map/ppermute | solution.py:497
  29.8 14.9 %collective-permute-start.6 = (bf16[192,768]{1,0:T(8,128)(2,1)S(1)}, bf16[192,768]{1,0:T(8,128)(2,1)}, u32[]{:S(2)}, u32[]{:S(2)}) collective-permute-start(bf16[192,768]{1,0:T(8,128)(2,1)S(1)} %collective-permute-done.3.refs_8_.refs_4_), channel_id=1, source_target_pairs={{0,4},{4,0},{8,12},{12,8},{16,20},{20,16},{24,28},{28,24},{1,5},{5... | collective-permute-start | bytes 884744 | tf_op jit(solution)/shard_map/ppermute | solution.py:497
  38.3 18.6 %collective-permute-start.13 = (bf16[240,1536]{1,0:T(8,128)(2,1)}, bf16[240,1536]{1,0:T(8,128)(2,1)}, u32[]{:S(2)}, u32[]{:S(2)}) collective-permute-start(bf16[240,1536]{1,0:T(8,128)(2,1)} %get-tuple-element.32.refs_6_.refs_1_.refs_2_.refs_0_), channel_id=1, source_target_pairs={{0,2},{1,3},{2,0},{3,1},{4,6},{5,7},{6,4},{7,5},{8,10},{9,11},{10,... | collective-permute-start | bytes 2211848 | tf_op jit(solution)/shard_map/ppermute | solution.py:614
  38.7 12.2 %collective-permute-start.10 = (bf16[192,768]{1,0:T(8,128)(2,1)}, bf16[192,768]{1,0:T(8,128)(2,1)S(1)}, u32[]{:S(2)}, u32[]{:S(2)}) collective-permute-start(bf16[192,768]{1,0:T(8,128)(2,1)} %relay.3.refs_3_.refs_1_), channel_id=1, source_target_pairs={{0,4},{4,0},{8,12},{12,8},{16,20},{20,16},{24,28},{28,24},{1,5},{5... | collective-permute-start | bytes 884744 | tf_op jit(solution)/shard_map/ppermute | solution.py:497
  50.9 8.7 %collective-permute-start.14 = (bf16[240,1536]{1,0:T(8,128)(2,1)}, bf16[240,1536]{1,0:T(8,128)(2,1)}, u32[]{:S(2)}, u32[]{:S(2)}) collective-permute-start(bf16[240,1536]{1,0:T(8,128)(2,1)} %get-tuple-element.36), channel_id=1, source_target_pairs={{0,1},{1,0},{2,3},{3,2},{4,5},{5,4},{6,7},{7,6},{8,9},{9,8},{10,11... | collective-permute-start | bytes 2211848 | tf_op jit(solution)/shard_map/ppermute | solution.py:618
  50.9 8.7 %collective-permute-start.16 = (bf16[480,768]{1,0:T(8,128)(2,1)}, bf16[480,768]{1,0:T(8,128)(2,1)}, u32[]{:S(2)}, u32[]{:S(2)}) collective-permute-start(bf16[480,768]{1,0:T(8,128)(2,1)} %get-tuple-element.35.refs_3_), channel_id=1, source_target_pairs={{0,1},{1,0},{2,3},{3,2},{4,5},{5,4},{6,7},{7,6},{8,9},{9,8},{10,11... | collective-permute-start | bytes 2211848 | tf_op jit(solution)/shard_map/ppermute | solution.py:618
  53.5 25.3 %collective-permute-start.20 = (bf16[240,1152]{1,0:T(8,128)(2,1)}, bf16[240,1152]{1,0:T(8,128)(2,1)}, u32[]{:S(2)}, u32[]{:S(2)}) collective-permute-start(bf16[240,1152]{1,0:T(8,128)(2,1)} %grad_attention_near.2.refs_5_), channel_id=1, source_target_pairs={{0,2},{1,3},{2,0},{3,1},{4,6},{5,7},{6,4},{7,5},{8,10},{9,11},{10,... | collective-permute-start | bytes 1658888 | tf_op jit(solution)/shard_map/ppermute | solution.py:614
  55.3 21.9 %collective-permute-start.21 = (bf16[240,384]{1,0:T(8,128)(2,1)}, bf16[240,384]{1,0:T(8,128)(2,1)}, u32[]{:S(2)}, u32[]{:S(2)}) collective-permute-start(bf16[240,384]{1,0:T(8,128)(2,1)} %grad_attention_far.2.refs_1_.refs_3_), channel_id=1, source_target_pairs={{0,2},{1,3},{2,0},{3,1},{4,6},{5,7},{6,4},{7,5},{8,10},{9,11},{10,... | collective-permute-start | bytes 552968 | tf_op jit(solution)/shard_map/ppermute | solution.py:614
  66.5 9.9 %collective-permute-start.18 = (bf16[192,768]{1,0:T(8,128)(2,1)S(1)}, bf16[192,768]{1,0:T(8,128)(2,1)S(1)}, u32[]{:S(2)}, u32[]{:S(2)}) collective-permute-start(bf16[192,768]{1,0:T(8,128)(2,1)S(1)} %get-tuple-element.40), channel_id=1, source_target_pairs={{0,4},{4,0},{8,12},{12,8},{16,20},{20,16},{24,28},{28,24},{1,5},{5... | collective-permute-start | bytes 884744 | tf_op jit(solution)/shard_map/ppermute | solution.py:497
  68.1 21.1 %collective-permute-start.17 = (bf16[384,768]{1,0:T(8,128)(2,1)}, bf16[384,768]{1,0:T(8,128)(2,1)}, u32[]{:S(2)}, u32[]{:S(2)}) collective-permute-start(bf16[384,768]{1,0:T(8,128)(2,1)} %get-tuple-element.38), channel_id=1, source_target_pairs={{0,4},{4,0},{8,12},{12,8},{16,20},{20,16},{24,28},{28,24},{1,5},{5... | collective-permute-start | bytes 1769480 | tf_op jit(solution)/shard_map/ppermute | solution.py:497
  73.2 23.3 %collective-permute-start.22 = (bf16[240,1536]{1,0:T(8,128)(2,1)}, bf16[240,1536]{1,0:T(8,128)(2,1)}, u32[]{:S(2)}, u32[]{:S(2)}) collective-permute-start(bf16[240,1536]{1,0:T(8,128)(2,1)} %project_half.2.refs_2_), channel_id=1, source_target_pairs={{0,2},{1,3},{2,0},{3,1},{4,6},{5,7},{6,4},{7,5},{8,10},{9,11},{10,... | collective-permute-start | bytes 2211848 | tf_op jit(solution)/shard_map/ppermute | solution.py:614
  77.2 13.7 %collective-permute-start.19 = (bf16[192,768]{1,0:T(8,128)(2,1)}, bf16[192,768]{1,0:T(8,128)(2,1)}, u32[]{:S(2)}, u32[]{:S(2)}) collective-permute-start(bf16[192,768]{1,0:T(8,128)(2,1)} %add.2.refs_4_.refs_1_), channel_id=1, source_target_pairs={{0,8},{4,12},{8,16},{12,20},{16,24},{20,28},{24,0},{28,4},{1,9},{5... | collective-permute-start | bytes 884744 | tf_op jit(solution)/shard_map/ppermute | solution.py:491
  77.3 31.3 %collective-permute-start.25 = (bf16[192,768]{1,0:T(8,128)(2,1)}, bf16[192,768]{1,0:T(8,128)(2,1)}, u32[]{:S(2)}, u32[]{:S(2)}) collective-permute-start(bf16[192,768]{1,0:T(8,128)(2,1)} %relay.5), channel_id=1, source_target_pairs={{0,4},{4,0},{8,12},{12,8},{16,20},{20,16},{24,28},{28,24},{1,5},{5... | collective-permute-start | bytes 884744 | tf_op jit(solution)/shard_map/ppermute | solution.py:497
  88.3 13.3 %collective-permute-start.23 = (bf16[120,3072]{1,0:T(8,128)(2,1)S(1)}, bf16[120,3072]{1,0:T(8,128)(2,1)S(1)}, u32[]{:S(2)}, u32[]{:S(2)}) collective-permute-start(bf16[120,3072]{1,0:T(8,128)(2,1)S(1)} %get-tuple-element.46), channel_id=1, source_target_pairs={{1,2},{2,1},{5,6},{6,5},{9,10},{10,9},{13,14},{14,13},{17,18},{18,... | collective-permute-start | bytes 2211848 | tf_op jit(solution)/shard_map/ppermute | solution.py:610
  89.2 12.4 %collective-permute-start.24 = (bf16[120,3072]{1,0:T(8,128)(2,1)S(1)}, bf16[120,3072]{1,0:T(8,128)(2,1)S(1)}, u32[]{:S(2)}, u32[]{:S(2)}) collective-permute-start(bf16[120,3072]{1,0:T(8,128)(2,1)S(1)} %get-tuple-element.47), channel_id=1, source_target_pairs={{0,1},{1,0},{2,3},{3,2},{4,5},{5,4},{6,7},{7,6},{8,9},{9,8},{10,11... | collective-permute-start | bytes 2211848 | tf_op jit(solution)/shard_map/ppermute | solution.py:618
  92.2 17.5 %collective-permute-start.27 = (bf16[192,768]{1,0:T(8,128)(2,1)S(1)}, bf16[192,768]{1,0:T(8,128)(2,1)S(1)}, u32[]{:S(2)}, u32[]{:S(2)}) collective-permute-start(bf16[192,768]{1,0:T(8,128)(2,1)S(1)} %get-tuple-element.44.refs_7_), channel_id=1, source_target_pairs={{0,8},{4,12},{8,16},{12,20},{16,24},{20,28},{24,0},{28,4},{1,9},{5... | collective-permute-start | bytes 884744 | tf_op jit(solution)/shard_map/ppermute | solution.py:491
  96.6 13.2 %collective-permute-start.26 = (bf16[192,768]{1,0:T(8,128)(2,1)S(1)}, bf16[192,768]{1,0:T(8,128)(2,1)S(1)}, u32[]{:S(2)}, u32[]{:S(2)}) collective-permute-start(bf16[192,768]{1,0:T(8,128)(2,1)S(1)} %get-tuple-element.52), channel_id=1, source_target_pairs={{0,24},{4,28},{8,0},{12,4},{16,8},{20,12},{24,16},{28,20},{1,25},{... | collective-permute-start | bytes 884744 | tf_op jit(solution)/shard_map/ppermute | solution.py:491
  (46 other events, 277.9 us)

commit v4 on v3

--- a/solution.py
+++ b/solution.py
@@ -392,7 +392,7 @@
     for i, shift in enumerate((*NEAR, FAR)):
         own, recv = (own_near, recv_near) if i < 3 else (own_far, recv_far)
         at = pl.ds(i * width if i < 3 else 0, width)
-        total = own[:, at] + recv[:, at].astype(F32)
+        total = own[:, at].astype(F32) + recv[:, at].astype(F32)
         out_ref[:, columns(block_at(shift) * width, width)] = total.astype(BF16)
 
 
@@ -410,29 +410,30 @@
 
 
 def project_kernel(
-    a_ref, near_own, near_other, own0, own1, other0, other1, out_ref, far_own, far_other
+    a_own, a_par, near_own, near_other, own0, own1, other0, other1, mine, theirs, far_own, far_other
 ):
     y, core = place()
     rows, width = far_own.shape
     lay((own0, own1), far_own)
     lay((other0, other1), far_other)
     for quarter, near, far in ((core, near_own, far_own), (1 - core, near_other, far_other)):
-        total = dot_nn(a_ref[:, columns(block_at(FAR) * rows, rows)], far[...])
-        for i, shift in enumerate(NEAR):
-            a = a_ref[:, columns(block_at(shift) * rows, rows)]
-            total += dot_nn(a, near[i * rows : (i + 1) * rows])
-        out_ref[:, columns(quarter * width, width)] = total.astype(BF16)
-
-
-def project_half(att, near, far, after):
-    rows = att.shape[0]
+        for a_ref, out_ref in ((a_par, theirs), (a_own, mine)):
+            total = dot_nn(a_ref[:, columns(block_at(FAR) * rows, rows)], far[...])
+            for i, shift in enumerate(NEAR):
+                a = a_ref[:, columns(block_at(shift) * rows, rows)]
+                total += dot_nn(a, near[i * rows : (i + 1) * rows])
+            out_ref[:, columns(quarter * width, width)] = total.astype(BF16)
+
+
+def project_half(att, att_partner, near, far, after):
+    rows, feats = att.shape
     feats, width = 2 * far[0].shape[0], far[0].shape[1]
     return run(
         project_kernel,
-        (att, *near, *far),
-        [whole()] * 7,
-        whole(),
-        shape((rows, 2 * width)),
+        (att, att_partner, *near, *far),
+        [whole()] * 8,
+        [whole()] * 2,
+        [shape((rows, 2 * width))] * 2,
         "project_half",
         after,
         scratch_shapes=[pltpu.VMEM((feats, width), BF16)] * 2,
@@ -513,12 +514,12 @@
     acc += dot_tn(a_sib[...], c_sib[...])
     acc += dot_tn(a_sibpar[...], c_sibpar[...])
     total[...] = acc
-    keeps, sends = outs[:3], outs[3:]
+    keep, *sends = outs
+    keep[...] = total[rows_at(x * half, half), :].astype(BF16)
     for at, (part, row) in enumerate(((0, 0), (1, 0), (1, half), (2, 0))):
 
         @pl.when(step == at)
         def _():
-            keeps[part][row : row + half] = total[rows_at(x * half, half), :]
             sends[part][row : row + half] = total[rows_at((1 - x) * half, half), :].astype(BF16)
 
 
@@ -544,8 +545,9 @@
         weight_grad_kernel,
         (a_own, a_par, a_sib, a_sibpar, cot, cot_par, c_sib, c_sib),
         [a_spec] * 4 + c_specs,
-        [pl.BlockSpec(d, lambda g: (0, 0)) for d in dims * 2],
-        [shape(d, F32) for d in dims] + [shape(d) for d in dims],
+        [pl.BlockSpec((part // 2, width), lambda g: (g, 0))]
+        + [pl.BlockSpec(d, lambda g: (0, 0)) for d in dims],
+        [shape((2 * part, width))] + [shape(d) for d in dims],
         "weight_grad_parts",
         after,
         (4,),
@@ -564,7 +566,16 @@
         total += dot_tn(a_sib, c_sib[:tokens]) + dot_tn(a_sibpar, c_sib[tokens:])
         return lax.psum_scatter(total, "dp", scatter_dimension=0, tiled=True)
     parts = weight_grad_parts(operands, after)
-    return (parts[0], across_x(parts[3])), (parts[1], across_x(parts[4])), (parts[2], parts[5])
+    return parts[0], across_x(parts[1]), across_x(parts[2]), parts[3]
+
+
+def kept(keep, slot):
+    rows, width = keep.shape
+    return pl.BlockSpec((rows // 4, width), lambda g: (slot, 0))
+
+
+def one_step(block):
+    return pl.BlockSpec(block.shape, lambda g: (0, 0))
 
 
 def add_kernel(*refs):
@@ -575,34 +586,36 @@
     out[...] = total.astype(out.dtype)
 
 
-def add(terms, dtype, after=()):
+def add(first, spec, terms, dtype, after=()):
     return run(
         add_kernel,
-        terms,
-        [whole()] * len(terms),
-        whole(),
+        (first, *terms),
+        [spec] + [one_step(term) for term in terms],
+        one_step(terms[0]),
         shape(terms[0].shape, dtype),
         "add",
         after,
-    )
-
-
-def middle_sums_kernel(keep, recv, from_two, one, three):
+        (1,),
+    )
+
+
+def middle_sums_kernel(keep_one, keep_three, recv, from_two, one, three):
     half = one.shape[0]
-    one[...] = (keep[:half] + recv[:half].astype(F32) + from_two[...].astype(F32)).astype(BF16)
-    three[...] = (keep[half:] + recv[half:].astype(F32)).astype(BF16)
+    total = keep_one[...].astype(F32) + recv[:half].astype(F32) + from_two[...].astype(F32)
+    one[...] = total.astype(BF16)
+    three[...] = (keep_three[...].astype(F32) + recv[half:].astype(F32)).astype(BF16)
 
 
 def middle_sums(keep, recv, from_two, after):
-    dims = (keep.shape[0] // 2, keep.shape[1])
     return run(
         middle_sums_kernel,
-        (keep, recv, from_two),
-        [whole()] * 3,
-        [whole()] * 2,
-        [shape(dims)] * 2,
+        (keep, keep, recv, from_two),
+        [kept(keep, 1), kept(keep, 2), one_step(recv), one_step(from_two)],
+        [one_step(from_two)] * 2,
+        [shape(from_two.shape)] * 2,
         "middle_sums",
         after,
+        (1,),
     )
 
 
@@ -653,33 +666,35 @@
 
     att_partner = relay(att_partner, (send_far,))
     att_core_partner = to_core(att_partner)
-    mine_near = grad_attention_near(cot, near, F32, True, (send_far,))
+    mine_near = grad_attention_near(cot, near, BF16, True, (send_far,))
     parts = weight_grad_sum(
         (att, att_partner, att_core, att_core_partner, cot, cot_partner, cot_core), (mine_near,)
     )
     grid = is_grid()
     mine_far = grad_attention_far(
-        cot, far, F32, True, (mine_near, parts[2][0]) if grid else (mine_near,)
-    )
-    proj_partner = project_half(att_partner, near, far, (mine_far,))
+        cot, far, BF16, True, (mine_near, parts[0]) if grid else (mine_near,)
+    )
+    proj_own, proj_partner = project_half(att, att_partner, near, far, (mine_far,))
     proj_recv = to_partner(proj_partner)
     if grid:
-        far_sum = add(parts[0], BF16, (proj_partner,))
+        far_sum = add(parts[0], kept(parts[0], 0), (parts[1],), BF16, (proj_partner,))
         from_two = along_z(far_sum, 1)
-        recv = across_x(relay(parts[2][1], (far_sum,)))
+        recv = across_x(relay(parts[3], (far_sum,)))
 
     ga = merge(mine_near, mine_far, recv_near, recv_far, (far_sum,) if grid else ())
     ds_halo, back_chip, back_core = halo_backward(ga, att, q, halo_chip, halo_core, probs_halo)
     from_chip, from_core = between_chips(back_chip), to_core(back_core)
     if grid:
-        one, three = middle_sums(*parts[1], from_two, (ds_halo,))
+        one, three = middle_sums(parts[0], parts[2], from_two, (ds_halo,))
         from_one, from_three = along_z(one, 1), along_z(three, 3)
-    proj_own = project_half(att, near, far, (one,) if grid else (proj_partner,))
     dq, dk, dv = main_backward(
-        ga, att, q, k, v, halo_chip, halo_core, probs, ds_halo, from_chip, from_core, (proj_own,)
+        ga, att, q, k, v, halo_chip, halo_core, probs, ds_halo, from_chip, from_core, (one,) if grid else ()
     )
     projected = join_halves(proj_own, proj_recv)
-    weight_grad = add((parts[2][0], recv, from_three, from_one), F32, (dq,)) if grid else parts
+    weight_grad = parts
+    if grid:
+        near_sum = add(parts[0], kept(parts[0], 3), (recv, from_three), F32, (dq,))
+        weight_grad = add(near_sum, one_step(near_sum), (from_one,), F32)
     return projected[None], dq[None], dk[None], dv[None], weight_grad
 
 

time: 113 us -> 111 us (0.982); the launches traced: 113 us -> 110 us
  Pallas kernels: 53.6 us -> 51.6 us
    ppermute x7, waiting for transfers between devices: 7.41 us -> 3.35 us  [across_x(): return lax.ppermute(block, 'dp', [(i, i ^ 1) for i in range(8)])]
    ppermute x5, waiting for transfers between devices: 0.01 us -> 2.58 us  [to_partner(): return lax.ppermute(block, 'tile', [(0, 2), (1, 3), (2, 0), (3, 1)])]
    pallas_call x18, Pallas kernels: 53.6 us -> 51.6 us  [run(): pl.pallas_call(body, grid=grid, in_specs=list(in_specs) + [anywhere()] *...]
    ppermute x6, waiting for transfers between devices: 13.7 us -> 15.5 us  [along_z(): lax.ppermute(block, 'dp', [(2 * z + x, 2 * ((z + shift) % 4) + x) for z i...]
    ppermute x5, starting transfers between devices: 2.73 us -> 4.37 us  [to_partner(): return lax.ppermute(block, 'tile', [(0, 2), (1, 3), (2, 0), (3, 1)])]
    unnamed x84 -> x80, local copies, waits for them, and re-layouts: 7.54 us -> 6.77 us
where the time goes in v4:
time: 111 us; the launch traced here: 110 us
  Pallas kernels  51.6 us (46%)
  starting transfers between devices  28.8 us (26%)
  waiting for transfers between devices  21.4 us (19%)
  local copies, waits for them, and re-layouts  6.77 us (6%)
    pallas_call x18, Pallas kernels, run(): pl.pallas_call(body, grid=grid, in_specs=list(in_specs) + [anywhere()] *...  51.6 us
    ppermute x6, waiting for transfers between devices, along_z(): lax.ppermute(block, 'dp', [(2 * z + x, 2 * ((z + shift) % 4) + x) for z i...  15.5 us
    ppermute x6, starting transfers between devices, along_z(): lax.ppermute(block, 'dp', [(2 * z + x, 2 * ((z + shift) % 4) + x) for z i...  8.66 us
    ppermute x7, starting transfers between devices, across_x(): return lax.ppermute(block, 'dp', [(i, i ^ 1) for i in range(8)])  7.81 us
    unnamed x80, local copies, waits for them, and re-layouts  6.77 us
    ppermute x8, starting transfers between devices, to_core(): return lax.ppermute(block, 'tile', [(0, 1), (1, 0), (2, 3), (3, 2)])  6.5 us
    ppermute x5, starting transfers between devices, to_partner(): return lax.ppermute(block, 'tile', [(0, 2), (1, 3), (2, 0), (3, 1)])  4.37 us
    ppermute x7, waiting for transfers between devices, across_x(): return lax.ppermute(block, 'dp', [(i, i ^ 1) for i in range(8)])  3.35 us
  transfers between devices with their start and end apart: 28, of which 7 were waited for; matrix products, arithmetic and copies ran while one was open for 0% of the time, Pallas kernels for 43%

profile of v4, /device:TPU:0, one launch (start us, length us, event | category | flops | bytes accessed | tf_op | source)
XLA Modules:
  0.0 109.6 jit_solution(11360719920349402703)
XLA Ops:
  0.7 3.5 %first_sends.1 = (bf16[120,3072]{1,0:T(8,128)(2,1)}, bf16[120,3072]{1,0:T(8,128)(2,1)}, bf16[192,768]{1,0:T(8,128)(2,1)}, bf16[240,1536]{1,0:T(8,128)(2,1)}) custom-call(bf16[240,1536]{1,0:T(8,128)(2,1)} %bitcast.16, bf16[240,1536]{1,0:T(8,128)(2,1)} %bitcast.19, bf16[192,768]{1,0:T(8,128)(2,1)} %refs_2_.1, bf16[240,3072]{1,0:T(8,128)(2,1)} %bitcast.8), custom_call_target="tpu_custom_call" | custom-call | flops 30000001024 | bytes 10000000000 | tf_op jit(solution)/shard_map/first_sends/pallas_call | solution.py:62
  4.8 4.3 %collective-permute-start.1 = (bf16[120,3072]{1,0:T(8,128)(2,1)}, bf16[120,3072]{1,0:T(8,128)(2,1)S(1)}, u32[]{:S(2)}, u32[]{:S(2)}) collective-permute-start(bf16[120,3072]{1,0:T(8,128)(2,1)} %get-tuple-element.30), channel_id=1, source_target_pairs={{0,1},{1,0},{2,3},{3,2},{4,5},{5,4},{6,7},{7,6},{8,9},{9,8},{10,11... | collective-permute-start | bytes 2211848 | tf_op jit(solution)/shard_map/ppermute | solution.py:631
  9.2 3.6 %collective-permute-start.3 = (bf16[192,768]{1,0:T(8,128)(2,1)}, bf16[192,768]{1,0:T(8,128)(2,1)S(1)}, u32[]{:S(2)}, u32[]{:S(2)}) collective-permute-start(bf16[192,768]{1,0:T(8,128)(2,1)} %get-tuple-element.31.refs_0_), channel_id=1, source_target_pairs={{0,24},{4,28},{8,0},{12,4},{16,8},{20,12},{24,16},{28,20},{1,25},{... | collective-permute-start | bytes 884744 | tf_op jit(solution)/shard_map/ppermute | solution.py:492
  12.8 1.5 %collective-permute-start.8 = (bf16[192,768]{1,0:T(8,128)(2,1)}, bf16[192,768]{1,0:T(8,128)(2,1)}, u32[]{:S(2)}, u32[]{:S(2)}) collective-permute-start(bf16[192,768]{1,0:T(8,128)(2,1)} %get-tuple-element.31.refs_0_), channel_id=1, source_target_pairs={{0,4},{4,0},{8,12},{12,8},{16,20},{20,16},{24,28},{28,24},{1,5},{5... | collective-permute-start | bytes 884744 | tf_op jit(solution)/shard_map/ppermute | solution.py:498
  14.3 6.2 %collective-permute-done.3.refs_8_.refs_4_ = bf16[192,768]{1,0:T(8,128)(2,1)S(1)} collective-permute-done((bf16[192,768]{1,0:T(8,128)(2,1)}, bf16[192,768]{1,0:T(8,128)(2,1)S(1)}, u32[]{:S(2)}, u32[]{:S(2)}) %collective-permute-start.3) | collective-permute-done | bytes 294944 | tf_op jit(solution)/shard_map/ppermute | solution.py:492
  20.5 6.2 %collective-permute-done.2.refs_7_.refs_2_ = bf16[192,768]{1,0:T(8,128)(2,1)S(1)} collective-permute-done((bf16[192,768]{1,0:T(8,128)(2,1)}, bf16[192,768]{1,0:T(8,128)(2,1)S(1)}, u32[]{:S(2)}, u32[]{:S(2)}) %collective-permute-start.2) | collective-permute-done | bytes 294944 | tf_op jit(solution)/shard_map/ppermute | solution.py:492
  26.7 1.5 %collective-permute-start.9 = (bf16[192,768]{1,0:T(8,128)(2,1)S(1)}, bf16[192,768]{1,0:T(8,128)(2,1)}, u32[]{:S(2)}, u32[]{:S(2)}) collective-permute-start(bf16[192,768]{1,0:T(8,128)(2,1)S(1)} %collective-permute-done.2.refs_7_.refs_2_), channel_id=1, source_target_pairs={{0,4},{4,0},{8,12},{12,8},{16,20},{20,16},{24,28},{28,24},{1,5},{5... | collective-permute-start | bytes 884744 | tf_op jit(solution)/shard_map/ppermute | solution.py:498
  28.2 1.6 %collective-permute-start.6 = (bf16[192,768]{1,0:T(8,128)(2,1)S(1)}, bf16[192,768]{1,0:T(8,128)(2,1)S(1)}, u32[]{:S(2)}, u32[]{:S(2)}) collective-permute-start(bf16[192,768]{1,0:T(8,128)(2,1)S(1)} %collective-permute-done.2.refs_7_.refs_2_), channel_id=1, source_target_pairs={{0,8},{4,12},{8,16},{12,20},{16,24},{20,28},{24,0},{28,4},{1,9},{5... | collective-permute-start | bytes 884744 | tf_op jit(solution)/shard_map/ppermute | solution.py:492
  30.4 7.2 %attention_forward.1 = (bf16[240,1536]{1,0:T(8,128)(2,1)}, bf16[12,240,240]{2,1,0:T(8,128)(2,1)}, bf16[12,240,120]{2,1,0:T(8,128)(2,1)}) custom-call(bf16[240,1536]{1,0:T(8,128)(2,1)S(1)} %bitcast.13, bf16[240,1536]{1,0:T(8,128)(2,1)S(1)} %bitcast.17, bf16[240,1536]{1,0:T(8,128)(2,1)S(1)} %bitcast.20, ...), custom_call_target="tpu_custom_call" | custom-call | flops 30000001024 | bytes 10000000000 | tf_op jit(solution)/shard_map/attention_forward/pallas_call | solution.py:62
  40.3 1.7 %collective-permute-done.10.refs_5_ = bf16[192,768]{1,0:T(8,128)(2,1)} collective-permute-done((bf16[192,768]{1,0:T(8,128)(2,1)S(1)}, bf16[192,768]{1,0:T(8,128)(2,1)}, u32[]{:S(2)}, u32[]{:S(2)}) %collective-permute-start.10) | collective-permute-done | bytes 294944 | tf_op jit(solution)/shard_map/ppermute | solution.py:498
  45.3 2.4 %core_sends.1 = (bf16[480,768]{1,0:T(8,128)(2,1)}, bf16[240,1536]{1,0:T(8,128)(2,1)}, bf16[192,768]{1,0:T(8,128)(2,1)S(1)}) custom-call(bf16[240,3072]{1,0:T(8,128)(2,1)S(1)} %bitcast.9, bf16[240,1536]{1,0:T(8,128)(2,1)S(1)} %copy-done.13, bf16[240,1536]{1,0:T(8,128)(2,1)} %get-tuple-element.32.refs_1_.refs_6_.refs_2_.refs_0_, ...), custom_call_target="tpu_custom_call" | custom-call | flops 30000001024 | bytes 10000000000 | tf_op jit(solution)/shard_map/core_sends/pallas_call | solution.py:62
  48.7 2.0 %grad_attention_near.2.refs_5_ = bf16[240,1152]{1,0:T(8,128)(2,1)} custom-call(bf16[240,1536]{1,0:T(8,128)(2,1)S(1)} %copy-done.14, bf16[1152,768]{1,0:T(8,128)(2,1)S(1)} %assemble_weight.1.refs_4_.refs_1_.refs_2_, bf16[1152,768]{1,0:T(8,128)(2,1)S(1)} %collective-permute-done.13.refs_2_.refs_3_, bf16[480,768]{1,0:T(8,128)(2,1)} %get-tuple-element.35.refs_3_), custom_call_target="tpu_custom_call" | custom-call | flops 30000001024 | bytes 10000000000 | tf_op jit(solution)/shard_map/grad_attention_near/pallas_call | solution.py:62
  52.7 1.4 %collective-permute-start.19 = (bf16[240,384]{1,0:T(8,128)(2,1)}, bf16[240,384]{1,0:T(8,128)(2,1)}, u32[]{:S(2)}, u32[]{:S(2)}) collective-permute-start(bf16[240,384]{1,0:T(8,128)(2,1)} %grad_attention_far.2.refs_1_.refs_3_), channel_id=1, source_target_pairs={{0,2},{1,3},{2,0},{3,1},{4,6},{5,7},{6,4},{7,5},{8,10},{9,11},{10,... | collective-permute-start | bytes 552968 | tf_op jit(solution)/shard_map/ppermute | solution.py:627
  54.2 2.6 %collective-permute-done.4.refs_0_ = bf16[240,1536]{1,0:T(8,128)(2,1)} collective-permute-done((bf16[240,1536]{1,0:T(8,128)(2,1)}, bf16[240,1536]{1,0:T(8,128)(2,1)}, u32[]{:S(2)}, u32[]{:S(2)}) %collective-permute-start.4) | collective-permute-done | bytes 737312 | tf_op jit(solution)/shard_map/ppermute | solution.py:627
  59.4 6.8 %weight_grad_parts.1 = (bf16[768,768]{1,0:T(8,128)(2,1)S(1)}, bf16[192,768]{1,0:T(8,128)(2,1)S(1)}, bf16[384,768]{1,0:T(8,128)(2,1)}, bf16[192,768]{1,0:T(8,128)(2,1)S(1)}) custom-call(bf16[240,1536]{1,0:T(8,128)(2,1)} %get-tuple-element.32.refs_1_.refs_6_.refs_2_.refs_0_, bf16[240,1536]{1,0:T(8,128)(2,1)} %relay.4.refs_1_, ...), custom_call_target="tpu_custom_call" | custom-call | flops 30000001024 | bytes 10000000000 | tf_op jit(solution)/shard_map/weight_grad_parts/pallas_call | solution.py:62
  68.9 5.5 %project_half.1 = (bf16[240,1536]{1,0:T(8,128)(2,1)S(1)}, bf16[240,1536]{1,0:T(8,128)(2,1)}) custom-call(bf16[240,1536]{1,0:T(8,128)(2,1)} %get-tuple-element.32.refs_1_.refs_6_.refs_2_.refs_0_, bf16[240,1536]{1,0:T(8,128)(2,1)} %relay.4.refs_1_, bf16[1152,768]{1,0:T(8,128)(2,1)S(1)} %assemble_weight.1.refs_4_.refs_1_.refs_2_, ...), custom_call_target="tpu_custom_call" | custom-call | flops 30000001024 | bytes 10000000000 | tf_op jit(solution)/shard_map/project_half/pallas_call | solution.py:62
  74.4 1.6 %collective-permute-start.17 = (bf16[240,1536]{1,0:T(8,128)(2,1)}, bf16[240,1536]{1,0:T(8,128)(2,1)}, u32[]{:S(2)}, u32[]{:S(2)}) collective-permute-start(bf16[240,1536]{1,0:T(8,128)(2,1)} %get-tuple-element.39.refs_2_), channel_id=1, source_target_pairs={{0,2},{1,3},{2,0},{3,1},{4,6},{5,7},{6,4},{7,5},{8,10},{9,11},{10,... | collective-permute-start | bytes 2211848 | tf_op jit(solution)/shard_map/ppermute | solution.py:627
  76.9 1.4 %collective-permute-start.25 = (bf16[192,768]{1,0:T(8,128)(2,1)}, bf16[192,768]{1,0:T(8,128)(2,1)}, u32[]{:S(2)}, u32[]{:S(2)}) collective-permute-start(bf16[192,768]{1,0:T(8,128)(2,1)} %relay.5), channel_id=1, source_target_pairs={{0,4},{4,0},{8,12},{12,8},{16,20},{20,16},{24,28},{28,24},{1,5},{5... | collective-permute-start | bytes 884744 | tf_op jit(solution)/shard_map/ppermute | solution.py:498
  80.5 5.9 %halo_backward.1 = (bf16[12,240,120]{2,1,0:T(8,128)(2,1)S(1)}, bf16[120,3072]{1,0:T(8,128)(2,1)S(1)}, bf16[120,3072]{1,0:T(8,128)(2,1)S(1)}) custom-call(bf16[240,1536]{1,0:T(8,128)(2,1)S(1)} %merge.1.refs_0_, bf16[240,1536]{1,0:T(8,128)(2,1)} %get-tuple-element.32.refs_1_.refs_6_.refs_2_.refs_0_, bf16[240,1536]{1,0:T(8,128)(2,1)S(1)} %bitcast.14, ...), custom_call_target="tpu_custom_call" | custom-call | flops 30000001024 | bytes 10000000000 | tf_op jit(solution)/shard_map/halo_backward/pallas_call | solution.py:62
  87.2 1.6 %collective-permute-done.23.refs_2_ = bf16[384,768]{1,0:T(8,128)(2,1)} collective-permute-done((bf16[384,768]{1,0:T(8,128)(2,1)}, bf16[384,768]{1,0:T(8,128)(2,1)}, u32[]{:S(2)}, u32[]{:S(2)}) %collective-permute-start.23) | collective-permute-done | bytes 589856 | tf_op jit(solution)/shard_map/ppermute | solution.py:498
  91.1 3.2 %collective-permute-start.26 = (bf16[192,768]{1,0:T(8,128)(2,1)S(1)}, bf16[192,768]{1,0:T(8,128)(2,1)S(1)}, u32[]{:S(2)}, u32[]{:S(2)}) collective-permute-start(bf16[192,768]{1,0:T(8,128)(2,1)S(1)} %get-tuple-element.52), channel_id=1, source_target_pairs={{0,24},{4,28},{8,0},{12,4},{16,8},{20,12},{24,16},{28,20},{1,25},{... | collective-permute-start | bytes 884744 | tf_op jit(solution)/shard_map/ppermute | solution.py:492
  94.4 2.5 %join_halves.1 = bf16[240,3072]{1,0:T(8,128)(2,1)} custom-call(bf16[240,1536]{1,0:T(8,128)(2,1)S(1)} %copy-done.34, bf16[240,1536]{1,0:T(8,128)(2,1)} %collective-permute-done.17.refs_1_), custom_call_target="tpu_custom_call" | custom-call | flops 30000001024 | bytes 10000000000 | tf_op jit(solution)/shard_map/join_halves/pallas_call | solution.py:62
  96.9 6.9 %main_backward.1 = (bf16[240,1536]{1,0:T(8,128)(2,1)}, bf16[240,1536]{1,0:T(8,128)(2,1)}, bf16[240,1536]{1,0:T(8,128)(2,1)}) custom-call(bf16[240,1536]{1,0:T(8,128)(2,1)S(1)} %merge.1.refs_0_, bf16[240,1536]{1,0:T(8,128)(2,1)} %get-tuple-element.32.refs_1_.refs_6_.refs_2_.refs_0_, bf16[240,1536]{1,0:T(8,128)(2,1)S(1)} %bitcast.15, ...), custom_call_target="tpu_custom_call" | custom-call | flops 30000001024 | bytes 10000000000 | tf_op jit(solution)/shard_map/main_backward/pallas_call | solution.py:62
  106.0 2.8 %collective-permute-done.27.refs_1_ = bf16[192,768]{1,0:T(8,128)(2,1)S(1)} collective-permute-done((bf16[192,768]{1,0:T(8,128)(2,1)S(1)}, bf16[192,768]{1,0:T(8,128)(2,1)S(1)}, u32[]{:S(2)}, u32[]{:S(2)}) %collective-permute-start.27) | collective-permute-done | bytes 294944 | tf_op jit(solution)/shard_map/ppermute | solution.py:492
  (133 shorter events, 24.8 us)
Async XLA Ops:
  4.1 24.1 %collective-permute-start = (bf16[120,3072]{1,0:T(8,128)(2,1)}, bf16[120,3072]{1,0:T(8,128)(2,1)S(1)}, u32[]{:S(2)}, u32[]{:S(2)}) collective-permute-start(bf16[120,3072]{1,0:T(8,128)(2,1)} %get-tuple-element.29), channel_id=1, source_target_pairs={{1,2},{2,1},{5,6},{6,5},{9,10},{10,9},{13,14},{14,13},{17,18},{18,... | collective-permute-start | bytes 2211848 | tf_op jit(solution)/shard_map/ppermute | solution.py:623
  4.8 25.0 %collective-permute-start.1 = (bf16[120,3072]{1,0:T(8,128)(2,1)}, bf16[120,3072]{1,0:T(8,128)(2,1)S(1)}, u32[]{:S(2)}, u32[]{:S(2)}) collective-permute-start(bf16[120,3072]{1,0:T(8,128)(2,1)} %get-tuple-element.30), channel_id=1, source_target_pairs={{0,1},{1,0},{2,3},{3,2},{4,5},{5,4},{6,7},{7,6},{8,9},{9,8},{10,11... | collective-permute-start | bytes 2211848 | tf_op jit(solution)/shard_map/ppermute | solution.py:631
  9.2 11.3 %collective-permute-start.3 = (bf16[192,768]{1,0:T(8,128)(2,1)}, bf16[192,768]{1,0:T(8,128)(2,1)S(1)}, u32[]{:S(2)}, u32[]{:S(2)}) collective-permute-start(bf16[192,768]{1,0:T(8,128)(2,1)} %get-tuple-element.31.refs_0_), channel_id=1, source_target_pairs={{0,24},{4,28},{8,0},{12,4},{16,8},{20,12},{24,16},{28,20},{1,25},{... | collective-permute-start | bytes 884744 | tf_op jit(solution)/shard_map/ppermute | solution.py:492
  12.8 13.9 %collective-permute-start.2 = (bf16[192,768]{1,0:T(8,128)(2,1)}, bf16[192,768]{1,0:T(8,128)(2,1)S(1)}, u32[]{:S(2)}, u32[]{:S(2)}) collective-permute-start(bf16[192,768]{1,0:T(8,128)(2,1)} %get-tuple-element.31.refs_0_), channel_id=1, source_target_pairs={{0,8},{4,12},{8,16},{12,20},{16,24},{20,28},{24,0},{28,4},{1,9},{5... | collective-permute-start | bytes 884744 | tf_op jit(solution)/shard_map/ppermute | solution.py:492
  12.8 26.6 %collective-permute-start.8 = (bf16[192,768]{1,0:T(8,128)(2,1)}, bf16[192,768]{1,0:T(8,128)(2,1)}, u32[]{:S(2)}, u32[]{:S(2)}) collective-permute-start(bf16[192,768]{1,0:T(8,128)(2,1)} %get-tuple-element.31.refs_0_), channel_id=1, source_target_pairs={{0,4},{4,0},{8,12},{12,8},{16,20},{20,16},{24,28},{28,24},{1,5},{5... | collective-permute-start | bytes 884744 | tf_op jit(solution)/shard_map/ppermute | solution.py:498
  20.5 21.4 %collective-permute-start.5 = (bf16[240,1536]{1,0:T(8,128)(2,1)}, bf16[240,1536]{1,0:T(8,128)(2,1)S(1)}, u32[]{:S(2)}, u32[]{:S(2)}) collective-permute-start(bf16[240,1536]{1,0:T(8,128)(2,1)} %get-tuple-element.33), channel_id=1, source_target_pairs={{0,2},{1,3},{2,0},{3,1},{4,6},{5,7},{6,4},{7,5},{8,10},{9,11},{10,... | collective-permute-start | bytes 2211848 | tf_op jit(solution)/shard_map/ppermute | solution.py:627
  26.7 15.2 %collective-permute-start.9 = (bf16[192,768]{1,0:T(8,128)(2,1)S(1)}, bf16[192,768]{1,0:T(8,128)(2,1)}, u32[]{:S(2)}, u32[]{:S(2)}) collective-permute-start(bf16[192,768]{1,0:T(8,128)(2,1)S(1)} %collective-permute-done.2.refs_7_.refs_2_), channel_id=1, source_target_pairs={{0,4},{4,0},{8,12},{12,8},{16,20},{20,16},{24,28},{28,24},{1,5},{5... | collective-permute-start | bytes 884744 | tf_op jit(solution)/shard_map/ppermute | solution.py:498
  28.2 9.7 %collective-permute-start.6 = (bf16[192,768]{1,0:T(8,128)(2,1)S(1)}, bf16[192,768]{1,0:T(8,128)(2,1)S(1)}, u32[]{:S(2)}, u32[]{:S(2)}) collective-permute-start(bf16[192,768]{1,0:T(8,128)(2,1)S(1)} %collective-permute-done.2.refs_7_.refs_2_), channel_id=1, source_target_pairs={{0,8},{4,12},{8,16},{12,20},{16,24},{20,28},{24,0},{28,4},{1,9},{5... | collective-permute-start | bytes 884744 | tf_op jit(solution)/shard_map/ppermute | solution.py:492
  29.8 12.1 %collective-permute-start.10 = (bf16[192,768]{1,0:T(8,128)(2,1)S(1)}, bf16[192,768]{1,0:T(8,128)(2,1)}, u32[]{:S(2)}, u32[]{:S(2)}) collective-permute-start(bf16[192,768]{1,0:T(8,128)(2,1)S(1)} %collective-permute-done.3.refs_8_.refs_4_), channel_id=1, source_target_pairs={{0,4},{4,0},{8,12},{12,8},{16,20},{20,16},{24,28},{28,24},{1,5},{5... | collective-permute-start | bytes 884744 | tf_op jit(solution)/shard_map/ppermute | solution.py:498
  38.6 18.1 %collective-permute-start.4 = (bf16[240,1536]{1,0:T(8,128)(2,1)}, bf16[240,1536]{1,0:T(8,128)(2,1)}, u32[]{:S(2)}, u32[]{:S(2)}) collective-permute-start(bf16[240,1536]{1,0:T(8,128)(2,1)} %get-tuple-element.32.refs_1_.refs_6_.refs_2_.refs_0_), channel_id=1, source_target_pairs={{0,2},{1,3},{2,0},{3,1},{4,6},{5,7},{6,4},{7,5},{8,10},{9,11},{10,... | collective-permute-start | bytes 2211848 | tf_op jit(solution)/shard_map/ppermute | solution.py:627
  39.4 8.8 %collective-permute-start.7 = (bf16[192,768]{1,0:T(8,128)(2,1)}, bf16[192,768]{1,0:T(8,128)(2,1)S(1)}, u32[]{:S(2)}, u32[]{:S(2)}) collective-permute-start(bf16[192,768]{1,0:T(8,128)(2,1)} %relay.3.refs_3_.refs_1_.refs_4_), channel_id=1, source_target_pairs={{0,4},{4,0},{8,12},{12,8},{16,20},{20,16},{24,28},{28,24},{1,5},{5... | collective-permute-start | bytes 884744 | tf_op jit(solution)/shard_map/ppermute | solution.py:498
  48.1 11.2 %collective-permute-start.14 = (bf16[240,1536]{1,0:T(8,128)(2,1)}, bf16[240,1536]{1,0:T(8,128)(2,1)}, u32[]{:S(2)}, u32[]{:S(2)}) collective-permute-start(bf16[240,1536]{1,0:T(8,128)(2,1)} %get-tuple-element.36), channel_id=1, source_target_pairs={{0,1},{1,0},{2,3},{3,2},{4,5},{5,4},{6,7},{7,6},{8,9},{9,8},{10,11... | collective-permute-start | bytes 2211848 | tf_op jit(solution)/shard_map/ppermute | solution.py:631
  48.2 11.2 %collective-permute-start.16 = (bf16[480,768]{1,0:T(8,128)(2,1)}, bf16[480,768]{1,0:T(8,128)(2,1)}, u32[]{:S(2)}, u32[]{:S(2)}) collective-permute-start(bf16[480,768]{1,0:T(8,128)(2,1)} %get-tuple-element.35.refs_3_), channel_id=1, source_target_pairs={{0,1},{1,0},{2,3},{3,2},{4,5},{5,4},{6,7},{7,6},{8,9},{9,8},{10,11... | collective-permute-start | bytes 2211848 | tf_op jit(solution)/shard_map/ppermute | solution.py:631
  50.8 27.5 %collective-permute-start.18 = (bf16[240,1152]{1,0:T(8,128)(2,1)}, bf16[240,1152]{1,0:T(8,128)(2,1)}, u32[]{:S(2)}, u32[]{:S(2)}) collective-permute-start(bf16[240,1152]{1,0:T(8,128)(2,1)} %grad_attention_near.2.refs_5_), channel_id=1, source_target_pairs={{0,2},{1,3},{2,0},{3,1},{4,6},{5,7},{6,4},{7,5},{8,10},{9,11},{10,... | collective-permute-start | bytes 1658888 | tf_op jit(solution)/shard_map/ppermute | solution.py:627
  52.7 24.1 %collective-permute-start.19 = (bf16[240,384]{1,0:T(8,128)(2,1)}, bf16[240,384]{1,0:T(8,128)(2,1)}, u32[]{:S(2)}, u32[]{:S(2)}) collective-permute-start(bf16[240,384]{1,0:T(8,128)(2,1)} %grad_attention_far.2.refs_1_.refs_3_), channel_id=1, source_target_pairs={{0,2},{1,3},{2,0},{3,1},{4,6},{5,7},{6,4},{7,5},{8,10},{9,11},{10,... | collective-permute-start | bytes 552968 | tf_op jit(solution)/shard_map/ppermute | solution.py:627
  66.2 9.8 %collective-permute-start.20 = (bf16[192,768]{1,0:T(8,128)(2,1)S(1)}, bf16[192,768]{1,0:T(8,128)(2,1)S(1)}, u32[]{:S(2)}, u32[]{:S(2)}) collective-permute-start(bf16[192,768]{1,0:T(8,128)(2,1)S(1)} %get-tuple-element.40), channel_id=1, source_target_pairs={{0,4},{4,0},{8,12},{12,8},{16,20},{20,16},{24,28},{28,24},{1,5},{5... | collective-permute-start | bytes 884744 | tf_op jit(solution)/shard_map/ppermute | solution.py:498
  67.5 21.2 %collective-permute-start.23 = (bf16[384,768]{1,0:T(8,128)(2,1)}, bf16[384,768]{1,0:T(8,128)(2,1)}, u32[]{:S(2)}, u32[]{:S(2)}) collective-permute-start(bf16[384,768]{1,0:T(8,128)(2,1)} %get-tuple-element.46), channel_id=1, source_target_pairs={{0,4},{4,0},{8,12},{12,8},{16,20},{20,16},{24,28},{28,24},{1,5},{5... | collective-permute-start | bytes 1769480 | tf_op jit(solution)/shard_map/ppermute | solution.py:498
  74.4 20.0 %collective-permute-start.17 = (bf16[240,1536]{1,0:T(8,128)(2,1)}, bf16[240,1536]{1,0:T(8,128)(2,1)}, u32[]{:S(2)}, u32[]{:S(2)}) collective-permute-start(bf16[240,1536]{1,0:T(8,128)(2,1)} %get-tuple-element.39.refs_2_), channel_id=1, source_target_pairs={{0,2},{1,3},{2,0},{3,1},{4,6},{5,7},{6,4},{7,5},{8,10},{9,11},{10,... | collective-permute-start | bytes 2211848 | tf_op jit(solution)/shard_map/ppermute | solution.py:627
  76.1 13.7 %collective-permute-start.24 = (bf16[192,768]{1,0:T(8,128)(2,1)S(1)}, bf16[192,768]{1,0:T(8,128)(2,1)S(1)}, u32[]{:S(2)}, u32[]{:S(2)}) collective-permute-start(bf16[192,768]{1,0:T(8,128)(2,1)S(1)} %add.3.refs_4_.refs_1_), channel_id=1, source_target_pairs={{0,8},{4,12},{8,16},{12,20},{16,24},{20,28},{24,0},{28,4},{1,9},{5... | collective-permute-start | bytes 884744 | tf_op jit(solution)/shard_map/ppermute | solution.py:492
  76.9 26.9 %collective-permute-start.25 = (bf16[192,768]{1,0:T(8,128)(2,1)}, bf16[192,768]{1,0:T(8,128)(2,1)}, u32[]{:S(2)}, u32[]{:S(2)}) collective-permute-start(bf16[192,768]{1,0:T(8,128)(2,1)} %relay.5), channel_id=1, source_target_pairs={{0,4},{4,0},{8,12},{12,8},{16,20},{20,16},{24,28},{28,24},{1,5},{5... | collective-permute-start | bytes 884744 | tf_op jit(solution)/shard_map/ppermute | solution.py:498
  86.4 10.4 %collective-permute-start.21 = (bf16[120,3072]{1,0:T(8,128)(2,1)S(1)}, bf16[120,3072]{1,0:T(8,128)(2,1)S(1)}, u32[]{:S(2)}, u32[]{:S(2)}) collective-permute-start(bf16[120,3072]{1,0:T(8,128)(2,1)S(1)} %get-tuple-element.44), channel_id=1, source_target_pairs={{1,2},{2,1},{5,6},{6,5},{9,10},{10,9},{13,14},{14,13},{17,18},{18,... | collective-permute-start | bytes 2211848 | tf_op jit(solution)/shard_map/ppermute | solution.py:623
  88.8 8.1 %collective-permute-start.22 = (bf16[120,3072]{1,0:T(8,128)(2,1)S(1)}, bf16[120,3072]{1,0:T(8,128)(2,1)S(1)}, u32[]{:S(2)}, u32[]{:S(2)}) collective-permute-start(bf16[120,3072]{1,0:T(8,128)(2,1)S(1)} %get-tuple-element.45), channel_id=1, source_target_pairs={{0,1},{1,0},{2,3},{3,2},{4,5},{5,4},{6,7},{7,6},{8,9},{9,8},{10,11... | collective-permute-start | bytes 2211848 | tf_op jit(solution)/shard_map/ppermute | solution.py:631
  91.1 12.6 %collective-permute-start.26 = (bf16[192,768]{1,0:T(8,128)(2,1)S(1)}, bf16[192,768]{1,0:T(8,128)(2,1)S(1)}, u32[]{:S(2)}, u32[]{:S(2)}) collective-permute-start(bf16[192,768]{1,0:T(8,128)(2,1)S(1)} %get-tuple-element.52), channel_id=1, source_target_pairs={{0,24},{4,28},{8,0},{12,4},{16,8},{20,12},{24,16},{28,20},{1,25},{... | collective-permute-start | bytes 884744 | tf_op jit(solution)/shard_map/ppermute | solution.py:492
  94.4 14.4 %collective-permute-start.27 = (bf16[192,768]{1,0:T(8,128)(2,1)S(1)}, bf16[192,768]{1,0:T(8,128)(2,1)S(1)}, u32[]{:S(2)}, u32[]{:S(2)}) collective-permute-start(bf16[192,768]{1,0:T(8,128)(2,1)S(1)} %get-tuple-element.47.refs_13_), channel_id=1, source_target_pairs={{0,8},{4,12},{8,16},{12,20},{16,24},{20,28},{24,0},{28,4},{1,9},{5... | collective-permute-start | bytes 884744 | tf_op jit(solution)/shard_map/ppermute | solution.py:492
  (44 other events, 253.7 us)

commit v5 on v4

--- a/solution.py
+++ b/solution.py
@@ -268,17 +268,16 @@
 def first_sends_kernel(k_ref, v_ref, w_ref, c_ref, chip_ref, core_ref, shard_ref, half_ref, held, sems):
     y, core = place()
     rows, feats = k_ref.shape
-    parts = 4
-    part = feats // parts
+    step = 48
     copies = []
     for i, source in enumerate((k_ref, v_ref)):
-        for j in range(parts):
-            at = pl.ds(j * part, part)
-            copies.append((source.at[:, at], held.at[i, :, at]))
+        for j in range(0, rows, step):
+            at = pl.ds(j, step)
+            copies.append((source.at[at], held.at[i, at]))
     copies.append((w_ref, shard_ref))
-    for j in range(parts):
-        at = columns((1 - y) * feats + j * part, part)
-        copies.append((c_ref.at[:, at], half_ref.at[:, pl.ds(j * part, part)]))
+    for j in range(0, rows, step):
+        at = pl.ds(j, step)
+        copies.append((c_ref.at[at, columns((1 - y) * feats, feats)], half_ref.at[at]))
     copies = [pltpu.make_async_copy(*ends, sems.at[i]) for i, ends in enumerate(copies)]
     for copy in copies:
         copy.start()
@@ -301,7 +300,7 @@
         [shape((TILE, 2 * feats))] * 2 + [shape(w.shape), shape((rows, cot.shape[1] // 2))],
         "first_sends",
         limit=FIRST,
-        scratch_shapes=[pltpu.VMEM((2, rows, feats), BF16), pltpu.SemaphoreType.DMA((13,))],
+        scratch_shapes=[pltpu.VMEM((2, rows, feats), BF16), pltpu.SemaphoreType.DMA((16,))],
     )
 
 

time: 111 us -> 111 us (level)
  transfers between devices with their start and end apart: 28 -> 28, of which waited for: 7 -> 8; matrix products, arithmetic and copies ran while one was open for 0% -> 0% of each run, Pallas kernels for 43% -> 43%
where the time goes in v5:
time: 111 us; the launch traced here: 110 us
  Pallas kernels  51.6 us (46%)
  starting transfers between devices  28.8 us (26%)
  waiting for transfers between devices  21.5 us (19%)
  local copies, waits for them, and re-layouts  6.75 us (6%)
    pallas_call x18, Pallas kernels, run(): pl.pallas_call(body, grid=grid, in_specs=list(in_specs) + [anywhere()] *...  51.6 us
    ppermute x6, waiting for transfers between devices, along_z(): lax.ppermute(block, 'dp', [(2 * z + x, 2 * ((z + shift) % 4) + x) for z i...  15.5 us
    ppermute x6, starting transfers between devices, along_z(): lax.ppermute(block, 'dp', [(2 * z + x, 2 * ((z + shift) % 4) + x) for z i...  8.7 us
    ppermute x7, starting transfers between devices, across_x(): return lax.ppermute(block, 'dp', [(i, i ^ 1) for i in range(8)])  7.81 us
    unnamed x80, local copies, waits for them, and re-layouts  6.75 us
    ppermute x8, starting transfers between devices, to_core(): return lax.ppermute(block, 'tile', [(0, 1), (1, 0), (2, 3), (3, 2)])  6.47 us
    ppermute x5, starting transfers between devices, to_partner(): return lax.ppermute(block, 'tile', [(0, 2), (1, 3), (2, 0), (3, 1)])  4.36 us
    ppermute x7, waiting for transfers between devices, across_x(): return lax.ppermute(block, 'dp', [(i, i ^ 1) for i in range(8)])  3.36 us
  transfers between devices with their start and end apart: 28, of which 8 were waited for; matrix products, arithmetic and copies ran while one was open for 0% of the time, Pallas kernels for 43%

profile of v5, /device:TPU:0, one launch (start us, length us, event | category | flops | bytes accessed | tf_op | source)
XLA Modules:
  0.0 109.6 jit_solution(8547386646242606020)
XLA Ops:
  0.7 3.5 %first_sends.1 = (bf16[120,3072]{1,0:T(8,128)(2,1)}, bf16[120,3072]{1,0:T(8,128)(2,1)}, bf16[192,768]{1,0:T(8,128)(2,1)}, bf16[240,1536]{1,0:T(8,128)(2,1)}) custom-call(bf16[240,1536]{1,0:T(8,128)(2,1)} %bitcast.16, bf16[240,1536]{1,0:T(8,128)(2,1)} %bitcast.19, bf16[192,768]{1,0:T(8,128)(2,1)} %refs_2_.1, bf16[240,3072]{1,0:T(8,128)(2,1)} %bitcast.8), custom_call_target="tpu_custom_call" | custom-call | flops 30000001024 | bytes 10000000000 | tf_op jit(solution)/shard_map/first_sends/pallas_call | solution.py:62
  4.8 4.3 %collective-permute-start.1 = (bf16[120,3072]{1,0:T(8,128)(2,1)}, bf16[120,3072]{1,0:T(8,128)(2,1)S(1)}, u32[]{:S(2)}, u32[]{:S(2)}) collective-permute-start(bf16[120,3072]{1,0:T(8,128)(2,1)} %get-tuple-element.30), channel_id=1, source_target_pairs={{0,1},{1,0},{2,3},{3,2},{4,5},{5,4},{6,7},{7,6},{8,9},{9,8},{10,11... | collective-permute-start | bytes 2211848 | tf_op jit(solution)/shard_map/ppermute | solution.py:630
  9.2 3.6 %collective-permute-start.3 = (bf16[192,768]{1,0:T(8,128)(2,1)}, bf16[192,768]{1,0:T(8,128)(2,1)S(1)}, u32[]{:S(2)}, u32[]{:S(2)}) collective-permute-start(bf16[192,768]{1,0:T(8,128)(2,1)} %get-tuple-element.31.refs_0_), channel_id=1, source_target_pairs={{0,24},{4,28},{8,0},{12,4},{16,8},{20,12},{24,16},{28,20},{1,25},{... | collective-permute-start | bytes 884744 | tf_op jit(solution)/shard_map/ppermute | solution.py:491
  12.8 1.5 %collective-permute-start.8 = (bf16[192,768]{1,0:T(8,128)(2,1)}, bf16[192,768]{1,0:T(8,128)(2,1)}, u32[]{:S(2)}, u32[]{:S(2)}) collective-permute-start(bf16[192,768]{1,0:T(8,128)(2,1)} %get-tuple-element.31.refs_0_), channel_id=1, source_target_pairs={{0,4},{4,0},{8,12},{12,8},{16,20},{20,16},{24,28},{28,24},{1,5},{5... | collective-permute-start | bytes 884744 | tf_op jit(solution)/shard_map/ppermute | solution.py:497
  14.3 6.2 %collective-permute-done.3.refs_8_.refs_4_ = bf16[192,768]{1,0:T(8,128)(2,1)S(1)} collective-permute-done((bf16[192,768]{1,0:T(8,128)(2,1)}, bf16[192,768]{1,0:T(8,128)(2,1)S(1)}, u32[]{:S(2)}, u32[]{:S(2)}) %collective-permute-start.3) | collective-permute-done | bytes 294944 | tf_op jit(solution)/shard_map/ppermute | solution.py:491
  20.5 6.2 %collective-permute-done.2.refs_7_.refs_2_ = bf16[192,768]{1,0:T(8,128)(2,1)S(1)} collective-permute-done((bf16[192,768]{1,0:T(8,128)(2,1)}, bf16[192,768]{1,0:T(8,128)(2,1)S(1)}, u32[]{:S(2)}, u32[]{:S(2)}) %collective-permute-start.2) | collective-permute-done | bytes 294944 | tf_op jit(solution)/shard_map/ppermute | solution.py:491
  26.7 1.5 %collective-permute-start.9 = (bf16[192,768]{1,0:T(8,128)(2,1)S(1)}, bf16[192,768]{1,0:T(8,128)(2,1)}, u32[]{:S(2)}, u32[]{:S(2)}) collective-permute-start(bf16[192,768]{1,0:T(8,128)(2,1)S(1)} %collective-permute-done.2.refs_7_.refs_2_), channel_id=1, source_target_pairs={{0,4},{4,0},{8,12},{12,8},{16,20},{20,16},{24,28},{28,24},{1,5},{5... | collective-permute-start | bytes 884744 | tf_op jit(solution)/shard_map/ppermute | solution.py:497
  28.2 1.6 %collective-permute-start.6 = (bf16[192,768]{1,0:T(8,128)(2,1)S(1)}, bf16[192,768]{1,0:T(8,128)(2,1)S(1)}, u32[]{:S(2)}, u32[]{:S(2)}) collective-permute-start(bf16[192,768]{1,0:T(8,128)(2,1)S(1)} %collective-permute-done.2.refs_7_.refs_2_), channel_id=1, source_target_pairs={{0,8},{4,12},{8,16},{12,20},{16,24},{20,28},{24,0},{28,4},{1,9},{5... | collective-permute-start | bytes 884744 | tf_op jit(solution)/shard_map/ppermute | solution.py:491
  30.4 7.2 %attention_forward.1 = (bf16[240,1536]{1,0:T(8,128)(2,1)}, bf16[12,240,240]{2,1,0:T(8,128)(2,1)}, bf16[12,240,120]{2,1,0:T(8,128)(2,1)}) custom-call(bf16[240,1536]{1,0:T(8,128)(2,1)S(1)} %bitcast.13, bf16[240,1536]{1,0:T(8,128)(2,1)S(1)} %bitcast.17, bf16[240,1536]{1,0:T(8,128)(2,1)S(1)} %bitcast.20, ...), custom_call_target="tpu_custom_call" | custom-call | flops 30000001024 | bytes 10000000000 | tf_op jit(solution)/shard_map/attention_forward/pallas_call | solution.py:62
  40.3 1.7 %collective-permute-done.10.refs_5_ = bf16[192,768]{1,0:T(8,128)(2,1)} collective-permute-done((bf16[192,768]{1,0:T(8,128)(2,1)S(1)}, bf16[192,768]{1,0:T(8,128)(2,1)}, u32[]{:S(2)}, u32[]{:S(2)}) %collective-permute-start.10) | collective-permute-done | bytes 294944 | tf_op jit(solution)/shard_map/ppermute | solution.py:497
  45.3 2.4 %core_sends.1 = (bf16[480,768]{1,0:T(8,128)(2,1)}, bf16[240,1536]{1,0:T(8,128)(2,1)}, bf16[192,768]{1,0:T(8,128)(2,1)S(1)}) custom-call(bf16[240,3072]{1,0:T(8,128)(2,1)S(1)} %bitcast.9, bf16[240,1536]{1,0:T(8,128)(2,1)S(1)} %copy-done.13, bf16[240,1536]{1,0:T(8,128)(2,1)} %get-tuple-element.32.refs_1_.refs_6_.refs_2_.refs_0_, ...), custom_call_target="tpu_custom_call" | custom-call | flops 30000001024 | bytes 10000000000 | tf_op jit(solution)/shard_map/core_sends/pallas_call | solution.py:62
  48.8 2.0 %grad_attention_near.2.refs_5_ = bf16[240,1152]{1,0:T(8,128)(2,1)} custom-call(bf16[240,1536]{1,0:T(8,128)(2,1)S(1)} %copy-done.14, bf16[1152,768]{1,0:T(8,128)(2,1)S(1)} %assemble_weight.1.refs_4_.refs_1_.refs_2_, bf16[1152,768]{1,0:T(8,128)(2,1)S(1)} %collective-permute-done.13.refs_2_.refs_3_, bf16[480,768]{1,0:T(8,128)(2,1)} %get-tuple-element.35.refs_3_), custom_call_target="tpu_custom_call" | custom-call | flops 30000001024 | bytes 10000000000 | tf_op jit(solution)/shard_map/grad_attention_near/pallas_call | solution.py:62
  52.8 1.4 %collective-permute-start.19 = (bf16[240,384]{1,0:T(8,128)(2,1)}, bf16[240,384]{1,0:T(8,128)(2,1)}, u32[]{:S(2)}, u32[]{:S(2)}) collective-permute-start(bf16[240,384]{1,0:T(8,128)(2,1)} %grad_attention_far.2.refs_1_.refs_3_), channel_id=1, source_target_pairs={{0,2},{1,3},{2,0},{3,1},{4,6},{5,7},{6,4},{7,5},{8,10},{9,11},{10,... | collective-permute-start | bytes 552968 | tf_op jit(solution)/shard_map/ppermute | solution.py:626
  54.2 2.6 %collective-permute-done.4.refs_0_ = bf16[240,1536]{1,0:T(8,128)(2,1)} collective-permute-done((bf16[240,1536]{1,0:T(8,128)(2,1)}, bf16[240,1536]{1,0:T(8,128)(2,1)}, u32[]{:S(2)}, u32[]{:S(2)}) %collective-permute-start.4) | collective-permute-done | bytes 737312 | tf_op jit(solution)/shard_map/ppermute | solution.py:626
  59.4 6.8 %weight_grad_parts.1 = (bf16[768,768]{1,0:T(8,128)(2,1)S(1)}, bf16[192,768]{1,0:T(8,128)(2,1)S(1)}, bf16[384,768]{1,0:T(8,128)(2,1)}, bf16[192,768]{1,0:T(8,128)(2,1)S(1)}) custom-call(bf16[240,1536]{1,0:T(8,128)(2,1)} %get-tuple-element.32.refs_1_.refs_6_.refs_2_.refs_0_, bf16[240,1536]{1,0:T(8,128)(2,1)} %relay.4.refs_1_, ...), custom_call_target="tpu_custom_call" | custom-call | flops 30000001024 | bytes 10000000000 | tf_op jit(solution)/shard_map/weight_grad_parts/pallas_call | solution.py:62
  68.9 5.5 %project_half.1 = (bf16[240,1536]{1,0:T(8,128)(2,1)S(1)}, bf16[240,1536]{1,0:T(8,128)(2,1)}) custom-call(bf16[240,1536]{1,0:T(8,128)(2,1)} %get-tuple-element.32.refs_1_.refs_6_.refs_2_.refs_0_, bf16[240,1536]{1,0:T(8,128)(2,1)} %relay.4.refs_1_, bf16[1152,768]{1,0:T(8,128)(2,1)S(1)} %assemble_weight.1.refs_4_.refs_1_.refs_2_, ...), custom_call_target="tpu_custom_call" | custom-call | flops 30000001024 | bytes 10000000000 | tf_op jit(solution)/shard_map/project_half/pallas_call | solution.py:62
  74.4 1.6 %collective-permute-start.17 = (bf16[240,1536]{1,0:T(8,128)(2,1)}, bf16[240,1536]{1,0:T(8,128)(2,1)}, u32[]{:S(2)}, u32[]{:S(2)}) collective-permute-start(bf16[240,1536]{1,0:T(8,128)(2,1)} %get-tuple-element.39.refs_2_), channel_id=1, source_target_pairs={{0,2},{1,3},{2,0},{3,1},{4,6},{5,7},{6,4},{7,5},{8,10},{9,11},{10,... | collective-permute-start | bytes 2211848 | tf_op jit(solution)/shard_map/ppermute | solution.py:626
  76.9 1.4 %collective-permute-start.25 = (bf16[192,768]{1,0:T(8,128)(2,1)}, bf16[192,768]{1,0:T(8,128)(2,1)}, u32[]{:S(2)}, u32[]{:S(2)}) collective-permute-start(bf16[192,768]{1,0:T(8,128)(2,1)} %relay.5), channel_id=1, source_target_pairs={{0,4},{4,0},{8,12},{12,8},{16,20},{20,16},{24,28},{28,24},{1,5},{5... | collective-permute-start | bytes 884744 | tf_op jit(solution)/shard_map/ppermute | solution.py:497
  80.6 5.9 %halo_backward.1 = (bf16[12,240,120]{2,1,0:T(8,128)(2,1)S(1)}, bf16[120,3072]{1,0:T(8,128)(2,1)S(1)}, bf16[120,3072]{1,0:T(8,128)(2,1)S(1)}) custom-call(bf16[240,1536]{1,0:T(8,128)(2,1)S(1)} %merge.1.refs_0_, bf16[240,1536]{1,0:T(8,128)(2,1)} %get-tuple-element.32.refs_1_.refs_6_.refs_2_.refs_0_, bf16[240,1536]{1,0:T(8,128)(2,1)S(1)} %bitcast.14, ...), custom_call_target="tpu_custom_call" | custom-call | flops 30000001024 | bytes 10000000000 | tf_op jit(solution)/shard_map/halo_backward/pallas_call | solution.py:62
  87.2 1.6 %collective-permute-done.23.refs_2_ = bf16[384,768]{1,0:T(8,128)(2,1)} collective-permute-done((bf16[384,768]{1,0:T(8,128)(2,1)}, bf16[384,768]{1,0:T(8,128)(2,1)}, u32[]{:S(2)}, u32[]{:S(2)}) %collective-permute-start.23) | collective-permute-done | bytes 589856 | tf_op jit(solution)/shard_map/ppermute | solution.py:497
  91.1 3.2 %collective-permute-start.26 = (bf16[192,768]{1,0:T(8,128)(2,1)S(1)}, bf16[192,768]{1,0:T(8,128)(2,1)S(1)}, u32[]{:S(2)}, u32[]{:S(2)}) collective-permute-start(bf16[192,768]{1,0:T(8,128)(2,1)S(1)} %get-tuple-element.52), channel_id=1, source_target_pairs={{0,24},{4,28},{8,0},{12,4},{16,8},{20,12},{24,16},{28,20},{1,25},{... | collective-permute-start | bytes 884744 | tf_op jit(solution)/shard_map/ppermute | solution.py:491
  94.4 2.5 %join_halves.1 = bf16[240,3072]{1,0:T(8,128)(2,1)} custom-call(bf16[240,1536]{1,0:T(8,128)(2,1)S(1)} %copy-done.34, bf16[240,1536]{1,0:T(8,128)(2,1)} %collective-permute-done.17.refs_1_), custom_call_target="tpu_custom_call" | custom-call | flops 30000001024 | bytes 10000000000 | tf_op jit(solution)/shard_map/join_halves/pallas_call | solution.py:62
  96.9 6.9 %main_backward.1 = (bf16[240,1536]{1,0:T(8,128)(2,1)}, bf16[240,1536]{1,0:T(8,128)(2,1)}, bf16[240,1536]{1,0:T(8,128)(2,1)}) custom-call(bf16[240,1536]{1,0:T(8,128)(2,1)S(1)} %merge.1.refs_0_, bf16[240,1536]{1,0:T(8,128)(2,1)} %get-tuple-element.32.refs_1_.refs_6_.refs_2_.refs_0_, bf16[240,1536]{1,0:T(8,128)(2,1)S(1)} %bitcast.15, ...), custom_call_target="tpu_custom_call" | custom-call | flops 30000001024 | bytes 10000000000 | tf_op jit(solution)/shard_map/main_backward/pallas_call | solution.py:62
  106.0 2.8 %collective-permute-done.27.refs_1_ = bf16[192,768]{1,0:T(8,128)(2,1)S(1)} collective-permute-done((bf16[192,768]{1,0:T(8,128)(2,1)S(1)}, bf16[192,768]{1,0:T(8,128)(2,1)S(1)}, u32[]{:S(2)}, u32[]{:S(2)}) %collective-permute-start.27) | collective-permute-done | bytes 294944 | tf_op jit(solution)/shard_map/ppermute | solution.py:491
  (133 shorter events, 24.8 us)
Async XLA Ops:
  4.1 24.1 %collective-permute-start = (bf16[120,3072]{1,0:T(8,128)(2,1)}, bf16[120,3072]{1,0:T(8,128)(2,1)S(1)}, u32[]{:S(2)}, u32[]{:S(2)}) collective-permute-start(bf16[120,3072]{1,0:T(8,128)(2,1)} %get-tuple-element.29), channel_id=1, source_target_pairs={{1,2},{2,1},{5,6},{6,5},{9,10},{10,9},{13,14},{14,13},{17,18},{18,... | collective-permute-start | bytes 2211848 | tf_op jit(solution)/shard_map/ppermute | solution.py:622
  4.8 25.0 %collective-permute-start.1 = (bf16[120,3072]{1,0:T(8,128)(2,1)}, bf16[120,3072]{1,0:T(8,128)(2,1)S(1)}, u32[]{:S(2)}, u32[]{:S(2)}) collective-permute-start(bf16[120,3072]{1,0:T(8,128)(2,1)} %get-tuple-element.30), channel_id=1, source_target_pairs={{0,1},{1,0},{2,3},{3,2},{4,5},{5,4},{6,7},{7,6},{8,9},{9,8},{10,11... | collective-permute-start | bytes 2211848 | tf_op jit(solution)/shard_map/ppermute | solution.py:630
  9.2 11.3 %collective-permute-start.3 = (bf16[192,768]{1,0:T(8,128)(2,1)}, bf16[192,768]{1,0:T(8,128)(2,1)S(1)}, u32[]{:S(2)}, u32[]{:S(2)}) collective-permute-start(bf16[192,768]{1,0:T(8,128)(2,1)} %get-tuple-element.31.refs_0_), channel_id=1, source_target_pairs={{0,24},{4,28},{8,0},{12,4},{16,8},{20,12},{24,16},{28,20},{1,25},{... | collective-permute-start | bytes 884744 | tf_op jit(solution)/shard_map/ppermute | solution.py:491
  12.8 13.9 %collective-permute-start.2 = (bf16[192,768]{1,0:T(8,128)(2,1)}, bf16[192,768]{1,0:T(8,128)(2,1)S(1)}, u32[]{:S(2)}, u32[]{:S(2)}) collective-permute-start(bf16[192,768]{1,0:T(8,128)(2,1)} %get-tuple-element.31.refs_0_), channel_id=1, source_target_pairs={{0,8},{4,12},{8,16},{12,20},{16,24},{20,28},{24,0},{28,4},{1,9},{5... | collective-permute-start | bytes 884744 | tf_op jit(solution)/shard_map/ppermute | solution.py:491
  12.8 26.6 %collective-permute-start.8 = (bf16[192,768]{1,0:T(8,128)(2,1)}, bf16[192,768]{1,0:T(8,128)(2,1)}, u32[]{:S(2)}, u32[]{:S(2)}) collective-permute-start(bf16[192,768]{1,0:T(8,128)(2,1)} %get-tuple-element.31.refs_0_), channel_id=1, source_target_pairs={{0,4},{4,0},{8,12},{12,8},{16,20},{20,16},{24,28},{28,24},{1,5},{5... | collective-permute-start | bytes 884744 | tf_op jit(solution)/shard_map/ppermute | solution.py:497
  20.5 21.4 %collective-permute-start.5 = (bf16[240,1536]{1,0:T(8,128)(2,1)}, bf16[240,1536]{1,0:T(8,128)(2,1)S(1)}, u32[]{:S(2)}, u32[]{:S(2)}) collective-permute-start(bf16[240,1536]{1,0:T(8,128)(2,1)} %get-tuple-element.33), channel_id=1, source_target_pairs={{0,2},{1,3},{2,0},{3,1},{4,6},{5,7},{6,4},{7,5},{8,10},{9,11},{10,... | collective-permute-start | bytes 2211848 | tf_op jit(solution)/shard_map/ppermute | solution.py:626
  26.7 15.2 %collective-permute-start.9 = (bf16[192,768]{1,0:T(8,128)(2,1)S(1)}, bf16[192,768]{1,0:T(8,128)(2,1)}, u32[]{:S(2)}, u32[]{:S(2)}) collective-permute-start(bf16[192,768]{1,0:T(8,128)(2,1)S(1)} %collective-permute-done.2.refs_7_.refs_2_), channel_id=1, source_target_pairs={{0,4},{4,0},{8,12},{12,8},{16,20},{20,16},{24,28},{28,24},{1,5},{5... | collective-permute-start | bytes 884744 | tf_op jit(solution)/shard_map/ppermute | solution.py:497
  28.2 9.7 %collective-permute-start.6 = (bf16[192,768]{1,0:T(8,128)(2,1)S(1)}, bf16[192,768]{1,0:T(8,128)(2,1)S(1)}, u32[]{:S(2)}, u32[]{:S(2)}) collective-permute-start(bf16[192,768]{1,0:T(8,128)(2,1)S(1)} %collective-permute-done.2.refs_7_.refs_2_), channel_id=1, source_target_pairs={{0,8},{4,12},{8,16},{12,20},{16,24},{20,28},{24,0},{28,4},{1,9},{5... | collective-permute-start | bytes 884744 | tf_op jit(solution)/shard_map/ppermute | solution.py:491
  29.9 12.1 %collective-permute-start.10 = (bf16[192,768]{1,0:T(8,128)(2,1)S(1)}, bf16[192,768]{1,0:T(8,128)(2,1)}, u32[]{:S(2)}, u32[]{:S(2)}) collective-permute-start(bf16[192,768]{1,0:T(8,128)(2,1)S(1)} %collective-permute-done.3.refs_8_.refs_4_), channel_id=1, source_target_pairs={{0,4},{4,0},{8,12},{12,8},{16,20},{20,16},{24,28},{28,24},{1,5},{5... | collective-permute-start | bytes 884744 | tf_op jit(solution)/shard_map/ppermute | solution.py:497
  38.6 18.1 %collective-permute-start.4 = (bf16[240,1536]{1,0:T(8,128)(2,1)}, bf16[240,1536]{1,0:T(8,128)(2,1)}, u32[]{:S(2)}, u32[]{:S(2)}) collective-permute-start(bf16[240,1536]{1,0:T(8,128)(2,1)} %get-tuple-element.32.refs_1_.refs_6_.refs_2_.refs_0_), channel_id=1, source_target_pairs={{0,2},{1,3},{2,0},{3,1},{4,6},{5,7},{6,4},{7,5},{8,10},{9,11},{10,... | collective-permute-start | bytes 2211848 | tf_op jit(solution)/shard_map/ppermute | solution.py:626
  39.4 8.8 %collective-permute-start.7 = (bf16[192,768]{1,0:T(8,128)(2,1)}, bf16[192,768]{1,0:T(8,128)(2,1)S(1)}, u32[]{:S(2)}, u32[]{:S(2)}) collective-permute-start(bf16[192,768]{1,0:T(8,128)(2,1)} %relay.3.refs_3_.refs_1_.refs_4_), channel_id=1, source_target_pairs={{0,4},{4,0},{8,12},{12,8},{16,20},{20,16},{24,28},{28,24},{1,5},{5... | collective-permute-start | bytes 884744 | tf_op jit(solution)/shard_map/ppermute | solution.py:497
  48.2 11.2 %collective-permute-start.14 = (bf16[240,1536]{1,0:T(8,128)(2,1)}, bf16[240,1536]{1,0:T(8,128)(2,1)}, u32[]{:S(2)}, u32[]{:S(2)}) collective-permute-start(bf16[240,1536]{1,0:T(8,128)(2,1)} %get-tuple-element.36), channel_id=1, source_target_pairs={{0,1},{1,0},{2,3},{3,2},{4,5},{5,4},{6,7},{7,6},{8,9},{9,8},{10,11... | collective-permute-start | bytes 2211848 | tf_op jit(solution)/shard_map/ppermute | solution.py:630
  48.2 11.2 %collective-permute-start.16 = (bf16[480,768]{1,0:T(8,128)(2,1)}, bf16[480,768]{1,0:T(8,128)(2,1)}, u32[]{:S(2)}, u32[]{:S(2)}) collective-permute-start(bf16[480,768]{1,0:T(8,128)(2,1)} %get-tuple-element.35.refs_3_), channel_id=1, source_target_pairs={{0,1},{1,0},{2,3},{3,2},{4,5},{5,4},{6,7},{7,6},{8,9},{9,8},{10,11... | collective-permute-start | bytes 2211848 | tf_op jit(solution)/shard_map/ppermute | solution.py:630
  50.8 27.5 %collective-permute-start.18 = (bf16[240,1152]{1,0:T(8,128)(2,1)}, bf16[240,1152]{1,0:T(8,128)(2,1)}, u32[]{:S(2)}, u32[]{:S(2)}) collective-permute-start(bf16[240,1152]{1,0:T(8,128)(2,1)} %grad_attention_near.2.refs_5_), channel_id=1, source_target_pairs={{0,2},{1,3},{2,0},{3,1},{4,6},{5,7},{6,4},{7,5},{8,10},{9,11},{10,... | collective-permute-start | bytes 1658888 | tf_op jit(solution)/shard_map/ppermute | solution.py:626
  52.8 24.1 %collective-permute-start.19 = (bf16[240,384]{1,0:T(8,128)(2,1)}, bf16[240,384]{1,0:T(8,128)(2,1)}, u32[]{:S(2)}, u32[]{:S(2)}) collective-permute-start(bf16[240,384]{1,0:T(8,128)(2,1)} %grad_attention_far.2.refs_1_.refs_3_), channel_id=1, source_target_pairs={{0,2},{1,3},{2,0},{3,1},{4,6},{5,7},{6,4},{7,5},{8,10},{9,11},{10,... | collective-permute-start | bytes 552968 | tf_op jit(solution)/shard_map/ppermute | solution.py:626
  66.2 9.8 %collective-permute-start.20 = (bf16[192,768]{1,0:T(8,128)(2,1)S(1)}, bf16[192,768]{1,0:T(8,128)(2,1)S(1)}, u32[]{:S(2)}, u32[]{:S(2)}) collective-permute-start(bf16[192,768]{1,0:T(8,128)(2,1)S(1)} %get-tuple-element.40), channel_id=1, source_target_pairs={{0,4},{4,0},{8,12},{12,8},{16,20},{20,16},{24,28},{28,24},{1,5},{5... | collective-permute-start | bytes 884744 | tf_op jit(solution)/shard_map/ppermute | solution.py:497
  67.5 21.2 %collective-permute-start.23 = (bf16[384,768]{1,0:T(8,128)(2,1)}, bf16[384,768]{1,0:T(8,128)(2,1)}, u32[]{:S(2)}, u32[]{:S(2)}) collective-permute-start(bf16[384,768]{1,0:T(8,128)(2,1)} %get-tuple-element.46), channel_id=1, source_target_pairs={{0,4},{4,0},{8,12},{12,8},{16,20},{20,16},{24,28},{28,24},{1,5},{5... | collective-permute-start | bytes 1769480 | tf_op jit(solution)/shard_map/ppermute | solution.py:497
  74.4 20.0 %collective-permute-start.17 = (bf16[240,1536]{1,0:T(8,128)(2,1)}, bf16[240,1536]{1,0:T(8,128)(2,1)}, u32[]{:S(2)}, u32[]{:S(2)}) collective-permute-start(bf16[240,1536]{1,0:T(8,128)(2,1)} %get-tuple-element.39.refs_2_), channel_id=1, source_target_pairs={{0,2},{1,3},{2,0},{3,1},{4,6},{5,7},{6,4},{7,5},{8,10},{9,11},{10,... | collective-permute-start | bytes 2211848 | tf_op jit(solution)/shard_map/ppermute | solution.py:626
  76.1 13.7 %collective-permute-start.24 = (bf16[192,768]{1,0:T(8,128)(2,1)S(1)}, bf16[192,768]{1,0:T(8,128)(2,1)S(1)}, u32[]{:S(2)}, u32[]{:S(2)}) collective-permute-start(bf16[192,768]{1,0:T(8,128)(2,1)S(1)} %add.3.refs_4_.refs_1_), channel_id=1, source_target_pairs={{0,8},{4,12},{8,16},{12,20},{16,24},{20,28},{24,0},{28,4},{1,9},{5... | collective-permute-start | bytes 884744 | tf_op jit(solution)/shard_map/ppermute | solution.py:491
  76.9 26.9 %collective-permute-start.25 = (bf16[192,768]{1,0:T(8,128)(2,1)}, bf16[192,768]{1,0:T(8,128)(2,1)}, u32[]{:S(2)}, u32[]{:S(2)}) collective-permute-start(bf16[192,768]{1,0:T(8,128)(2,1)} %relay.5), channel_id=1, source_target_pairs={{0,4},{4,0},{8,12},{12,8},{16,20},{20,16},{24,28},{28,24},{1,5},{5... | collective-permute-start | bytes 884744 | tf_op jit(solution)/shard_map/ppermute | solution.py:497
  86.4 10.4 %collective-permute-start.21 = (bf16[120,3072]{1,0:T(8,128)(2,1)S(1)}, bf16[120,3072]{1,0:T(8,128)(2,1)S(1)}, u32[]{:S(2)}, u32[]{:S(2)}) collective-permute-start(bf16[120,3072]{1,0:T(8,128)(2,1)S(1)} %get-tuple-element.44), channel_id=1, source_target_pairs={{1,2},{2,1},{5,6},{6,5},{9,10},{10,9},{13,14},{14,13},{17,18},{18,... | collective-permute-start | bytes 2211848 | tf_op jit(solution)/shard_map/ppermute | solution.py:622
  88.8 8.1 %collective-permute-start.22 = (bf16[120,3072]{1,0:T(8,128)(2,1)S(1)}, bf16[120,3072]{1,0:T(8,128)(2,1)S(1)}, u32[]{:S(2)}, u32[]{:S(2)}) collective-permute-start(bf16[120,3072]{1,0:T(8,128)(2,1)S(1)} %get-tuple-element.45), channel_id=1, source_target_pairs={{0,1},{1,0},{2,3},{3,2},{4,5},{5,4},{6,7},{7,6},{8,9},{9,8},{10,11... | collective-permute-start | bytes 2211848 | tf_op jit(solution)/shard_map/ppermute | solution.py:630
  91.1 12.7 %collective-permute-start.26 = (bf16[192,768]{1,0:T(8,128)(2,1)S(1)}, bf16[192,768]{1,0:T(8,128)(2,1)S(1)}, u32[]{:S(2)}, u32[]{:S(2)}) collective-permute-start(bf16[192,768]{1,0:T(8,128)(2,1)S(1)} %get-tuple-element.52), channel_id=1, source_target_pairs={{0,24},{4,28},{8,0},{12,4},{16,8},{20,12},{24,16},{28,20},{1,25},{... | collective-permute-start | bytes 884744 | tf_op jit(solution)/shard_map/ppermute | solution.py:491
  94.4 14.4 %collective-permute-start.27 = (bf16[192,768]{1,0:T(8,128)(2,1)S(1)}, bf16[192,768]{1,0:T(8,128)(2,1)S(1)}, u32[]{:S(2)}, u32[]{:S(2)}) collective-permute-start(bf16[192,768]{1,0:T(8,128)(2,1)S(1)} %get-tuple-element.47.refs_13_), channel_id=1, source_target_pairs={{0,8},{4,12},{8,16},{12,20},{16,24},{20,28},{24,0},{28,4},{1,9},{5... | collective-permute-start | bytes 884744 | tf_op jit(solution)/shard_map/ppermute | solution.py:491
  (44 other events, 253.7 us)
